TPU v7x, 32 devices: a whole 2x2x4 slice. The times are simulated.
32 devices in a mesh: gy: 8 (over z, y), gz: 4 (over x, core).
Axes of the slice: x: 2, y: 2, z: 4, core: 2. Of those that a mesh axis runs over, the one named last changes fastest.
Arguments:
- observed: float32 [2, 256, 64, 512], P(None, 'gy', 'gz'), may hold values from 0.1 to 4
- psf_rows: float32 [2, 31], replicated, may hold values from 0.05 to 1
- psf_columns: float32 [2, 31], replicated, may hold values from 0.05 to 1
- psf_axial: float32 [2, 101], replicated, may hold values from 0.05 to 1
- live_list: int32 [8, 4, 32], P('gy'), may hold values from -1 to 31, as said below
Outputs:
- estimate: float32 [2, 256, 64, 512], P(None, 'gy', 'gz')
Inputs may be any that keep to these rules, and one draw needn't show every extreme that they name: Each row live_list[i, j] lists distinct brick numbers of device (i, j) in any order, followed by entries -1; at least 8 entries of every row are brick numbers, and some row names all 32 bricks.
All inputs are finite; a program needn't handle non-finite values.
Results may differ from a plain program's by a relative error of at most 0.0001.
Values sent between devices are 32-bit elements; how exact they have to be, the bound alone decides.
No kernel may reach another device: no remote copies, remote signals or barrier semaphores. Data moves between devices by JAX's collectives and lax.ppermute only.
A program may use at most 128 MiB of HBM per device.

v0:
```python
import jax
import jax.numpy as jnp
from jax import lax
from jax.sharding import PartitionSpec as P

ITERS = 2
Y_DEV = 32
Z_DEV = 16
X = 512
BY = 8
BZ = 8
BX = 128


def with_halo(cells, sides, width):
    for axis, dim in sides:
        count = lax.axis_size(axis)
        ends = count - 1
        head = lax.slice_in_dim(cells, 0, width, axis=dim)
        tail = lax.slice_in_dim(cells, cells.shape[dim] - width, cells.shape[dim], axis=dim)
        cells = jnp.concatenate(
            [
                lax.ppermute(tail, axis, [(i, (i + 1) % count) for i in range(ends)]),
                cells,
                lax.ppermute(head, axis, [((i + 1) % count, i) for i in range(ends)]),
            ],
            axis=dim,
        )
    return cells


def normalized(kernel):
    return kernel / jnp.sum(kernel, axis=1, keepdims=True)


def tap_sum(padded, kernel, axis_number):
    extent = kernel.shape[1]
    length = padded.shape[axis_number] - extent + 1
    summed = None
    for offset in range(extent):
        weight = kernel[:, offset].reshape((kernel.shape[0], 1, 1, 1))
        addend = weight * lax.slice_in_dim(padded, offset, offset + length, axis=axis_number)
        summed = addend if summed is None else summed + addend
    return summed


def along_rows(volume, kernel):
    padded = with_halo(volume, (("gy", 1),), kernel.shape[1] // 2)
    return tap_sum(padded, kernel, 1)


def along_columns(volume, kernel):
    radius = kernel.shape[1] // 2
    padded = jnp.pad(volume, ((0, 0), (0, 0), (0, 0), (radius, radius)))
    return tap_sum(padded, kernel, 3)


def axial_band(kernel, depth):
    radius = kernel.shape[1] // 2
    source = jnp.arange(depth)[None, :, None]
    target = jnp.arange(depth)[None, None, :]
    offsets = jnp.arange(kernel.shape[1])[:, None, None]
    onehot = (source - target + radius == offsets).astype(jnp.float32)
    return jnp.einsum("ck,kst->cst", kernel, onehot, precision=lax.Precision.HIGHEST)


def axial_forward(volume, band):
    return jnp.einsum("cysx,cst->cytx", volume, band, precision=lax.Precision.HIGHEST)


def axial_adjoint(volume, band):
    return jnp.einsum("cysx,cts->cytx", volume, band, precision=lax.Precision.HIGHEST)


def spread_cells(bricks):
    tiles, depths, blocks = bricks.shape
    widened = jnp.broadcast_to(
        bricks[:, None, :, None, :, None], (tiles, BY, depths, BZ, blocks, BX)
    )
    return widened.reshape(tiles * BY, depths * BZ, blocks * BX)


def per_device(observed, psf_rows, psf_columns, psf_axial, live_list):
    rows_kernel = normalized(psf_rows)
    columns_kernel = normalized(psf_columns)
    axial_kernel = normalized(psf_axial)
    rows_flipped = rows_kernel[:, ::-1]
    columns_flipped = columns_kernel[:, ::-1]
    groups = lax.axis_size("gz")
    band = axial_band(axial_kernel, observed.shape[2] * groups)
    listed = live_list[0]
    numbers = jnp.arange(listed.shape[1], dtype=jnp.int32)
    hits = jnp.any(listed[:, :, None] == numbers, axis=1)
    tiled = hits.reshape(groups, Y_DEV // BY, Z_DEV // BZ, X // BX)
    quarter = observed.shape[3] // groups
    pencil_bricks = jnp.transpose(tiled, (1, 0, 2, 3)).reshape(
        Y_DEV // BY, groups * (Z_DEV // BZ), X // BX
    )
    pencil_live = lax.dynamic_slice_in_dim(
        spread_cells(pencil_bricks), lax.axis_index("gz") * quarter, quarter, 2
    )[None]
    observed_pencil = lax.all_to_all(observed, "gz", split_axis=3, concat_axis=2, tiled=True)
    own_bricks = lax.dynamic_index_in_dim(tiled, lax.axis_index("gz"), 0, keepdims=False)
    brick_live = spread_cells(own_bricks)[None]
    estimate = observed
    for iteration in range(ITERS):
        lateral = along_rows(along_columns(estimate, columns_kernel), rows_kernel)
        pencil = lax.all_to_all(lateral, "gz", split_axis=3, concat_axis=2, tiled=True)
        blurred = axial_forward(pencil, band)
        quotient = jnp.where(pencil_live, observed_pencil / blurred, 1.0)
        spread = axial_adjoint(quotient, band)
        returned = lax.all_to_all(spread, "gz", split_axis=2, concat_axis=3, tiled=True)
        correction = along_columns(along_rows(returned, rows_flipped), columns_flipped)
        estimate = jnp.where(brick_live, estimate * correction, estimate)
    return estimate


def solution(mesh):
    placed = (P(None, "gy", "gz", None), P(), P(), P(), P("gy", None, None))
    return jax.shard_map(
        per_device, mesh=mesh, in_specs=placed, out_specs=P(None, "gy", "gz", None), check_vma=False
    )
```

profile of v0, /device:TPU:0, one launch (start us, length us, event | category | flops | bytes accessed | tf_op | source)
XLA Modules:
  0.0 540.8 jit_solution(3065404205976101752)
XLA Ops:
  0.0 0.8 reduce_sum.27
  0.8 0.7 broadcast_divide_fusion.1
  2.0 0.5 slice_reduce_fusion.61
  2.5 42.3 %fusion.53 = f32[2,32,16,512]{3,2,1,0:T(8,128)S(1)} fusion(f32[2,32,16,512]{3,2,1,0:T(8,128)} %param.5, f32[2]{0:T(128)S(1)} %get-tuple-element.37, f32[2]{0:T(128)S(1)} %get-tuple-element.38, f32[2]{0:T(128)S(1)} %get-tuple-element.39, f32[2]{0:T(128)S(1)} %get-tuple-element.40, f32[2]{0:T(128)S(1)} %get-tuple-element.41, f32[2]{0:T(128)S(1)} %get-tuple-element.42, ...), kind=kLoop, calls=%fused_computation.287 | loop fusion | flops 31981568 | bytes 4194552 | tf_op jit(solution)/shard_map/add | solution.py:43
  44.9 1.3 copy-done.4
  46.2 1.4 fusion.498
  47.6 4.9 collective-permute-start
  52.5 1.3 collective-permute-start.1
  53.8 7.6 %copy.111 = f32[2,32,16,512]{1,2,0,3:T(8,128)} copy(f32[2,32,16,512]{3,2,1,0:T(8,128)S(1)} %copy-done) | data formatting | bytes 4194304 | tf_op args[0]
  61.5 7.1 %reshape.225 = f32[4,1,131072]{2,1,0:T(1,128)} reshape(f32[512,2,16,32]{3,2,1,0:T(8,128)} %bitcast.67) | data formatting | bytes 4194304
  68.6 4.9 all-to-all-start
  73.7 0.9 slice_reduce_fusion.59
  75.4 19.5 %collective-permute-done = f32[2,15,16,512]{3,2,1,0:T(8,128)S(1)} collective-permute-done((f32[2,15,16,512]{3,2,1,0:T(8,128)}, f32[2,15,16,512]{3,2,1,0:T(8,128)S(1)}, u32[]{:S(2)}, u32[]{:S(2)}) %collective-permute-start) | collective-permute-done | bytes 983072 | tf_op jit(solution)/shard_map/ppermute | solution.py:23
  94.9 12.2 %fusion.329 = f32[2,32,16,512]{3,2,1,0:T(8,128)} fusion(f32[2,32,16,512]{3,2,1,0:T(8,128)S(1)} %copy-done.5, f32[2,15,16,512]{3,2,1,0:T(8,128)} %collective-permute-done.1, f32[2,15,16,512]{3,2,1,0:T(8,128)S(1)} %collective-permute-done, f32[2]{0:T(128)S(1)} %get-tuple-element.6, f32[2]{0:T(128)S(1)} %get-tuple-element.7, f32[2]{0:T(128)S(1)} %get-tuple-element.8, ...), kind=kLoop, calls=%fused_computation.563 | loop fusion | flops 47710208 | bytes 6160632 | tf_op jit(solution)/shard_map/add | solution.py:43
  107.0 8.4 %copy.113 = f32[2,32,16,512]{1,2,0,3:T(8,128)} copy(f32[2,32,16,512]{3,2,1,0:T(8,128)} %fusion.329) | data formatting | bytes 4194304 | tf_op jit(solution)/shard_map/add | solution.py:43
  115.4 7.1 %reshape.227 = f32[4,1,131072]{2,1,0:T(1,128)} reshape(f32[512,2,16,32]{3,2,1,0:T(8,128)} %bitcast.62) | data formatting | bytes 4194304
  122.5 5.1 all-to-all-start.1
  128.2 2.8 fusion.484
  131.1 0.5 broadcast_in_dim.57
  131.8 0.6 broadcast.88
  132.4 7.8 %reduce.124 = f32[4,131072]{1,0:T(4,128)S(1)} reduce(f32[4,1,131072]{2,1,0:T(1,128)} %all-to-all-done, f32[]{:T(128)} %broadcast.88), dimensions={1}, to_apply=%all_to_all.65.reduce_sub_computation | reduce | bytes 4194308 | tf_op jit(solution)/shard_map/all_to_all | solution.py:102
  140.1 6.1 %reshape.226 = f32[512,2,16,32]{3,2,1,0:T(8,128)} reshape(f32[4,131072]{1,0:T(4,128)S(1)} %reduce.124) | data formatting | bytes 4194304
  146.3 7.4 %copy.112 = f32[2,32,16,4,128]{4,2,3,1,0:T(8,128)} copy(f32[2,32,16,4,128]{1,2,0,4,3:T(8,128)} %bitcast.63) | data formatting | bytes 4194304 | tf_op jit(solution)/shard_map/all_to_all | solution.py:102
  153.7 7.8 %reduce.125 = f32[4,131072]{1,0:T(4,128)S(1)} reduce(f32[4,1,131072]{2,1,0:T(1,128)} %all-to-all-done.1, f32[]{:T(128)} %broadcast.88), dimensions={1}, to_apply=%all_to_all.69.reduce_sub_computation | reduce | bytes 4194308 | tf_op jit(solution)/shard_map/all_to_all | solution.py:108
  161.4 6.1 %reshape.228 = f32[512,2,16,32]{3,2,1,0:T(8,128)} reshape(f32[4,131072]{1,0:T(4,128)S(1)} %reduce.125) | data formatting | bytes 4194304
  167.6 6.2 %copy.136 = f32[2,32,16,4,128]{4,3,2,1,0:T(4,128)S(1)} copy(f32[2,32,16,4,128]{1,2,0,4,3:T(8,128)} %bitcast.64) | data formatting | bytes 4194304 | tf_op jit(solution)/shard_map/all_to_all | solution.py:108
  174.1 1.3 copy-done.6
  175.4 2.3 fusion.479
  177.8 1.9 convolution_bitcast_fusion
  179.7 1.2 copy.118
  180.9 28.8 %all_to_all.90 = f32[2,32,64,128]{3,1,0,2:T(8,128)S(1)} all-to-all(f32[2,32,64,128]{3,1,0,2:T(8,128)S(1)} %copy.118), channel_id=1, replica_groups=mesh['gy'=8,'gz'=4] {'gz'}, dimensions={2} | all-to-all | bytes 4194304 | tf_op jit(solution)/shard_map/all_to_all | solution.py:112
  209.7 2.7 copy.149
  212.4 2.1 all_to_all.76
  214.5 1.5 fusion.497
  216.0 5.2 collective-permute-start.2
  221.2 1.3 collective-permute-start.3
  222.8 39.5 %collective-permute-done.2 = f32[2,15,16,512]{3,2,1,0:T(8,128)} collective-permute-done((f32[2,15,16,512]{3,2,1,0:T(8,128)}, f32[2,15,16,512]{3,2,1,0:T(8,128)}, u32[]{:S(2)}, u32[]{:S(2)}) %collective-permute-start.2) | collective-permute-done | bytes 983072 | tf_op jit(solution)/shard_map/ppermute | solution.py:23
  262.2 1.3 constant_dynamic-update-slice_fusion.1
  263.5 0.5 constant_dynamic-update-slice_fusion
  264.4 9.8 %fusion.444 = f32[2,32,16,512]{3,2,1,0:T(8,128)S(1)} fusion(f32[2,47,16,512]{3,2,1,0:T(8,128)S(1)} %constant_dynamic-update-slice_fusion.2, f32[2,47,16,512]{3,2,1,0:T(8,128)S(1)} %get-tuple-element.73, f32[2,32,16,512]{3,2,1,0:T(8,128)S(1)} %all_to_all.76, f32[2]{0:T(128)S(1)} %get-tuple-element.6, f32[2]{0:T(128)S(1)} %get-tuple-element.7, ...), kind=kLoop, calls=%fused_computation.711 | loop fusion | flops 31981568 | bytes 67109112 | tf_op jit(solution)/shard_map/add | solution.py:43
  274.4 16.7 %multiply_select_fusion.1 = f32[2,32,16,512]{3,2,1,0:T(8,128)S(1)} fusion(f32[2,32,16,512]{3,2,1,0:T(8,128)S(1)} %copy-done.1, f32[2,32,16,512]{3,2,1,0:T(8,128)S(1)} %fusion.444, f32[2]{0:T(128)S(1)} %get-tuple-element.37, f32[2]{0:T(128)S(1)} %get-tuple-element.38, f32[2]{0:T(128)S(1)} %get-tuple-element.39, f32[2]{0:T(128)S(1)} %get-tuple-element.40, ...), kind=kLoop, calls=%fused_computation.233 | loop fusion | flops 33030144 | bytes 6553848 | tf_op jit(solution)/shard_map/jit(_where)/select_n | solution.py:114
  291.3 16.7 %fusion.173 = f32[2,32,16,512]{3,2,1,0:T(8,128)S(1)} fusion(f32[2,32,16,512]{3,2,1,0:T(8,128)S(1)} %multiply_select_fusion.1, f32[2]{0:T(128)S(1)} %get-tuple-element.37, f32[2]{0:T(128)S(1)} %get-tuple-element.38, f32[2]{0:T(128)S(1)} %get-tuple-element.39, f32[2]{0:T(128)S(1)} %get-tuple-element.40, f32[2]{0:T(128)S(1)} %get-tuple-element.41, ...), kind=kLoop, calls=%fused_computation.407 | loop fusion | flops 31981568 | bytes 4194552 | tf_op jit(solution)/shard_map/add | solution.py:43
  308.4 4.4 collective-permute-start.4
  312.9 1.5 collective-permute-start.5
  314.3 39.2 %collective-permute-done.4 = f32[2,15,16,512]{3,2,1,0:T(8,128)S(1)} collective-permute-done((f32[2,15,16,512]{3,2,1,0:T(8,128)S(1)}, f32[2,15,16,512]{3,2,1,0:T(8,128)S(1)}, u32[]{:S(2)}, u32[]{:S(2)}) %collective-permute-start.4) | collective-permute-done | bytes 983072 | tf_op jit(solution)/shard_map/ppermute | solution.py:23
  353.8 10.1 %fusion.243 = f32[2,32,16,512]{3,2,1,0:T(8,128)S(1)} fusion(f32[2,32,16,512]{3,2,1,0:T(8,128)S(1)} %fusion.173, f32[2,15,16,512]{3,2,1,0:T(8,128)S(1)} %collective-permute-done.5, f32[2,15,16,512]{3,2,1,0:T(8,128)S(1)} %collective-permute-done.4, f32[2]{0:T(128)S(1)} %copy-done.36, f32[2]{0:T(128)S(1)} %copy-done.39, f32[2]{0:T(128)S(1)} %copy-done.42, ...), kind=kLoop, calls=%fused_computation.477 | loop fusion | flops 47710208 | bytes 6160632 | tf_op jit(solution)/shard_map/add | solution.py:43
  363.9 7.6 %copy.120 = f32[2,32,16,512]{1,2,0,3:T(8,128)} copy(f32[2,32,16,512]{3,2,1,0:T(8,128)S(1)} %fusion.243) | data formatting | bytes 4194304 | tf_op jit(solution)/shard_map/add | solution.py:43
  371.5 6.1 %reshape.229 = f32[4,1,131072]{2,1,0:T(1,128)S(1)} reshape(f32[512,2,16,32]{3,2,1,0:T(8,128)} %bitcast.65) | data formatting | bytes 4194304
  377.6 28.9 %all_to_all.91 = f32[4,1,131072]{2,1,0:T(1,128)} all-to-all(f32[4,1,131072]{2,1,0:T(1,128)S(1)} %reshape.229), channel_id=1, replica_groups=mesh['gy'=8,'gz'=4] {'gz'}, dimensions={0} | all-to-all | bytes 4194304 | tf_op jit(solution)/shard_map/all_to_all | solution.py:108
  406.6 7.8 %reduce.126 = f32[4,131072]{1,0:T(4,128)S(1)} reduce(f32[4,1,131072]{2,1,0:T(1,128)} %all_to_all.91, f32[]{:T(128)} %broadcast.88), dimensions={1}, to_apply=%all_to_all.77.reduce_sub_computation | reduce | bytes 4194308 | tf_op jit(solution)/shard_map/all_to_all | solution.py:108
  414.3 6.1 %reshape.230 = f32[512,2,16,32]{3,2,1,0:T(8,128)} reshape(f32[4,131072]{1,0:T(4,128)S(1)} %reduce.126) | data formatting | bytes 4194304
  420.4 6.2 %copy.141 = f32[2,32,16,4,128]{4,3,2,1,0:T(4,128)S(1)} copy(f32[2,32,16,4,128]{1,2,0,4,3:T(8,128)} %bitcast.66) | data formatting | bytes 4194304 | tf_op jit(solution)/shard_map/all_to_all | solution.py:108
  426.9 1.9 fusion.499
  428.9 2.2 fusion.481
  431.1 1.2 copy.125
  432.4 28.2 %all_to_all.92 = f32[2,32,64,128]{3,1,0,2:T(8,128)S(1)} all-to-all(f32[2,32,64,128]{3,1,0,2:T(8,128)S(1)} %copy.125), channel_id=1, replica_groups=mesh['gy'=8,'gz'=4] {'gz'}, dimensions={2} | all-to-all | bytes 4194304 | tf_op jit(solution)/shard_map/all_to_all | solution.py:112
  460.5 2.7 copy.148
  463.2 2.1 all_to_all.84
  465.5 4.5 collective-permute-start.6
  469.9 1.3 collective-permute-start.7
  471.2 40.3 %collective-permute-done.6 = f32[2,15,16,512]{3,2,1,0:T(8,128)S(1)} collective-permute-done((f32[2,15,16,512]{3,2,1,0:T(8,128)S(1)}, f32[2,15,16,512]{3,2,1,0:T(8,128)S(1)}, u32[]{:S(2)}, u32[]{:S(2)}) %collective-permute-start.6) | collective-permute-done | bytes 983072 | tf_op jit(solution)/shard_map/ppermute | solution.py:23
  511.9 0.5 constant_dynamic-update-slice_fusion.4
  513.0 9.7 %fusion.412 = f32[2,32,16,512]{3,2,1,0:T(8,128)S(1)} fusion(f32[2,47,16,512]{3,2,1,0:T(8,128)S(1)} %constant_dynamic-update-slice_fusion.6, f32[2,47,16,512]{3,2,1,0:T(8,128)S(1)} %get-tuple-element.67, f32[2,32,16,512]{3,2,1,0:T(8,128)S(1)} %all_to_all.84, f32[2]{0:T(128)S(1)} %copy-done.37, f32[2]{0:T(128)S(1)} %copy-done.40, f32[2]{0:T(128)S(1)} %copy-done.43, ...), kind=kLoop, calls=%fused_computation.647 | loop fusion | flops 31981568 | bytes 67109112 | tf_op jit(solution)/shard_map/add | solution.py:43
  522.8 17.5 %multiply_select_fusion = f32[2,32,16,512]{3,2,1,0:T(8,128)} fusion(f32[2,32,16,512]{3,2,1,0:T(8,128)S(1)} %copy-done.3, f32[2,32,16,512]{3,2,1,0:T(8,128)S(1)} %fusion.412, f32[2]{0:T(128)S(1)} %get-tuple-element.37, f32[2]{0:T(128)S(1)} %get-tuple-element.38, f32[2]{0:T(128)S(1)} %get-tuple-element.39, f32[2]{0:T(128)S(1)} %get-tuple-element.40, ...), kind=kLoop, calls=%fused_computation.232 | loop fusion | flops 33030144 | bytes 6553848 | tf_op jit(solution)/shard_map/jit(_where)/select_n | solution.py:114
  (248 shorter events, 3.7 us)
Async XLA Ops:
  1.9 289.3 %copy-start.10 = (f32[2]{0:T(128)}, f32[2]{0:T(128)S(1)}, u32[]{:S(2)}) copy-start(f32[2]{0:T(128)S(1)} %get-tuple-element.56) | copy-start | bytes 28
  1.9 289.3 %copy-start.12 = (f32[2]{0:T(128)}, f32[2]{0:T(128)S(1)}, u32[]{:S(2)}) copy-start(f32[2]{0:T(128)S(1)} %get-tuple-element.57) | copy-start | bytes 28
  1.9 289.3 %copy-start.14 = (f32[2]{0:T(128)}, f32[2]{0:T(128)S(1)}, u32[]{:S(2)}) copy-start(f32[2]{0:T(128)S(1)} %get-tuple-element.58) | copy-start | bytes 28
  1.9 289.3 %copy-start.16 = (f32[2]{0:T(128)}, f32[2]{0:T(128)S(1)}, u32[]{:S(2)}) copy-start(f32[2]{0:T(128)S(1)} %get-tuple-element.59) | copy-start | bytes 28
  2.0 289.3 %copy-start.18 = (f32[2]{0:T(128)}, f32[2]{0:T(128)S(1)}, u32[]{:S(2)}) copy-start(f32[2]{0:T(128)S(1)} %get-tuple-element.60) | copy-start | bytes 28
  2.0 289.3 %copy-start.20 = (f32[2]{0:T(128)}, f32[2]{0:T(128)S(1)}, u32[]{:S(2)}) copy-start(f32[2]{0:T(128)S(1)} %get-tuple-element.61) | copy-start | bytes 28
  2.0 289.3 %copy-start.22 = (f32[2]{0:T(128)}, f32[2]{0:T(128)S(1)}, u32[]{:S(2)}) copy-start(f32[2]{0:T(128)S(1)} %get-tuple-element.62) | copy-start | bytes 28
  2.0 289.3 %copy-start.24 = (f32[2]{0:T(128)}, f32[2]{0:T(128)S(1)}, u32[]{:S(2)}) copy-start(f32[2]{0:T(128)S(1)} %get-tuple-element.63) | copy-start | bytes 28
  2.0 289.3 %copy-start.26 = (f32[2]{0:T(128)}, f32[2]{0:T(128)S(1)}, u32[]{:S(2)}) copy-start(f32[2]{0:T(128)S(1)} %get-tuple-element.64) | copy-start | bytes 28
  2.0 289.3 %copy-start.28 = (f32[2]{0:T(128)}, f32[2]{0:T(128)S(1)}, u32[]{:S(2)}) copy-start(f32[2]{0:T(128)S(1)} %get-tuple-element.65) | copy-start | bytes 28
  2.0 289.3 %copy-start.30 = (f32[2]{0:T(128)}, f32[2]{0:T(128)S(1)}, u32[]{:S(2)}) copy-start(f32[2]{0:T(128)S(1)} %get-tuple-element.66) | copy-start | bytes 28
  47.6 47.2 %collective-permute-start = (f32[2,15,16,512]{3,2,1,0:T(8,128)}, f32[2,15,16,512]{3,2,1,0:T(8,128)S(1)}, u32[]{:S(2)}, u32[]{:S(2)}) collective-permute-start(f32[2,15,16,512]{3,2,1,0:T(8,128)} %get-tuple-element.77), channel_id=1, source_target_pairs={{0,4},{4,8},{8,12},{12,16},{16,20},{20,24},{24,28},{1,5},{5,9},{9,... | collective-permute-start | bytes 2949128 | tf_op jit(solution)/shard_map/ppermute | solution.py:23
  52.5 42.3 %collective-permute-start.1 = (f32[2,15,16,512]{3,2,1,0:T(8,128)}, f32[2,15,16,512]{3,2,1,0:T(8,128)}, u32[]{:S(2)}, u32[]{:S(2)}) collective-permute-start(f32[2,15,16,512]{3,2,1,0:T(8,128)} %get-tuple-element.78), channel_id=1, source_target_pairs={{4,0},{8,4},{12,8},{16,12},{20,16},{24,20},{28,24},{5,1},{9,5},{13... | collective-permute-start | bytes 2949128 | tf_op jit(solution)/shard_map/ppermute | solution.py:25
  68.6 54.0 %all-to-all-start = ((f32[4,1,131072]{2,1,0:T(1,128)}), f32[4,1,131072]{2,1,0:T(1,128)}, u32[]{:S(2)}, u32[]{:S(2)}) async-start(f32[4,1,131072]{2,1,0:T(1,128)} %reshape.225), calls=%async_computation | async-start | bytes 4194304 | tf_op jit(solution)/shard_map/all_to_all | solution.py:102
  74.6 189.5 %copy-start.89 = (f32[2]{0:T(128)}, f32[2]{0:T(128)S(1)}, u32[]{:S(2)}) copy-start(f32[2]{0:T(128)S(1)} %get-tuple-element.24) | copy-start | bytes 28
  74.7 189.5 %copy-start.92 = (f32[2]{0:T(128)}, f32[2]{0:T(128)S(1)}, u32[]{:S(2)}) copy-start(f32[2]{0:T(128)S(1)} %get-tuple-element.25) | copy-start | bytes 28
  74.7 189.5 %copy-start.95 = (f32[2]{0:T(128)}, f32[2]{0:T(128)S(1)}, u32[]{:S(2)}) copy-start(f32[2]{0:T(128)S(1)} %get-tuple-element.26) | copy-start | bytes 28
  74.7 189.5 %copy-start.98 = (f32[2]{0:T(128)}, f32[2]{0:T(128)S(1)}, u32[]{:S(2)}) copy-start(f32[2]{0:T(128)S(1)} %get-tuple-element.27) | copy-start | bytes 28
  74.7 189.5 %copy-start.100 = (f32[2]{0:T(128)}, f32[2]{0:T(128)S(1)}, u32[]{:S(2)}) copy-start(f32[2]{0:T(128)S(1)} %get-tuple-element.28) | copy-start | bytes 28
  74.7 189.5 %copy-start.102 = (f32[2]{0:T(128)}, f32[2]{0:T(128)S(1)}, u32[]{:S(2)}) copy-start(f32[2]{0:T(128)S(1)} %get-tuple-element.29) | copy-start | bytes 28
  74.7 189.5 %copy-start.104 = (f32[2]{0:T(128)}, f32[2]{0:T(128)S(1)}, u32[]{:S(2)}) copy-start(f32[2]{0:T(128)S(1)} %get-tuple-element.30) | copy-start | bytes 28
  74.7 189.5 %copy-start.106 = (f32[2]{0:T(128)}, f32[2]{0:T(128)S(1)}, u32[]{:S(2)}) copy-start(f32[2]{0:T(128)S(1)} %get-tuple-element.31) | copy-start | bytes 28
  75.2 189.0 %copy-start.32 = (f32[2]{0:T(128)}, f32[2]{0:T(128)S(1)}, u32[]{:S(2)}) copy-start(f32[2]{0:T(128)S(1)} %get-tuple-element.5) | copy-start | bytes 28
  75.2 189.0 %copy-start.35 = (f32[2]{0:T(128)}, f32[2]{0:T(128)S(1)}, u32[]{:S(2)}) copy-start(f32[2]{0:T(128)S(1)} %get-tuple-element.6) | copy-start | bytes 28
  75.2 189.0 %copy-start.38 = (f32[2]{0:T(128)}, f32[2]{0:T(128)S(1)}, u32[]{:S(2)}) copy-start(f32[2]{0:T(128)S(1)} %get-tuple-element.7) | copy-start | bytes 28
  75.2 189.0 %copy-start.41 = (f32[2]{0:T(128)}, f32[2]{0:T(128)S(1)}, u32[]{:S(2)}) copy-start(f32[2]{0:T(128)S(1)} %get-tuple-element.8) | copy-start | bytes 28
  75.2 189.0 %copy-start.44 = (f32[2]{0:T(128)}, f32[2]{0:T(128)S(1)}, u32[]{:S(2)}) copy-start(f32[2]{0:T(128)S(1)} %get-tuple-element.9) | copy-start | bytes 28
  75.2 189.0 %copy-start.47 = (f32[2]{0:T(128)}, f32[2]{0:T(128)S(1)}, u32[]{:S(2)}) copy-start(f32[2]{0:T(128)S(1)} %get-tuple-element.10) | copy-start | bytes 28
  75.3 189.0 %copy-start.50 = (f32[2]{0:T(128)}, f32[2]{0:T(128)S(1)}, u32[]{:S(2)}) copy-start(f32[2]{0:T(128)S(1)} %get-tuple-element.11) | copy-start | bytes 28
  75.3 189.0 %copy-start.53 = (f32[2]{0:T(128)}, f32[2]{0:T(128)S(1)}, u32[]{:S(2)}) copy-start(f32[2]{0:T(128)S(1)} %get-tuple-element.12) | copy-start | bytes 28
  75.3 189.0 %copy-start.56 = (f32[2]{0:T(128)}, f32[2]{0:T(128)S(1)}, u32[]{:S(2)}) copy-start(f32[2]{0:T(128)S(1)} %get-tuple-element.13) | copy-start | bytes 28
  75.3 189.0 %copy-start.59 = (f32[2]{0:T(128)}, f32[2]{0:T(128)S(1)}, u32[]{:S(2)}) copy-start(f32[2]{0:T(128)S(1)} %get-tuple-element.14) | copy-start | bytes 28
  75.3 189.0 %copy-start.62 = (f32[2]{0:T(128)}, f32[2]{0:T(128)S(1)}, u32[]{:S(2)}) copy-start(f32[2]{0:T(128)S(1)} %get-tuple-element.15) | copy-start | bytes 28
  75.3 189.0 %copy-start.65 = (f32[2]{0:T(128)}, f32[2]{0:T(128)S(1)}, u32[]{:S(2)}) copy-start(f32[2]{0:T(128)S(1)} %get-tuple-element.16) | copy-start | bytes 28
  75.3 189.0 %copy-start.68 = (f32[2]{0:T(128)}, f32[2]{0:T(128)S(1)}, u32[]{:S(2)}) copy-start(f32[2]{0:T(128)S(1)} %get-tuple-element.17) | copy-start | bytes 28
  75.3 189.0 %copy-start.71 = (f32[2]{0:T(128)}, f32[2]{0:T(128)S(1)}, u32[]{:S(2)}) copy-start(f32[2]{0:T(128)S(1)} %get-tuple-element.18) | copy-start | bytes 28
  75.3 189.0 %copy-start.74 = (f32[2]{0:T(128)}, f32[2]{0:T(128)S(1)}, u32[]{:S(2)}) copy-start(f32[2]{0:T(128)S(1)} %get-tuple-element.19) | copy-start | bytes 28
  75.3 189.0 %copy-start.77 = (f32[2]{0:T(128)}, f32[2]{0:T(128)S(1)}, u32[]{:S(2)}) copy-start(f32[2]{0:T(128)S(1)} %get-tuple-element.20) | copy-start | bytes 28
  75.4 189.0 %copy-start.80 = (f32[2]{0:T(128)}, f32[2]{0:T(128)S(1)}, u32[]{:S(2)}) copy-start(f32[2]{0:T(128)S(1)} %get-tuple-element.21) | copy-start | bytes 28
  75.4 189.0 %copy-start.83 = (f32[2]{0:T(128)}, f32[2]{0:T(128)S(1)}, u32[]{:S(2)}) copy-start(f32[2]{0:T(128)S(1)} %get-tuple-element.22) | copy-start | bytes 28
  75.4 189.0 %copy-start.86 = (f32[2]{0:T(128)}, f32[2]{0:T(128)S(1)}, u32[]{:S(2)}) copy-start(f32[2]{0:T(128)S(1)} %get-tuple-element.23) | copy-start | bytes 28
  122.5 31.1 %all-to-all-start.1 = ((f32[4,1,131072]{2,1,0:T(1,128)}), f32[4,1,131072]{2,1,0:T(1,128)}, u32[]{:S(2)}, u32[]{:S(2)}) async-start(f32[4,1,131072]{2,1,0:T(1,128)} %reshape.227), calls=%async_computation.1 | async-start | bytes 4194304 | tf_op jit(solution)/shard_map/all_to_all | solution.py:108
  216.0 46.3 %collective-permute-start.2 = (f32[2,15,16,512]{3,2,1,0:T(8,128)}, f32[2,15,16,512]{3,2,1,0:T(8,128)}, u32[]{:S(2)}, u32[]{:S(2)}) collective-permute-start(f32[2,15,16,512]{3,2,1,0:T(8,128)} %get-tuple-element.75), channel_id=1, source_target_pairs={{0,4},{4,8},{8,12},{12,16},{16,20},{20,24},{24,28},{1,5},{5,9},{9,... | collective-permute-start | bytes 2949128 | tf_op jit(solution)/shard_map/ppermute | solution.py:23
  221.2 42.9 %collective-permute-start.3 = (f32[2,15,16,512]{3,2,1,0:T(8,128)}, f32[2,15,16,512]{3,2,1,0:T(8,128)S(1)}, u32[]{:S(2)}, u32[]{:S(2)}) collective-permute-start(f32[2,15,16,512]{3,2,1,0:T(8,128)} %get-tuple-element.76), channel_id=1, source_target_pairs={{4,0},{8,4},{12,8},{16,12},{20,16},{24,20},{28,24},{5,1},{9,5},{13... | collective-permute-start | bytes 2949128 | tf_op jit(solution)/shard_map/ppermute | solution.py:25
  308.0 45.6 %copy-start.33 = (f32[2]{0:T(128)S(1)}, f32[2]{0:T(128)}, u32[]{:S(2)}) copy-start(f32[2]{0:T(128)} %copy-done.32) | copy-start | bytes 28
  308.0 45.6 %copy-start.36 = (f32[2]{0:T(128)S(1)}, f32[2]{0:T(128)}, u32[]{:S(2)}) copy-start(f32[2]{0:T(128)} %copy-done.35) | copy-start | bytes 28
  308.1 45.5 %copy-start.39 = (f32[2]{0:T(128)S(1)}, f32[2]{0:T(128)}, u32[]{:S(2)}) copy-start(f32[2]{0:T(128)} %copy-done.38) | copy-start | bytes 28
  308.1 45.5 %copy-start.42 = (f32[2]{0:T(128)S(1)}, f32[2]{0:T(128)}, u32[]{:S(2)}) copy-start(f32[2]{0:T(128)} %copy-done.41) | copy-start | bytes 28
  308.1 45.5 %copy-start.45 = (f32[2]{0:T(128)S(1)}, f32[2]{0:T(128)}, u32[]{:S(2)}) copy-start(f32[2]{0:T(128)} %copy-done.44) | copy-start | bytes 28
  308.1 45.5 %copy-start.48 = (f32[2]{0:T(128)S(1)}, f32[2]{0:T(128)}, u32[]{:S(2)}) copy-start(f32[2]{0:T(128)} %copy-done.47) | copy-start | bytes 28
  308.1 45.5 %copy-start.51 = (f32[2]{0:T(128)S(1)}, f32[2]{0:T(128)}, u32[]{:S(2)}) copy-start(f32[2]{0:T(128)} %copy-done.50) | copy-start | bytes 28
  308.1 45.5 %copy-start.54 = (f32[2]{0:T(128)S(1)}, f32[2]{0:T(128)}, u32[]{:S(2)}) copy-start(f32[2]{0:T(128)} %copy-done.53) | copy-start | bytes 28
  308.1 45.5 %copy-start.57 = (f32[2]{0:T(128)S(1)}, f32[2]{0:T(128)}, u32[]{:S(2)}) copy-start(f32[2]{0:T(128)} %copy-done.56) | copy-start | bytes 28
  308.1 45.5 %copy-start.60 = (f32[2]{0:T(128)S(1)}, f32[2]{0:T(128)}, u32[]{:S(2)}) copy-start(f32[2]{0:T(128)} %copy-done.59) | copy-start | bytes 28
  308.1 45.5 %copy-start.63 = (f32[2]{0:T(128)S(1)}, f32[2]{0:T(128)}, u32[]{:S(2)}) copy-start(f32[2]{0:T(128)} %copy-done.62) | copy-start | bytes 28
  308.1 45.5 %copy-start.66 = (f32[2]{0:T(128)S(1)}, f32[2]{0:T(128)}, u32[]{:S(2)}) copy-start(f32[2]{0:T(128)} %copy-done.65) | copy-start | bytes 28
  308.2 45.5 %copy-start.69 = (f32[2]{0:T(128)S(1)}, f32[2]{0:T(128)}, u32[]{:S(2)}) copy-start(f32[2]{0:T(128)} %copy-done.68) | copy-start | bytes 28
  308.2 45.5 %copy-start.72 = (f32[2]{0:T(128)S(1)}, f32[2]{0:T(128)}, u32[]{:S(2)}) copy-start(f32[2]{0:T(128)} %copy-done.71) | copy-start | bytes 28
  308.2 45.5 %copy-start.75 = (f32[2]{0:T(128)S(1)}, f32[2]{0:T(128)}, u32[]{:S(2)}) copy-start(f32[2]{0:T(128)} %copy-done.74) | copy-start | bytes 28
  308.2 45.5 %copy-start.78 = (f32[2]{0:T(128)S(1)}, f32[2]{0:T(128)}, u32[]{:S(2)}) copy-start(f32[2]{0:T(128)} %copy-done.77) | copy-start | bytes 28
  308.4 45.2 %collective-permute-start.4 = (f32[2,15,16,512]{3,2,1,0:T(8,128)S(1)}, f32[2,15,16,512]{3,2,1,0:T(8,128)S(1)}, u32[]{:S(2)}, u32[]{:S(2)}) collective-permute-start(f32[2,15,16,512]{3,2,1,0:T(8,128)S(1)} %get-tuple-element.71), channel_id=1, source_target_pairs={{0,4},{4,8},{8,12},{12,16},{16,20},{20,24},{24,28},{1,5},{5,9},{9,... | collective-permute-start | bytes 2949128 | tf_op jit(solution)/shard_map/ppermute | solution.py:23
  312.9 40.7 %collective-permute-start.5 = (f32[2,15,16,512]{3,2,1,0:T(8,128)S(1)}, f32[2,15,16,512]{3,2,1,0:T(8,128)S(1)}, u32[]{:S(2)}, u32[]{:S(2)}) collective-permute-start(f32[2,15,16,512]{3,2,1,0:T(8,128)S(1)} %get-tuple-element.72), channel_id=1, source_target_pairs={{4,0},{8,4},{12,8},{16,12},{20,16},{24,20},{28,24},{5,1},{9,5},{13... | collective-permute-start | bytes 2949128 | tf_op jit(solution)/shard_map/ppermute | solution.py:25
  465.5 46.1 %collective-permute-start.6 = (f32[2,15,16,512]{3,2,1,0:T(8,128)S(1)}, f32[2,15,16,512]{3,2,1,0:T(8,128)S(1)}, u32[]{:S(2)}, u32[]{:S(2)}) collective-permute-start(f32[2,15,16,512]{3,2,1,0:T(8,128)S(1)} %get-tuple-element.69), channel_id=1, source_target_pairs={{0,4},{4,8},{8,12},{12,16},{16,20},{20,24},{24,28},{1,5},{5,9},{9,... | collective-permute-start | bytes 2949128 | tf_op jit(solution)/shard_map/ppermute | solution.py:23
  469.9 42.5 %collective-permute-start.7 = (f32[2,15,16,512]{3,2,1,0:T(8,128)S(1)}, f32[2,15,16,512]{3,2,1,0:T(8,128)S(1)}, u32[]{:S(2)}, u32[]{:S(2)}) collective-permute-start(f32[2,15,16,512]{3,2,1,0:T(8,128)S(1)} %get-tuple-element.70), channel_id=1, source_target_pairs={{4,0},{8,4},{12,8},{16,12},{20,16},{24,20},{28,24},{5,1},{9,5},{13... | collective-permute-start | bytes 2949128 | tf_op jit(solution)/shard_map/ppermute | solution.py:25
  (57 other events, 541.6 us)
where the time goes:
time: 550 us; the launch traced here: 541 us
  other arithmetic  160 us (29%)
  waiting for transfers between devices  139 us (25%)
  local copies, waits for them, and re-layouts  108 us (20%)
  blocking collectives  85.9 us (16%)
  starting transfers between devices  34.5 us (6%)
  matrix products  11.2 us (2%)
    ppermute x4, waiting for transfers between devices, with_halo(): lax.ppermute(tail, axis, [(i, (i + 1) % count) for i in range(ends)])  139 us
    add x6, other arithmetic, tap_sum(): summed = addend if summed is None else summed + addend  101 us
    all_to_all x2, blocking collectives, per_device(): lax.all_to_all(spread, 'gz', split_axis=2, concat_axis=3, tiled=True)  56.9 us
    unnamed x231, local copies, waits for them, and re-layouts  50.8 us
    select_n x2, other arithmetic, per_device(): estimate = jnp.where(brick_live, estimate * correction, estimate)  34.3 us
    all_to_all x1, blocking collectives, per_device(): lax.all_to_all(lateral, 'gz', split_axis=3, concat_axis=2, tiled=True)  28.9 us
    ppermute x4, starting transfers between devices, with_halo(): lax.ppermute(tail, axis, [(i, (i + 1) % count) for i in range(ends)])  19.1 us
    add x2, local copies, waits for them, and re-layouts, tap_sum(): summed = addend if summed is None else summed + addend  16 us
  transfers between devices with their start and end apart: 10, of which 4 were waited for; matrix products, arithmetic and copies ran while one was open for 13% of the time, Pallas kernels for 0%

commit v1 on v0

v1 whole, which is shorter than its diff:
```python
import jax
import jax.numpy as jnp
from jax import lax
from jax.experimental import pallas as pl
from jax.experimental.pallas import tpu as pltpu
from jax.sharding import Mesh, PartitionSpec as P

ITERS = 2
BY = 8
BZ = 8
LANES = 128
STRIP = 16
F32, BF16 = jnp.float32, jnp.bfloat16
VMEM = pl.BlockSpec(memory_space=pltpu.VMEM)
SMEM = pl.BlockSpec(memory_space=pltpu.SMEM)
PARAMS = pltpu.CompilerParams(vmem_limit_bytes=40 * 1024 * 1024)


def shape(dims, dtype=F32):
    return jax.ShapeDtypeStruct(dims, dtype)


def halves(cells):
    high = cells.astype(BF16)
    return high, (cells - high.astype(F32)).astype(BF16)


def dot(a, b):
    return jnp.dot(a, b, preferred_element_type=F32)


def other(bits, d):
    return tuple(jnp.where((d >> s) & 1, 1 - b, b) for b, s in zip(bits, (2, 1, 0)))


def deal_kernel(me, observed, *outs):
    for d in range(8):
        yl, zh, zl = other((me[0], me[1], me[2]), d)
        start = pl.multiple_of((2 * yl + zl) * LANES, LANES)
        outs[d][...] = observed[zh, :, :, pl.ds(start, LANES)]


def gather_kernel(me, *rest):
    pieces, out = rest[:8], rest[8]
    for d in range(8):
        yl, zh, zl = other((me[0], me[1], me[2]), d)
        start = pl.multiple_of((2 * yl + zl) * LANES, LANES)
        out[zh, :, :, pl.ds(start, LANES)] = pieces[d][...]


def pack_strips(me, cells, to_pair, to_next):
    groups = LANES // STRIP
    lane_group = lax.broadcasted_iota(jnp.int32, (cells.shape[1], LANES), 1) // STRIP
    left_first = me[2] == 1
    for out, edge in (
        (to_pair, jnp.where(left_first, 0, LANES - STRIP)),
        (to_next, jnp.where(left_first, LANES - STRIP, 0)),
    ):
        def one(y, _):
            total = jnp.zeros((cells.shape[1], LANES), F32)
            for j in range(groups):
                shift = lax.rem(STRIP * j - edge + LANES, LANES)
                total = jnp.where(lane_group == j, pltpu.roll(cells[groups * j + y], shift, 1), total)
            out[y] = total
            return 0

        lax.fori_loop(0, groups, one, 0)


def join_kernel(me, *rest):
    pieces, cells, to_pair, to_next = rest[:8], rest[8], rest[9], rest[10]
    bits = (me[0], me[1], me[2])
    rows, depth = pieces[0].shape[:2]
    for d in range(8):
        yl, zh, zl = other(bits, d)
        y0 = pl.multiple_of(yl * rows, rows)
        z0 = pl.multiple_of((2 * zh + zl) * depth, depth)
        cells[pl.ds(y0, rows), pl.ds(z0, depth), :] = pieces[d][...]
    pack_strips(me, cells, to_pair, to_next)


def weights_kernel(me, rows, columns, axial, *outs):
    channel = me[1]
    nx, nz = LANES, outs[0].shape[0] // 4
    radius, reach = columns.shape[1] // 2, axial.shape[1] // 2

    def toeplitz(taps, offsets):
        def one(k, total):
            return jnp.where(offsets == k, taps[channel, k], total)

        return lax.fori_loop(0, taps.shape[1], one, jnp.zeros(offsets.shape, F32))

    for flip in (False, True):
        wz, wx, wh_edge, wh_inner, wy = outs[5 * flip : 5 * flip + 5]

        def offsets(source, target, half):
            return (target - source if flip else source - target) + half

        def iota(dims, axis):
            return lax.broadcasted_iota(jnp.int32, dims, axis)

        dims = (nz, 2 * nz)
        high, low = halves(toeplitz(axial, offsets(iota(dims, 1) % nz, iota(dims, 0), reach)))
        zero = jnp.zeros(dims, BF16)
        wz[...] = jnp.concatenate(
            [
                jnp.concatenate([high, zero], 1),
                jnp.concatenate([low, zero], 1),
                jnp.concatenate([zero, high], 1),
                jnp.concatenate([zero, low], 1),
            ],
            0,
        )
        dims = (nx, nx)
        high, low = halves(toeplitz(columns, offsets(iota(dims, 0), iota(dims, 1), radius)))
        both = jnp.concatenate([high, low], 1)
        wx[...] = jnp.concatenate([both, both], 0)
        dims = (STRIP, nx)
        wh_edge[...] = jnp.zeros(wh_edge.shape, BF16)
        wh_inner[...] = jnp.zeros(wh_inner.shape, BF16)
        for k, first in ((0, me[2] == 0), (1, me[2] == 1)):
            source = iota(dims, 0) + jnp.where(first, nx, -STRIP)
            both = jnp.concatenate(halves(toeplitz(columns, offsets(source, iota(dims, 1), radius))), 1)
            for j in range(nx // STRIP):
                ref, at = place(j, wh_edge, wh_inner)
                ref[at, k * nx + STRIP * j : k * nx + STRIP * (j + 1), :] = both
        for i in range(rows.shape[1]):
            k = rows.shape[1] - 1 - i if flip else i
            wy[i] = jnp.full((8, LANES), rows[channel, k], F32)


def place(j, edge, inner):
    return (edge, j) if j < 2 else (inner, j - 2) if j < 6 else (edge, j - 4)


def blur_z(weights, slabs):
    depth = slabs[0].shape[0]
    parts = [jnp.concatenate(halves(slab), 0) for slab in slabs]
    stacked = jnp.concatenate(
        [jnp.concatenate(parts[:2], 0), jnp.concatenate(parts[2:], 0)], 1
    )
    out = dot(weights, stacked)
    return [
        out[2 * a * depth : (2 * a + 1) * depth, b * LANES : (b + 1) * LANES]
        + out[(2 * a + 1) * depth : (2 * a + 2) * depth, b * LANES : (b + 1) * LANES]
        for b in range(2)
        for a in range(2)
    ]


def own_kernel(cells, wz, wx, edge, inner):
    rows, depth = cells.shape[:2]

    def one(g, _):
        slabs = blur_z(wz[...], [cells[4 * g + i] for i in range(4)])
        out = dot(jnp.concatenate(halves(jnp.concatenate(slabs, 0)), 1), wx[...])
        out = (out[:, :LANES] + out[:, LANES:]).reshape(4, depth, LANES)

        @pl.when(g < rows // 16)
        def _():
            edge[pl.ds(4 * g, 4)] = out

        @pl.when(g >= 3 * rows // 16)
        def _():
            edge[pl.ds(4 * g - rows // 2, 4)] = out

        @pl.when((g >= rows // 16) & (g < 3 * rows // 16))
        def _():
            inner[pl.ds(4 * g - rows // 4, 4)] = out

        return 0

    lax.fori_loop(0, rows // 4, one, 0)


def strip_terms(strips, weights):
    out = dot(strips, weights)
    out = out[:, :LANES] + out[:, LANES:]
    half = out.shape[0] // 2
    return out[:half] + out[half:]


def edge_kernel(me, own_edge, pair, after, wz, wh, edge, strips, send_a, send_b):
    rows, depth = own_edge.shape[0], own_edge.shape[1]
    for g in range(pair.shape[0] // 4):
        a = blur_z(wz[...], [pair[4 * g + i] for i in range(4)])
        b = blur_z(wz[...], [after[4 * g + i] for i in range(4)])
        high_a, low_a = halves(jnp.concatenate(a, 0))
        high_b, low_b = halves(jnp.concatenate(b, 0))
        at = 4 * depth * g
        half = strips.shape[0] // 2
        strips[at : at + 4 * depth, :] = jnp.concatenate([high_a, high_b], 1)
        strips[half + at : half + at + 4 * depth, :] = jnp.concatenate([low_a, low_b], 1)
    for j in range(4):
        add = strip_terms(strips[...], wh[j]).reshape(8, depth, LANES)
        edge[8 * j : 8 * j + 8] = own_edge[8 * j : 8 * j + 8] + add
    count = send_a.shape[0]
    even = me[3] == 0

    @pl.when(even)
    def _():
        send_a[...] = edge[rows - count :]
        send_b[...] = edge[:count]

    @pl.when(jnp.logical_not(even))
    def _():
        send_a[...] = edge[:count]
        send_b[...] = edge[rows - count :]


def inner_kernel(own_inner, edge, strips, wh, wy, out, inner):
    rows, depth = out.shape[:2]
    for j in range(4):
        add = strip_terms(strips[...], wh[j]).reshape(8, depth, LANES)
        inner[8 * j : 8 * j + 8] = own_inner[8 * j : 8 * j + 8] + add
    radius = wy.shape[0] // 2
    quarter = rows // 4
    chunk = 16

    def source(y):
        if y < quarter:
            return edge, y
        if y < 3 * quarter:
            return inner, y - quarter
        return edge, y - 2 * quarter

    def one(t, _):
        z = pl.ds(pl.multiple_of(8 * t, 8), 8)
        taps = [wy[i] for i in range(wy.shape[0])]
        for first in range(0, rows, chunk):
            sums = [None] * chunk
            for y in range(max(0, first - radius), min(rows, first + chunk + radius)):
                ref, at = source(y)
                cell = ref[at, z, :]
                for o in range(chunk):
                    i = y - (first + o) + radius
                    if 0 <= i < len(taps):
                        term = taps[i] * cell
                        sums[o] = term if sums[o] is None else sums[o] + term
            for o in range(chunk):
                out[first + o, z, :] = sums[o]
        return 0

    lax.fori_loop(0, depth // 8, one, 0)


def add_halo(me, part, recv_a, recv_b, wy, halo, blurred):
    rows, depth = part.shape[:2]
    radius = wy.shape[0] // 2
    even = me[3] == 0
    halo[jnp.where(even, 1, 0)] = recv_a[...]
    halo[jnp.where(even, 0, 1)] = recv_b[...]

    def one(t, _):
        z = pl.ds(pl.multiple_of(8 * t, 8), 8)
        taps = [wy[i] for i in range(wy.shape[0])]
        for side in range(2):
            sums = {}
            for h in range(radius):
                y = h - radius if side == 0 else rows + h
                cell = halo[side, h, z, :]
                for o in range(radius) if side == 0 else range(rows - radius, rows):
                    i = y - o + radius
                    if 0 <= i < len(taps):
                        term = taps[i] * cell
                        sums[o] = sums[o] + term if o in sums else term
            for o in sums:
                blurred[o, z, :] = part[o, z, :] + sums[o]
        return 0

    lax.fori_loop(0, depth // 8, one, 0)


def each_row(rows, radius, part, blurred, do):
    def one(y, _):
        do(y, part[y])
        return 0

    def edge(y, _):
        do(y, blurred[y])
        return 0

    lax.fori_loop(0, radius, edge, 0)
    lax.fori_loop(radius, rows - radius, one, 0)
    lax.fori_loop(rows - radius, rows, edge, 0)


def quotient_kernel(me, part, recv_a, recv_b, wy, observed, live, out, to_pair, to_next, halo, blurred):
    add_halo(me, part, recv_a, recv_b, wy, halo, blurred)
    rows = part.shape[0]

    def do(y, value):
        out[y] = jnp.where(live[y // BY] != 0, observed[y] / value, 1.0)

    each_row(rows, wy.shape[0] // 2, part, blurred, do)
    pack_strips(me, out, to_pair, to_next)


def correct(me, part, recv_a, recv_b, wy, estimate, live, out, halo, blurred):
    add_halo(me, part, recv_a, recv_b, wy, halo, blurred)

    def do(y, value):
        out[y] = jnp.where(live[y // BY] != 0, estimate[y] * value, estimate[y])

    each_row(part.shape[0], wy.shape[0] // 2, part, blurred, do)


def estimate_kernel(me, part, recv_a, recv_b, wy, estimate, live, out, to_pair, to_next, halo, blurred):
    correct(me, part, recv_a, recv_b, wy, estimate, live, out, halo, blurred)
    pack_strips(me, out, to_pair, to_next)


def last_kernel(me, part, recv_a, recv_b, wy, estimate, live, *rest):
    pieces, out, halo, blurred = rest[:8], rest[8], rest[9], rest[10]
    correct(me, part, recv_a, recv_b, wy, estimate, live, out, halo, blurred)
    rows, depth = pieces[0].shape[:2]
    for d in range(8):
        yl, zh, zl = other((me[0], me[1], me[2]), d)
        y0 = pl.multiple_of(yl * rows, rows)
        z0 = pl.multiple_of((2 * zh + zl) * depth, depth)
        pieces[d][...] = out[pl.ds(y0, rows), pl.ds(z0, depth), :]


def call(kernel, out, ins, scratch=(), us=1, name=None):
    many = isinstance(out, (tuple, list))
    return pl.pallas_call(
        kernel,
        out_shape=out,
        in_specs=ins,
        out_specs=[VMEM] * len(out) if many else VMEM,
        scratch_shapes=list(scratch),
        compiler_params=PARAMS,
        cost_estimate=pl.CostEstimate(flops=0, bytes_accessed=int(us * 3.0e6), transcendentals=0),
        name=name,
    )


def per_device(observed, psf_rows, psf_columns, psf_axial, live_list):
    yh = lax.axis_index("yh")
    yl, zh, zl = lax.axis_index("yl"), lax.axis_index("zh"), lax.axis_index("zl")
    me = jnp.stack([yl, zh, zl, yh % 2]).astype(jnp.int32)
    channels, rows, depth, columns = observed.shape
    ny, nz = 2 * rows, 4 * depth
    radius = psf_rows.shape[1] // 2
    group = ("yl", "zh", "zl")

    def trade(pieces):
        return [pieces[0]] + [
            lax.ppermute(pieces[d], group, [(i, i ^ d) for i in range(8)]) for d in range(1, 8)
        ]

    piece = shape((rows, depth, LANES))
    dealt = call(deal_kernel, [piece] * 8, [SMEM, VMEM], us=3, name="deal")(me, observed)
    pieces = trade(dealt)

    def normalized(kernel):
        return kernel / jnp.sum(kernel, axis=1, keepdims=True)

    wide = [
        shape((4 * nz, 4 * nz), BF16),
        shape((2 * LANES, 2 * LANES), BF16),
        shape((4, 2 * LANES, 2 * LANES), BF16),
        shape((4, 2 * LANES, 2 * LANES), BF16),
        shape((psf_rows.shape[1], 8, LANES)),
    ]
    weights = call(weights_kernel, wide * 2, [SMEM] * 4, us=4, name="weights")(
        me, normalized(psf_rows), normalized(psf_columns), normalized(psf_axial)
    )

    listed = live_list[0]
    theirs = lax.ppermute(listed, "yl", [(0, 1), (1, 0)])

    def bricks(lists):
        numbers = jnp.arange(lists.shape[1], dtype=jnp.int32)
        hits = jnp.any(lists[:, :, None] == numbers, axis=1)
        hits = hits.reshape(lists.shape[0], rows // BY, depth // BZ, columns // LANES)
        hits = lax.dynamic_index_in_dim(hits, 2 * yl + zl, 3, False)
        return jnp.transpose(hits, (1, 0, 2)).reshape(rows // BY, -1)

    mine, yours = bricks(listed), bricks(theirs)
    both = jnp.where(yl == 0, jnp.concatenate([mine, yours]), jnp.concatenate([yours, mine]))
    live = jnp.broadcast_to(
        jnp.repeat(both, BZ, 1)[:, :, None].astype(F32), (ny // BY, nz, LANES)
    )

    whole = shape((ny, nz, LANES))
    half = shape((ny // 2, nz, LANES))
    strip = shape((LANES // STRIP, nz, LANES))
    halo = shape((radius, nz, LANES))
    taken, to_pair, to_next = call(
        join_kernel, [whole, strip, strip], [SMEM] + [VMEM] * 8, us=4, name="join"
    )(me, *pieces)

    high = lax.axis_size("yh")
    evens = [p for i in range(0, high - 1, 2) for p in ((i, i + 1), (i + 1, i))]
    odds = [p for i in range(1, high - 1, 2) for p in ((i, i + 1), (i + 1, i))]

    def blur(cells, to_pair, to_next, w):
        wz, wx, wh_edge, wh_inner, wy = w
        after = lax.ppermute(to_next, ("yl", "zl"), [(1, 2), (2, 1)])
        pair = lax.ppermute(to_pair, "zl", [(0, 1), (1, 0)])
        own_edge, own_inner = call(own_kernel, [half, half], [VMEM] * 3, us=6, name="own")(cells, wz, wx)
        edge, strips, send_a, send_b = call(
            edge_kernel,
            [half, shape((2 * strip.shape[0] * nz, 2 * LANES), BF16), halo, halo],
            [SMEM] + [VMEM] * 5,
            us=2, name="edge",
        )(me, own_edge, pair, after, wz, wh_edge)
        recv_a = lax.ppermute(send_a, "yh", evens)
        recv_b = lax.ppermute(send_b, "yh", odds)
        part = call(
            inner_kernel, whole, [VMEM] * 5,
            [pltpu.VMEM(half.shape, F32)], us=5, name="inner",
        )(own_inner, edge, strips, wh_inner, wy)
        return part, recv_a, recv_b, wy

    scratch = [pltpu.VMEM((2,) + halo.shape, F32), pltpu.VMEM(whole.shape, F32)]
    estimate = taken
    for iteration in range(ITERS):
        found = blur(estimate, to_pair, to_next, weights[:5])
        quotient, to_pair, to_next = call(
            quotient_kernel, [whole, strip, strip], [SMEM] + [VMEM] * 6, scratch, us=4, name="quotient"
        )(me, *found, taken, live)
        found = blur(quotient, to_pair, to_next, weights[5:])
        if iteration + 1 < ITERS:
            estimate, to_pair, to_next = call(
                estimate_kernel, [whole, strip, strip], [SMEM] + [VMEM] * 6, scratch, us=4, name="estimate"
            )(me, *found, estimate, live)
    pieces = call(
        last_kernel, [piece] * 8, [SMEM] + [VMEM] * 6,
        [pltpu.VMEM(whole.shape, F32)] + scratch, us=2, name="last",
    )(me, *found, estimate, live)
    return call(gather_kernel, shape(observed.shape), [SMEM] + [VMEM] * 8, us=3, name="gather")(
        me, *trade(pieces)
    )


def solution(mesh):
    fine = Mesh(
        mesh.devices.reshape(mesh.devices.shape[0] // 2, 2, 2, mesh.devices.shape[1] // 2),
        ("yh", "yl", "zh", "zl"),
    )
    spread = P(None, ("yh", "yl"), ("zh", "zl"), None)
    placed = (spread, P(), P(), P(), P(("yh", "yl"), None, None))
    return jax.shard_map(per_device, mesh=fine, in_specs=placed, out_specs=spread, check_vma=False)
```

time: 550 us -> 199 us (0.36); the launches traced: 541 us -> 197 us
  other arithmetic: 160 us -> 0.79 us
  local copies, waits for them, and re-layouts: 108 us -> 18.6 us
  blocking collectives: 85.9 us -> 0 us
  waiting for transfers between devices: 139 us -> 53.5 us
  Pallas kernels: 0 us -> 78.6 us
  matrix products: 11.2 us -> 0 us
  starting transfers between devices: 34.5 us -> 44.8 us
    add x7 -> x0, other arithmetic: 101 us -> none  [the longest x6 101 us: tap_sum(): summed = addend if summed is None else summed + addend]
    all_to_all x3 -> x0, blocking collectives: 85.9 us -> none  [the longest x2 56.9 us: per_device(): lax.all_to_all(spread, 'gz', split_axis=2, concat_axis=3, tiled=True)]
    ppermute x8 -> x31, waiting for transfers between devices: 139 us -> 53.5 us  [the longest x14 39.3 us: trade(): lax.ppermute(pieces[d], group, [(i, i ^ d) for i in range(8)])]
    pallas_call x0 -> x20, Pallas kernels: none -> 78.6 us  [the longest x4 24.6 us: blur(): call(own_kernel, [half, half], [VMEM] * 3, us=6, name='own')(cells, wz, wx)]
    unnamed x231 -> x56, local copies, waits for them, and re-layouts: 50.8 us -> 16.3 us
    select_n x2 -> x0, other arithmetic: 34.3 us -> none  [per_device(): estimate = jnp.where(brick_live, estimate * correction, estimate)]
    all_to_all x10 -> x0, local copies, waits for them, and re-layouts: 30.5 us -> none  [the longest x4 12.9 us: per_device(): lax.all_to_all(lateral, 'gz', split_axis=3, concat_axis=2, tiled=True)]
    all_to_all x3 -> x0, other arithmetic: 23.3 us -> none  [the longest x2 15.5 us: per_device(): lax.all_to_all(lateral, 'gz', split_axis=3, concat_axis=2, tiled=True)]
  transfers between devices with their start and end apart: 10 -> 31, of which waited for: 4 -> 10; matrix products, arithmetic and copies ran while one was open for 13% -> 1% of each run, Pallas kernels for 0% -> 25%
where the time goes in v1:
time: 199 us; the launch traced here: 197 us
  Pallas kernels  78.6 us (39%)
  waiting for transfers between devices  53.5 us (27%)
  starting transfers between devices  44.8 us (23%)
  local copies, waits for them, and re-layouts  18.6 us (9%)
    ppermute x14, waiting for transfers between devices, trade(): lax.ppermute(pieces[d], group, [(i, i ^ d) for i in range(8)])  39.3 us
    pallas_call x4, Pallas kernels, blur(): call(own_kernel, [half, half], [VMEM] * 3, us=6, name='own')(cells, wz, wx)  24.6 us
    pallas_call x4, Pallas kernels, blur(): call(inner_kernel, whole, [VMEM] * 5, [pltpu.VMEM(half.shape, F32)], us=5...  20.7 us
    ppermute x14, starting transfers between devices, trade(): lax.ppermute(pieces[d], group, [(i, i ^ d) for i in range(8)])  16.7 us
    unnamed x56, local copies, waits for them, and re-layouts  16.3 us
    ppermute x4, starting transfers between devices, blur(): recv_a = lax.ppermute(send_a, 'yh', evens)  13.3 us
    ppermute x4, waiting for transfers between devices, blur(): recv_a = lax.ppermute(send_a, 'yh', evens)  12.7 us
    pallas_call x2, Pallas kernels, per_device(): call(quotient_kernel, [whole, strip, strip], [SMEM] + [VMEM] * 6, scratch...  9.27 us
  transfers between devices with their start and end apart: 31, of which 10 were waited for; matrix products, arithmetic and copies ran while one was open for 1% of the time, Pallas kernels for 25%

profile of v1, /device:TPU:0, one launch (start us, length us, event | category | flops | bytes accessed | tf_op | source)
XLA Modules:
  0.0 196.6 jit_solution(3022731919120384092)
XLA Ops:
  0.1 1.6 copy-done.5
  1.7 0.8 deal.1
  3.0 2.6 %collective-permute-start.1 = (f32[32,16,128]{2,1,0:T(8,128)S(1)}, f32[32,16,128]{2,1,0:T(8,128)S(1)}, u32[]{:S(2)}, u32[]{:S(2)}) collective-permute-start(f32[32,16,128]{2,1,0:T(8,128)S(1)} %get-tuple-element.69), channel_id=1, source_target_pairs={{0,2},{1,3},{2,0},{3,1},{4,6},{5,7},{6,4},{7,5},{8,10},{9,11},{10,... | collective-permute-start | bytes 786440 | tf_op jit(solution)/shard_map/ppermute | solution.py:349
  5.7 1.8 collective-permute-start.3
  7.4 2.6 %collective-permute-start.5 = (f32[32,16,128]{2,1,0:T(8,128)S(1)}, f32[32,16,128]{2,1,0:T(8,128)S(1)}, u32[]{:S(2)}, u32[]{:S(2)}) collective-permute-start(f32[32,16,128]{2,1,0:T(8,128)S(1)} %get-tuple-element.73), channel_id=1, source_target_pairs={{0,6},{1,7},{2,4},{3,5},{4,2},{5,3},{6,0},{7,1},{8,14},{9,15},{10,... | collective-permute-start | bytes 786440 | tf_op jit(solution)/shard_map/ppermute | solution.py:349
  10.0 2.7 %collective-permute-done.1.rest_2_ = f32[32,16,128]{2,1,0:T(8,128)S(1)} collective-permute-done((f32[32,16,128]{2,1,0:T(8,128)S(1)}, f32[32,16,128]{2,1,0:T(8,128)S(1)}, u32[]{:S(2)}, u32[]{:S(2)}) %collective-permute-start.1) | collective-permute-done | bytes 262176 | tf_op jit(solution)/shard_map/ppermute | solution.py:349
  12.7 1.7 collective-permute-start.6
  14.6 3.3 %collective-permute-done.2.rest_3_ = f32[32,16,128]{2,1,0:T(8,128)S(1)} collective-permute-done((f32[32,16,128]{2,1,0:T(8,128)S(1)}, f32[32,16,128]{2,1,0:T(8,128)S(1)}, u32[]{:S(2)}, u32[]{:S(2)}) %collective-permute-start.2) | collective-permute-done | bytes 262176 | tf_op jit(solution)/shard_map/ppermute | solution.py:349
  17.8 12.5 %collective-permute-done.4.rest_5_ = f32[32,16,128]{2,1,0:T(8,128)S(1)} collective-permute-done((f32[32,16,128]{2,1,0:T(8,128)S(1)}, f32[32,16,128]{2,1,0:T(8,128)S(1)}, u32[]{:S(2)}, u32[]{:S(2)}) %collective-permute-start.4) | collective-permute-done | bytes 262176 | tf_op jit(solution)/shard_map/ppermute | solution.py:349
  32.5 0.9 copy-done.19
  33.4 0.9 copy-done.21
  34.4 0.9 copy-done.23
  35.3 3.6 %join.1 = (f32[64,64,128]{2,1,0:T(8,128)S(1)}, f32[8,64,128]{2,1,0:T(8,128)}, f32[8,64,128]{2,1,0:T(8,128)}) custom-call(s32[4]{0:T(128)S(1)} %pad_add_fusion.me, f32[32,16,128]{2,1,0:T(8,128)S(1)} %get-tuple-element.67.rest_0_, f32[32,16,128]{2,1,0:T(8,128)S(1)} %collective-permute-done.rest_1_, f32[32,16,128]{2,1,0:T(8,128)S(1)} %collective-permute-done.1.rest_2_, ...), custom_call_target="tpu_custom_call" | custom-call | bytes 12000000 | tf_op jit(solution)/shard_map/join/pallas_call | solution.py:390
  39.5 1.4 collective-permute-start.8
  41.2 3.7 %weights.1 = (bf16[256,256]{1,0:T(8,128)(2,1)S(1)}, bf16[256,256]{1,0:T(8,128)(2,1)S(1)}, bf16[4,256,256]{2,1,0:T(8,128)(2,1)S(1)}, bf16[4,256,256]{2,1,0:T(8,12...) custom-call(s32[4]{0:T(128)S(1)} %pad_add_fusion.me, ...), custom_call_target="tpu_custom_call" | custom-call | bytes 12000000 | tf_op jit(solution)/shard_map/weights/pallas_call | solution.py:366
  45.0 0.8 copy-done
  46.4 6.2 %own.4 = (f32[32,64,128]{2,1,0:T(8,128)S(1)}, f32[32,64,128]{2,1,0:T(8,128)S(1)}) custom-call(f32[64,64,128]{2,1,0:T(8,128)S(1)} %get-tuple-element.75.cells.observed.estimate, bf16[256,256]{1,0:T(8,128)(2,1)S(1)} %get-tuple-element.76.wz, bf16[256,256]{1,0:T(8,128)(2,1)S(1)} %get-tuple-element.77.wx), custom_call_target="tpu_custom_call" | custom-call | bytes 18000000 | tf_op jit(solution)/shard_map/own/pallas_call | solution.py:402
  52.6 1.0 copy-done.8
  53.6 2.9 %edge.4 = (f32[32,64,128]{2,1,0:T(8,128)S(1)}, bf16[1024,256]{1,0:T(8,128)(2,1)S(1)}, f32[15,64,128]{2,1,0:T(8,128)}, f32[15,64,128]{2,1,0:T(8,128)}) custom-call(s32[4]{0:T(128)S(1)} %pad_add_fusion.me, f32[32,64,128]{2,1,0:T(8,128)S(1)} %get-tuple-element.79.own_edge, f32[8,64,128]{2,1,0:T(8,128)} %collective-permute-done.7.pair, ...), custom_call_target="tpu_custom_call" | custom-call | bytes 6000000 | tf_op jit(solution)/shard_map/edge/pallas_call | solution.py:403
  56.5 1.0 copy-done.10
  57.5 0.8 copy-done.12
  58.3 1.8 collective-permute-start.9
  60.1 1.4 collective-permute-start.10
  61.6 2.3 %collective-permute-start.11 = (s32[4,32]{1,0:T(4,128)S(1)}, s32[4,32]{1,0:T(4,128)S(1)}, u32[]{:S(2)}, u32[]{:S(2)}) collective-permute-start(s32[4,32]{1,0:T(4,128)S(1)} %bitcast.17), channel_id=1, source_target_pairs={{0,4},{4,0},{1,5},{5,1},{2,6},{6,2},{3,7},{7,3},{8,12},{12,8},{9,1... | collective-permute-start | bytes 1544 | tf_op jit(solution)/shard_map/ppermute | solution.py:371
  64.1 1.4 collective-permute-done.11
  66.8 0.8 convert_element_type.13
  67.6 1.0 copy-done.1
  68.6 0.9 copy-done.7
  69.5 1.2 copy-done.9
  70.8 1.2 copy-done.11
  72.0 1.0 copy-done.13
  73.0 5.1 %inner.4.part = f32[64,64,128]{2,1,0:T(8,128)S(1)} custom-call(f32[32,64,128]{2,1,0:T(8,128)S(1)} %copy-done.9, f32[32,64,128]{2,1,0:T(8,128)S(1)} %copy-done.11, bf16[1024,256]{1,0:T(8,128)(2,1)S(1)} %copy-done.13, bf16[4,256,256]{2,1,0:T(8,128)(2,1)S(1)} %copy-done.1, f32[31,8,128]{2,1,0:T(8,128)S(1)} %copy-done.7), custom_call_target="tpu_custom_call" | custom-call | bytes 15000000 | tf_op jit(solution)/shard_map/inner/pallas_call | solution.py:411
  78.3 5.0 %quotient.2 = (f32[64,64,128]{2,1,0:T(8,128)S(1)}, f32[8,64,128]{2,1,0:T(8,128)S(1)}, f32[8,64,128]{2,1,0:T(8,128)S(1)}) custom-call(s32[4]{0:T(128)S(1)} %pad_add_fusion.me, f32[64,64,128]{2,1,0:T(8,128)S(1)} %inner.4.part, f32[15,64,128]{2,1,0:T(8,128)} %collective-permute-done.9.recv_a, f32[15,64,128]{2,1,0:T(8,128)} %collective-permute-done.10.recv_b, ...), custom_call_target="tpu_custom_call" | custom-call | bytes 12000000 | tf_op jit(solution)/shard_map/quotient/pallas_call | solution.py:421
  83.3 0.9 collective-permute-start.12
  84.9 6.2 %own.5 = (f32[32,64,128]{2,1,0:T(8,128)S(1)}, f32[32,64,128]{2,1,0:T(8,128)S(1)}) custom-call(f32[64,64,128]{2,1,0:T(8,128)S(1)} %get-tuple-element.89.cells, bf16[256,256]{1,0:T(8,128)(2,1)S(1)} %get-tuple-element.90.wz, bf16[256,256]{1,0:T(8,128)(2,1)S(1)} %copy-done.15), custom_call_target="tpu_custom_call" | custom-call | bytes 18000000 | tf_op jit(solution)/shard_map/own/pallas_call | solution.py:402
  91.1 1.5 edge.5
  92.6 3.5 %collective-permute-start.14 = (f32[15,64,128]{2,1,0:T(8,128)S(1)}, f32[15,64,128]{2,1,0:T(8,128)S(1)}, u32[]{:S(2)}, u32[]{:S(2)}) collective-permute-start(f32[15,64,128]{2,1,0:T(8,128)S(1)} %get-tuple-element.101), channel_id=1, source_target_pairs={{0,8},{8,0},{16,24},{24,16},{1,9},{9,1},{17,25},{25,17},{2,10},{10... | collective-permute-start | bytes 1474568 | tf_op jit(solution)/shard_map/ppermute | solution.py:409
  96.8 5.2 %inner.5.part = f32[64,64,128]{2,1,0:T(8,128)S(1)} custom-call(f32[32,64,128]{2,1,0:T(8,128)S(1)} %get-tuple-element.92.own_inner, f32[32,64,128]{2,1,0:T(8,128)S(1)} %get-tuple-element.97.edge, bf16[1024,256]{1,0:T(8,128)(2,1)S(1)} %get-tuple-element.98.strips, bf16[4,256,256]{2,1,0:T(8,128)(2,1)S(1)} %get-tuple-element.99.wh, ...), custom_call_target="tpu_custom_call" | custom-call | bytes 15000000 | tf_op jit(solution)/shard_map/inner/pallas_call | solution.py:411
  102.0 4.0 %collective-permute-done.14.recv_a = f32[15,64,128]{2,1,0:T(8,128)S(1)} collective-permute-done((f32[15,64,128]{2,1,0:T(8,128)S(1)}, f32[15,64,128]{2,1,0:T(8,128)S(1)}, u32[]{:S(2)}, u32[]{:S(2)}) %collective-permute-start.14) | collective-permute-done | bytes 491552 | tf_op jit(solution)/shard_map/ppermute | solution.py:409
  106.0 4.1 %estimate.1 = (f32[64,64,128]{2,1,0:T(8,128)S(1)}, f32[8,64,128]{2,1,0:T(8,128)S(1)}, f32[8,64,128]{2,1,0:T(8,128)S(1)}) custom-call(s32[4]{0:T(128)S(1)} %pad_add_fusion.me, f32[64,64,128]{2,1,0:T(8,128)S(1)} %inner.5.part, f32[15,64,128]{2,1,0:T(8,128)S(1)} %collective-permute-done.14.recv_a, f32[15,64,128]{2,1,0:T(8,128)S(1)} %collective-permute-done.15.recv_b, ...), custom_call_target="tpu_custom_call" | custom-call | bytes 12000000 | tf_op jit(solution)/shard_map/estimate/pallas_call | solution.py:426
  110.2 2.1 %collective-permute-start.16 = (f32[8,64,128]{2,1,0:T(8,128)S(1)}, f32[8,64,128]{2,1,0:T(8,128)S(1)}, u32[]{:S(2)}, u32[]{:S(2)}) collective-permute-start(f32[8,64,128]{2,1,0:T(8,128)S(1)} %get-tuple-element.106), channel_id=1, source_target_pairs={{0,1},{1,0},{2,3},{3,2},{4,5},{5,4},{6,7},{7,6},{8,9},{9,8},{10,11... | collective-permute-start | bytes 786440 | tf_op jit(solution)/shard_map/ppermute | solution.py:401
  112.9 6.2 %own.6 = (f32[32,64,128]{2,1,0:T(8,128)S(1)}, f32[32,64,128]{2,1,0:T(8,128)S(1)}) custom-call(f32[64,64,128]{2,1,0:T(8,128)S(1)} %get-tuple-element.103.cells.estimate, bf16[256,256]{1,0:T(8,128)(2,1)S(1)} %get-tuple-element.76.wz, bf16[256,256]{1,0:T(8,128)(2,1)S(1)} %copy-done.17), custom_call_target="tpu_custom_call" | custom-call | bytes 18000000 | tf_op jit(solution)/shard_map/own/pallas_call | solution.py:402
  119.2 1.5 edge.6
  120.7 4.0 %collective-permute-start.18 = (f32[15,64,128]{2,1,0:T(8,128)S(1)}, f32[15,64,128]{2,1,0:T(8,128)S(1)}, u32[]{:S(2)}, u32[]{:S(2)}) collective-permute-start(f32[15,64,128]{2,1,0:T(8,128)S(1)} %get-tuple-element.110), channel_id=1, source_target_pairs={{0,8},{8,0},{16,24},{24,16},{1,9},{9,1},{17,25},{25,17},{2,10},{10... | collective-permute-start | bytes 1474568 | tf_op jit(solution)/shard_map/ppermute | solution.py:409
  125.3 5.1 %inner.6.part = f32[64,64,128]{2,1,0:T(8,128)S(1)} custom-call(f32[32,64,128]{2,1,0:T(8,128)S(1)} %get-tuple-element.104.own_inner, f32[32,64,128]{2,1,0:T(8,128)S(1)} %get-tuple-element.108.edge, bf16[1024,256]{1,0:T(8,128)(2,1)S(1)} %get-tuple-element.109.strips, bf16[4,256,256]{2,1,0:T(8,128)(2,1)S(1)} %copy-done.2, f32[31,8,128]{2,1,0:T(8,128)S(1)} %copy-done.7), custom_call_target="tpu_custom_call" | custom-call | bytes 15000000 | tf_op jit(solution)/shard_map/inner/pallas_call | solution.py:411
  130.5 4.2 %collective-permute-done.18.recv_a = f32[15,64,128]{2,1,0:T(8,128)S(1)} collective-permute-done((f32[15,64,128]{2,1,0:T(8,128)S(1)}, f32[15,64,128]{2,1,0:T(8,128)S(1)}, u32[]{:S(2)}, u32[]{:S(2)}) %collective-permute-start.18) | collective-permute-done | bytes 491552 | tf_op jit(solution)/shard_map/ppermute | solution.py:409
  134.7 4.3 %quotient.3 = (f32[64,64,128]{2,1,0:T(8,128)S(1)}, f32[8,64,128]{2,1,0:T(8,128)S(1)}, f32[8,64,128]{2,1,0:T(8,128)S(1)}) custom-call(s32[4]{0:T(128)S(1)} %pad_add_fusion.me, f32[64,64,128]{2,1,0:T(8,128)S(1)} %inner.6.part, f32[15,64,128]{2,1,0:T(8,128)S(1)} %collective-permute-done.18.recv_a, f32[15,64,128]{2,1,0:T(8,128)S(1)} %collective-permute-done.19.recv_b, ...), custom_call_target="tpu_custom_call" | custom-call | bytes 12000000 | tf_op jit(solution)/shard_map/quotient/pallas_call | solution.py:421
  139.0 1.9 collective-permute-start.20
  140.9 0.8 collective-permute-start.21
  141.8 6.2 %own.7 = (f32[32,64,128]{2,1,0:T(8,128)S(1)}, f32[32,64,128]{2,1,0:T(8,128)S(1)}) custom-call(f32[64,64,128]{2,1,0:T(8,128)S(1)} %get-tuple-element.112.cells, bf16[256,256]{1,0:T(8,128)(2,1)S(1)} %get-tuple-element.90.wz, bf16[256,256]{1,0:T(8,128)(2,1)S(1)} %copy-done.15), custom_call_target="tpu_custom_call" | custom-call | bytes 18000000 | tf_op jit(solution)/shard_map/own/pallas_call | solution.py:402
  147.9 1.5 edge.7
  149.4 4.0 %collective-permute-start.22 = (f32[15,64,128]{2,1,0:T(8,128)S(1)}, f32[15,64,128]{2,1,0:T(8,128)S(1)}, u32[]{:S(2)}, u32[]{:S(2)}) collective-permute-start(f32[15,64,128]{2,1,0:T(8,128)S(1)} %get-tuple-element.119), channel_id=1, source_target_pairs={{0,8},{8,0},{16,24},{24,16},{1,9},{9,1},{17,25},{25,17},{2,10},{10... | collective-permute-start | bytes 1474568 | tf_op jit(solution)/shard_map/ppermute | solution.py:409
  154.1 5.2 %inner.7.part = f32[64,64,128]{2,1,0:T(8,128)S(1)} custom-call(f32[32,64,128]{2,1,0:T(8,128)S(1)} %get-tuple-element.113.own_inner, f32[32,64,128]{2,1,0:T(8,128)S(1)} %get-tuple-element.117.edge, bf16[1024,256]{1,0:T(8,128)(2,1)S(1)} %get-tuple-element.118.strips, bf16[4,256,256]{2,1,0:T(8,128)(2,1)S(1)} %get-tuple-element.99.wh, ...), custom_call_target="tpu_custom_call" | custom-call | bytes 15000000 | tf_op jit(solution)/shard_map/inner/pallas_call | solution.py:411
  159.4 4.5 %collective-permute-done.22.recv_a = f32[15,64,128]{2,1,0:T(8,128)S(1)} collective-permute-done((f32[15,64,128]{2,1,0:T(8,128)S(1)}, f32[15,64,128]{2,1,0:T(8,128)S(1)}, u32[]{:S(2)}, u32[]{:S(2)}) %collective-permute-start.22) | collective-permute-done | bytes 491552 | tf_op jit(solution)/shard_map/ppermute | solution.py:409
  163.9 2.1 %last.1 = (f32[32,16,128]{2,1,0:T(8,128)S(1)}, f32[32,16,128]{2,1,0:T(8,128)S(1)}, f32[32,16,128]{2,1,0:T(8,128)S(1)}, f32[32,16,128]{2,1,0:T(8,128)S(1)}, f32[3...) custom-call(s32[4]{0:T(128)S(1)} %pad_add_fusion.me, ...), custom_call_target="tpu_custom_call" | custom-call | bytes 6000000 | tf_op jit(solution)/shard_map/last/pallas_call | solution.py:429
  166.0 1.5 collective-permute-start.24
  167.5 1.5 collective-permute-start.25
  169.1 1.2 collective-permute-start.27
  170.3 0.8 collective-permute-start.28
  171.0 1.9 collective-permute-start.29
  172.9 3.8 %collective-permute-done.25.rest_2_ = f32[32,16,128]{2,1,0:T(8,128)S(1)} collective-permute-done((f32[32,16,128]{2,1,0:T(8,128)S(1)}, f32[32,16,128]{2,1,0:T(8,128)S(1)}, u32[]{:S(2)}, u32[]{:S(2)}) %collective-permute-start.25) | collective-permute-done | bytes 262176 | tf_op jit(solution)/shard_map/ppermute | solution.py:349
  177.3 4.0 %collective-permute-done.26.rest_3_ = f32[32,16,128]{2,1,0:T(8,128)S(1)} collective-permute-done((f32[32,16,128]{2,1,0:T(8,128)S(1)}, f32[32,16,128]{2,1,0:T(8,128)S(1)}, u32[]{:S(2)}, u32[]{:S(2)}) %collective-permute-start.26) | collective-permute-done | bytes 262176 | tf_op jit(solution)/shard_map/ppermute | solution.py:349
  181.3 13.1 %collective-permute-done.28.rest_5_ = f32[32,16,128]{2,1,0:T(8,128)S(1)} collective-permute-done((f32[32,16,128]{2,1,0:T(8,128)S(1)}, f32[32,16,128]{2,1,0:T(8,128)S(1)}, u32[]{:S(2)}, u32[]{:S(2)}) %collective-permute-start.28) | collective-permute-done | bytes 262176 | tf_op jit(solution)/shard_map/ppermute | solution.py:349
  194.4 2.1 %gather.1 = f32[2,32,16,512]{3,2,1,0:T(8,128)} custom-call(s32[4]{0:T(128)S(1)} %pad_add_fusion.me, f32[32,16,128]{2,1,0:T(8,128)S(1)} %get-tuple-element.121.rest_0_, f32[32,16,128]{2,1,0:T(8,128)S(1)} %collective-permute-done.24.rest_1_, f32[32,16,128]{2,1,0:T(8,128)S(1)} %collective-permute-done.25.rest_2_, ...), custom_call_target="tpu_custom_call" | custom-call | bytes 9000000 | tf_op jit(solution)/shard_map/gather/pallas_call | solution.py:433
  (93 shorter events, 10.3 us)
Async XLA Ops:
  0.0 14.5 %copy-start.26 = (f32[2,101]{1,0:T(2,128)S(1)}, f32[2,101]{1,0:T(2,128)}, u32[]{:S(2)}) copy-start(f32[2,101]{1,0:T(2,128)} %param.8) | copy-start | bytes 2428
  0.1 1.6 copy-start.5
  1.7 39.2 %copy-start.25 = (f32[2,31]{1,0:T(2,128)S(1)}, f32[2,31]{1,0:T(2,128)}, u32[]{:S(2)}) copy-start(f32[2,31]{1,0:T(2,128)} %param.6) | copy-start | bytes 748
  1.7 39.3 %copy-start.24 = (f32[2,31]{1,0:T(2,128)S(1)}, f32[2,31]{1,0:T(2,128)}, u32[]{:S(2)}) copy-start(f32[2,31]{1,0:T(2,128)} %param.7) | copy-start | bytes 748
  2.5 4.9 %collective-permute-start = (f32[32,16,128]{2,1,0:T(8,128)S(1)}, f32[32,16,128]{2,1,0:T(8,128)S(1)}, u32[]{:S(2)}, u32[]{:S(2)}) collective-permute-start(f32[32,16,128]{2,1,0:T(8,128)S(1)} %get-tuple-element.68), channel_id=1, source_target_pairs={{0,1},{1,0},{2,3},{3,2},{4,5},{5,4},{6,7},{7,6},{8,9},{9,8},{10,11... | collective-permute-start | bytes 786440 | tf_op jit(solution)/shard_map/ppermute | solution.py:349
  3.0 9.7 %collective-permute-start.1 = (f32[32,16,128]{2,1,0:T(8,128)S(1)}, f32[32,16,128]{2,1,0:T(8,128)S(1)}, u32[]{:S(2)}, u32[]{:S(2)}) collective-permute-start(f32[32,16,128]{2,1,0:T(8,128)S(1)} %get-tuple-element.69), channel_id=1, source_target_pairs={{0,2},{1,3},{2,0},{3,1},{4,6},{5,7},{6,4},{7,5},{8,10},{9,11},{10,... | collective-permute-start | bytes 786440 | tf_op jit(solution)/shard_map/ppermute | solution.py:349
  5.6 12.3 %collective-permute-start.2 = (f32[32,16,128]{2,1,0:T(8,128)S(1)}, f32[32,16,128]{2,1,0:T(8,128)S(1)}, u32[]{:S(2)}, u32[]{:S(2)}) collective-permute-start(f32[32,16,128]{2,1,0:T(8,128)S(1)} %get-tuple-element.70), channel_id=1, source_target_pairs={{0,3},{1,2},{2,1},{3,0},{4,7},{5,6},{6,5},{7,4},{8,11},{9,10},{10,... | collective-permute-start | bytes 786440 | tf_op jit(solution)/shard_map/ppermute | solution.py:349
  5.7 12.2 %collective-permute-start.3 = (f32[32,16,128]{2,1,0:T(8,128)S(1)}, f32[32,16,128]{2,1,0:T(8,128)S(1)}, u32[]{:S(2)}, u32[]{:S(2)}) collective-permute-start(f32[32,16,128]{2,1,0:T(8,128)S(1)} %get-tuple-element.71), channel_id=1, source_target_pairs={{0,4},{1,5},{2,6},{3,7},{4,0},{5,1},{6,2},{7,3},{8,12},{9,13},{10,... | collective-permute-start | bytes 786440 | tf_op jit(solution)/shard_map/ppermute | solution.py:349
  7.4 22.9 %collective-permute-start.4 = (f32[32,16,128]{2,1,0:T(8,128)S(1)}, f32[32,16,128]{2,1,0:T(8,128)S(1)}, u32[]{:S(2)}, u32[]{:S(2)}) collective-permute-start(f32[32,16,128]{2,1,0:T(8,128)S(1)} %get-tuple-element.72), channel_id=1, source_target_pairs={{0,5},{1,4},{2,7},{3,6},{4,1},{5,0},{6,3},{7,2},{8,13},{9,12},{10,... | collective-permute-start | bytes 786440 | tf_op jit(solution)/shard_map/ppermute | solution.py:349
  7.4 23.6 %collective-permute-start.5 = (f32[32,16,128]{2,1,0:T(8,128)S(1)}, f32[32,16,128]{2,1,0:T(8,128)S(1)}, u32[]{:S(2)}, u32[]{:S(2)}) collective-permute-start(f32[32,16,128]{2,1,0:T(8,128)S(1)} %get-tuple-element.73), channel_id=1, source_target_pairs={{0,6},{1,7},{2,4},{3,5},{4,2},{5,3},{6,0},{7,1},{8,14},{9,15},{10,... | collective-permute-start | bytes 786440 | tf_op jit(solution)/shard_map/ppermute | solution.py:349
  12.7 19.0 %collective-permute-start.6 = (f32[32,16,128]{2,1,0:T(8,128)S(1)}, f32[32,16,128]{2,1,0:T(8,128)S(1)}, u32[]{:S(2)}, u32[]{:S(2)}) collective-permute-start(f32[32,16,128]{2,1,0:T(8,128)S(1)} %get-tuple-element.74), channel_id=1, source_target_pairs={{0,7},{1,6},{2,5},{3,4},{4,3},{5,2},{6,1},{7,0},{8,15},{9,14},{10,... | collective-permute-start | bytes 786440 | tf_op jit(solution)/shard_map/ppermute | solution.py:349
  30.3 0.7 copy-start.18
  31.0 0.7 copy-start.20
  31.8 0.7 copy-start.22
  32.5 0.9 copy-start.19
  33.4 0.9 copy-start.21
  34.4 0.9 copy-start.23
  38.9 14.7 %collective-permute-start.7 = (f32[8,64,128]{2,1,0:T(8,128)}, f32[8,64,128]{2,1,0:T(8,128)}, u32[]{:S(2)}, u32[]{:S(2)}) collective-permute-start(f32[8,64,128]{2,1,0:T(8,128)} %get-tuple-element.80), channel_id=1, source_target_pairs={{0,1},{1,0},{2,3},{3,2},{4,5},{5,4},{6,7},{7,6},{8,9},{9,8},{10,11... | collective-permute-start | bytes 786440 | tf_op jit(solution)/shard_map/ppermute | solution.py:401
  39.5 14.1 %collective-permute-start.8 = (f32[8,64,128]{2,1,0:T(8,128)}, f32[8,64,128]{2,1,0:T(8,128)}, u32[]{:S(2)}, u32[]{:S(2)}) collective-permute-start(f32[8,64,128]{2,1,0:T(8,128)} %get-tuple-element.81), channel_id=1, source_target_pairs={{1,4},{4,1},{3,6},{6,3},{9,12},{12,9},{11,14},{14,11},{17,20},{20,... | collective-permute-start | bytes 786440 | tf_op jit(solution)/shard_map/ppermute | solution.py:400
  45.0 0.8 copy-start
  45.8 0.7 copy-start.14
  46.4 10.1 %copy-start.3 = (bf16[4,256,256]{2,1,0:T(8,128)(2,1)}, bf16[4,256,256]{2,1,0:T(8,128)(2,1)S(1)}, u32[]{:S(2)}) copy-start(bf16[4,256,256]{2,1,0:T(8,128)(2,1)S(1)} %get-tuple-element.82.wh) | copy-start | bytes 1572868
  46.4 10.1 %copy-start.6 = (f32[31,8,128]{2,1,0:T(8,128)}, f32[31,8,128]{2,1,0:T(8,128)S(1)}, u32[]{:S(2)}) copy-start(f32[31,8,128]{2,1,0:T(8,128)S(1)} %get-tuple-element.86.wy) | copy-start | bytes 380932
  46.4 10.1 %copy-start.16 = (bf16[256,256]{1,0:T(8,128)(2,1)}, bf16[256,256]{1,0:T(8,128)(2,1)S(1)}, u32[]{:S(2)}) copy-start(bf16[256,256]{1,0:T(8,128)(2,1)S(1)} %get-tuple-element.77.wx) | copy-start | bytes 393220
  46.4 15.1 %copy-start.27 = (s32[1,4,32]{2,1,0:T(4,128)S(1)}, s32[1,4,32]{2,1,0:T(4,128)}, u32[]{:S(2)}) copy-start(s32[1,4,32]{2,1,0:T(4,128)} %param.9) | copy-start | bytes 1540
  52.6 1.0 copy-start.8
  56.5 1.0 copy-start.10
  57.5 0.8 copy-start.12
  58.3 19.8 %collective-permute-start.9 = (f32[15,64,128]{2,1,0:T(8,128)}, f32[15,64,128]{2,1,0:T(8,128)}, u32[]{:S(2)}, u32[]{:S(2)}) collective-permute-start(f32[15,64,128]{2,1,0:T(8,128)} %get-tuple-element.87), channel_id=1, source_target_pairs={{0,8},{8,0},{16,24},{24,16},{1,9},{9,1},{17,25},{25,17},{2,10},{10... | collective-permute-start | bytes 1474568 | tf_op jit(solution)/shard_map/ppermute | solution.py:409
  60.1 18.1 %collective-permute-start.10 = (f32[15,64,128]{2,1,0:T(8,128)}, f32[15,64,128]{2,1,0:T(8,128)}, u32[]{:S(2)}, u32[]{:S(2)}) collective-permute-start(f32[15,64,128]{2,1,0:T(8,128)} %get-tuple-element.88), channel_id=1, source_target_pairs={{8,16},{16,8},{9,17},{17,9},{10,18},{18,10},{11,19},{19,11},{12,20... | collective-permute-start | bytes 1474568 | tf_op jit(solution)/shard_map/ppermute | solution.py:410
  61.6 3.9 %collective-permute-start.11 = (s32[4,32]{1,0:T(4,128)S(1)}, s32[4,32]{1,0:T(4,128)S(1)}, u32[]{:S(2)}, u32[]{:S(2)}) collective-permute-start(s32[4,32]{1,0:T(4,128)S(1)} %bitcast.17), channel_id=1, source_target_pairs={{0,4},{4,0},{1,5},{5,1},{2,6},{6,2},{3,7},{7,3},{8,12},{12,8},{9,1... | collective-permute-start | bytes 1544 | tf_op jit(solution)/shard_map/ppermute | solution.py:371
  67.6 1.0 copy-start.1
  68.6 0.9 copy-start.7
  69.5 1.2 copy-start.9
  70.8 1.2 copy-start.11
  72.0 1.0 copy-start.13
  78.3 6.6 %copy-start.15 = (bf16[256,256]{1,0:T(8,128)(2,1)S(1)}, bf16[256,256]{1,0:T(8,128)(2,1)}, u32[]{:S(2)}) copy-start(bf16[256,256]{1,0:T(8,128)(2,1)} %copy-done.14) | copy-start | bytes 393220
  83.3 7.8 %collective-permute-start.12 = (f32[8,64,128]{2,1,0:T(8,128)S(1)}, f32[8,64,128]{2,1,0:T(8,128)S(1)}, u32[]{:S(2)}, u32[]{:S(2)}) collective-permute-start(f32[8,64,128]{2,1,0:T(8,128)S(1)} %get-tuple-element.94), channel_id=1, source_target_pairs={{0,1},{1,0},{2,3},{3,2},{4,5},{5,4},{6,7},{7,6},{8,9},{9,8},{10,11... | collective-permute-start | bytes 786440 | tf_op jit(solution)/shard_map/ppermute | solution.py:401
  84.2 6.9 %collective-permute-start.13 = (f32[8,64,128]{2,1,0:T(8,128)S(1)}, f32[8,64,128]{2,1,0:T(8,128)S(1)}, u32[]{:S(2)}, u32[]{:S(2)}) collective-permute-start(f32[8,64,128]{2,1,0:T(8,128)S(1)} %get-tuple-element.95), channel_id=1, source_target_pairs={{1,4},{4,1},{3,6},{6,3},{9,12},{12,9},{11,14},{14,11},{17,20},{20,... | collective-permute-start | bytes 786440 | tf_op jit(solution)/shard_map/ppermute | solution.py:400
  92.6 13.4 %collective-permute-start.14 = (f32[15,64,128]{2,1,0:T(8,128)S(1)}, f32[15,64,128]{2,1,0:T(8,128)S(1)}, u32[]{:S(2)}, u32[]{:S(2)}) collective-permute-start(f32[15,64,128]{2,1,0:T(8,128)S(1)} %get-tuple-element.101), channel_id=1, source_target_pairs={{0,8},{8,0},{16,24},{24,16},{1,9},{9,1},{17,25},{25,17},{2,10},{10... | collective-permute-start | bytes 1474568 | tf_op jit(solution)/shard_map/ppermute | solution.py:409
  96.1 9.9 %collective-permute-start.15 = (f32[15,64,128]{2,1,0:T(8,128)S(1)}, f32[15,64,128]{2,1,0:T(8,128)S(1)}, u32[]{:S(2)}, u32[]{:S(2)}) collective-permute-start(f32[15,64,128]{2,1,0:T(8,128)S(1)} %get-tuple-element.102), channel_id=1, source_target_pairs={{8,16},{16,8},{9,17},{17,9},{10,18},{18,10},{11,19},{19,11},{12,20... | collective-permute-start | bytes 1474568 | tf_op jit(solution)/shard_map/ppermute | solution.py:410
  102.0 10.9 %copy-start.17 = (bf16[256,256]{1,0:T(8,128)(2,1)S(1)}, bf16[256,256]{1,0:T(8,128)(2,1)}, u32[]{:S(2)}) copy-start(bf16[256,256]{1,0:T(8,128)(2,1)} %copy-done.16) | copy-start | bytes 393220
  110.2 9.0 %copy-start.4 = (bf16[4,256,256]{2,1,0:T(8,128)(2,1)S(1)}, bf16[4,256,256]{2,1,0:T(8,128)(2,1)}, u32[]{:S(2)}) copy-start(bf16[4,256,256]{2,1,0:T(8,128)(2,1)} %copy-done.3) | copy-start | bytes 1572868
  110.2 9.0 %collective-permute-start.16 = (f32[8,64,128]{2,1,0:T(8,128)S(1)}, f32[8,64,128]{2,1,0:T(8,128)S(1)}, u32[]{:S(2)}, u32[]{:S(2)}) collective-permute-start(f32[8,64,128]{2,1,0:T(8,128)S(1)} %get-tuple-element.106), channel_id=1, source_target_pairs={{0,1},{1,0},{2,3},{3,2},{4,5},{5,4},{6,7},{7,6},{8,9},{9,8},{10,11... | collective-permute-start | bytes 786440 | tf_op jit(solution)/shard_map/ppermute | solution.py:401
  112.2 6.9 %collective-permute-start.17 = (f32[8,64,128]{2,1,0:T(8,128)S(1)}, f32[8,64,128]{2,1,0:T(8,128)S(1)}, u32[]{:S(2)}, u32[]{:S(2)}) collective-permute-start(f32[8,64,128]{2,1,0:T(8,128)S(1)} %get-tuple-element.107), channel_id=1, source_target_pairs={{1,4},{4,1},{3,6},{6,3},{9,12},{12,9},{11,14},{14,11},{17,20},{20,... | collective-permute-start | bytes 786440 | tf_op jit(solution)/shard_map/ppermute | solution.py:400
  112.9 12.4 %copy-start.2 = (bf16[4,256,256]{2,1,0:T(8,128)(2,1)S(1)}, bf16[4,256,256]{2,1,0:T(8,128)(2,1)}, u32[]{:S(2)}) copy-start(bf16[4,256,256]{2,1,0:T(8,128)(2,1)} %copy-done) | copy-start | bytes 1572868
  120.7 14.0 %collective-permute-start.18 = (f32[15,64,128]{2,1,0:T(8,128)S(1)}, f32[15,64,128]{2,1,0:T(8,128)S(1)}, u32[]{:S(2)}, u32[]{:S(2)}) collective-permute-start(f32[15,64,128]{2,1,0:T(8,128)S(1)} %get-tuple-element.110), channel_id=1, source_target_pairs={{0,8},{8,0},{16,24},{24,16},{1,9},{9,1},{17,25},{25,17},{2,10},{10... | collective-permute-start | bytes 1474568 | tf_op jit(solution)/shard_map/ppermute | solution.py:409
  124.6 10.0 %collective-permute-start.19 = (f32[15,64,128]{2,1,0:T(8,128)S(1)}, f32[15,64,128]{2,1,0:T(8,128)S(1)}, u32[]{:S(2)}, u32[]{:S(2)}) collective-permute-start(f32[15,64,128]{2,1,0:T(8,128)S(1)} %get-tuple-element.111), channel_id=1, source_target_pairs={{8,16},{16,8},{9,17},{17,9},{10,18},{18,10},{11,19},{19,11},{12,20... | collective-permute-start | bytes 1474568 | tf_op jit(solution)/shard_map/ppermute | solution.py:410
  139.0 8.9 %collective-permute-start.20 = (f32[8,64,128]{2,1,0:T(8,128)S(1)}, f32[8,64,128]{2,1,0:T(8,128)S(1)}, u32[]{:S(2)}, u32[]{:S(2)}) collective-permute-start(f32[8,64,128]{2,1,0:T(8,128)S(1)} %get-tuple-element.115), channel_id=1, source_target_pairs={{0,1},{1,0},{2,3},{3,2},{4,5},{5,4},{6,7},{7,6},{8,9},{9,8},{10,11... | collective-permute-start | bytes 786440 | tf_op jit(solution)/shard_map/ppermute | solution.py:401
  140.9 7.0 %collective-permute-start.21 = (f32[8,64,128]{2,1,0:T(8,128)S(1)}, f32[8,64,128]{2,1,0:T(8,128)S(1)}, u32[]{:S(2)}, u32[]{:S(2)}) collective-permute-start(f32[8,64,128]{2,1,0:T(8,128)S(1)} %get-tuple-element.116), channel_id=1, source_target_pairs={{1,4},{4,1},{3,6},{6,3},{9,12},{12,9},{11,14},{14,11},{17,20},{20,... | collective-permute-start | bytes 786440 | tf_op jit(solution)/shard_map/ppermute | solution.py:400
  149.4 14.5 %collective-permute-start.22 = (f32[15,64,128]{2,1,0:T(8,128)S(1)}, f32[15,64,128]{2,1,0:T(8,128)S(1)}, u32[]{:S(2)}, u32[]{:S(2)}) collective-permute-start(f32[15,64,128]{2,1,0:T(8,128)S(1)} %get-tuple-element.119), channel_id=1, source_target_pairs={{0,8},{8,0},{16,24},{24,16},{1,9},{9,1},{17,25},{25,17},{2,10},{10... | collective-permute-start | bytes 1474568 | tf_op jit(solution)/shard_map/ppermute | solution.py:409
  153.4 10.5 %collective-permute-start.23 = (f32[15,64,128]{2,1,0:T(8,128)S(1)}, f32[15,64,128]{2,1,0:T(8,128)S(1)}, u32[]{:S(2)}, u32[]{:S(2)}) collective-permute-start(f32[15,64,128]{2,1,0:T(8,128)S(1)} %get-tuple-element.120), channel_id=1, source_target_pairs={{8,16},{16,8},{9,17},{17,9},{10,18},{18,10},{11,19},{19,11},{12,20... | collective-permute-start | bytes 1474568 | tf_op jit(solution)/shard_map/ppermute | solution.py:410
  166.0 5.0 %collective-permute-start.24 = (f32[32,16,128]{2,1,0:T(8,128)S(1)}, f32[32,16,128]{2,1,0:T(8,128)S(1)}, u32[]{:S(2)}, u32[]{:S(2)}) collective-permute-start(f32[32,16,128]{2,1,0:T(8,128)S(1)} %get-tuple-element.122), channel_id=1, source_target_pairs={{0,1},{1,0},{2,3},{3,2},{4,5},{5,4},{6,7},{7,6},{8,9},{9,8},{10,11... | collective-permute-start | bytes 786440 | tf_op jit(solution)/shard_map/ppermute | solution.py:349
  167.5 9.2 %collective-permute-start.25 = (f32[32,16,128]{2,1,0:T(8,128)S(1)}, f32[32,16,128]{2,1,0:T(8,128)S(1)}, u32[]{:S(2)}, u32[]{:S(2)}) collective-permute-start(f32[32,16,128]{2,1,0:T(8,128)S(1)} %get-tuple-element.123), channel_id=1, source_target_pairs={{0,2},{1,3},{2,0},{3,1},{4,6},{5,7},{6,4},{7,5},{8,10},{9,11},{10,... | collective-permute-start | bytes 786440 | tf_op jit(solution)/shard_map/ppermute | solution.py:349
  169.0 12.3 %collective-permute-start.26 = (f32[32,16,128]{2,1,0:T(8,128)S(1)}, f32[32,16,128]{2,1,0:T(8,128)S(1)}, u32[]{:S(2)}, u32[]{:S(2)}) collective-permute-start(f32[32,16,128]{2,1,0:T(8,128)S(1)} %get-tuple-element.124), channel_id=1, source_target_pairs={{0,3},{1,2},{2,1},{3,0},{4,7},{5,6},{6,5},{7,4},{8,11},{9,10},{10,... | collective-permute-start | bytes 786440 | tf_op jit(solution)/shard_map/ppermute | solution.py:349
  169.1 12.3 %collective-permute-start.27 = (f32[32,16,128]{2,1,0:T(8,128)S(1)}, f32[32,16,128]{2,1,0:T(8,128)S(1)}, u32[]{:S(2)}, u32[]{:S(2)}) collective-permute-start(f32[32,16,128]{2,1,0:T(8,128)S(1)} %get-tuple-element.125), channel_id=1, source_target_pairs={{0,4},{1,5},{2,6},{3,7},{4,0},{5,1},{6,2},{7,3},{8,12},{9,13},{10,... | collective-permute-start | bytes 786440 | tf_op jit(solution)/shard_map/ppermute | solution.py:349
  170.3 24.1 %collective-permute-start.28 = (f32[32,16,128]{2,1,0:T(8,128)S(1)}, f32[32,16,128]{2,1,0:T(8,128)S(1)}, u32[]{:S(2)}, u32[]{:S(2)}) collective-permute-start(f32[32,16,128]{2,1,0:T(8,128)S(1)} %get-tuple-element.126), channel_id=1, source_target_pairs={{0,5},{1,4},{2,7},{3,6},{4,1},{5,0},{6,3},{7,2},{8,13},{9,12},{10,... | collective-permute-start | bytes 786440 | tf_op jit(solution)/shard_map/ppermute | solution.py:349
  171.0 23.4 %collective-permute-start.29 = (f32[32,16,128]{2,1,0:T(8,128)S(1)}, f32[32,16,128]{2,1,0:T(8,128)S(1)}, u32[]{:S(2)}, u32[]{:S(2)}) collective-permute-start(f32[32,16,128]{2,1,0:T(8,128)S(1)} %get-tuple-element.127), channel_id=1, source_target_pairs={{0,6},{1,7},{2,4},{3,5},{4,2},{5,3},{6,0},{7,1},{8,14},{9,15},{10,... | collective-permute-start | bytes 786440 | tf_op jit(solution)/shard_map/ppermute | solution.py:349
  176.7 17.7 %collective-permute-start.30 = (f32[32,16,128]{2,1,0:T(8,128)S(1)}, f32[32,16,128]{2,1,0:T(8,128)S(1)}, u32[]{:S(2)}, u32[]{:S(2)}) collective-permute-start(f32[32,16,128]{2,1,0:T(8,128)S(1)} %get-tuple-element.128), channel_id=1, source_target_pairs={{0,7},{1,6},{2,5},{3,4},{4,3},{5,2},{6,1},{7,0},{8,15},{9,14},{10,... | collective-permute-start | bytes 786440 | tf_op jit(solution)/shard_map/ppermute | solution.py:349

commit v2 on v1

--- a/solution.py
+++ b/solution.py
@@ -13,7 +13,7 @@
 F32, BF16 = jnp.float32, jnp.bfloat16
 VMEM = pl.BlockSpec(memory_space=pltpu.VMEM)
 SMEM = pl.BlockSpec(memory_space=pltpu.SMEM)
-PARAMS = pltpu.CompilerParams(vmem_limit_bytes=40 * 1024 * 1024)
+PARAMS = pltpu.CompilerParams(vmem_limit_bytes=16 * 1024 * 1024)
 
 
 def shape(dims, dtype=F32):
@@ -48,23 +48,27 @@
         out[zh, :, :, pl.ds(start, LANES)] = pieces[d][...]
 
 
-def pack_strips(me, cells, to_pair, to_next):
+def pack_tile(me, z, cells, to_pair, to_next):
     groups = LANES // STRIP
-    lane_group = lax.broadcasted_iota(jnp.int32, (cells.shape[1], LANES), 1) // STRIP
-    left_first = me[2] == 1
-    for out, edge in (
-        (to_pair, jnp.where(left_first, 0, LANES - STRIP)),
-        (to_next, jnp.where(left_first, LANES - STRIP, 0)),
-    ):
-        def one(y, _):
-            total = jnp.zeros((cells.shape[1], LANES), F32)
-            for j in range(groups):
-                shift = lax.rem(STRIP * j - edge + LANES, LANES)
-                total = jnp.where(lane_group == j, pltpu.roll(cells[groups * j + y], shift, 1), total)
-            out[y] = total
-            return 0
-
-        lax.fori_loop(0, groups, one, 0)
+    lane_group = lax.broadcasted_iota(jnp.int32, (8, LANES), 1) // STRIP
+    left_first = jnp.full((8, LANES), me[2], jnp.int32) == 1
+    for y in range(groups):
+        left = right = None
+        for j in range(groups):
+            cell = cells[groups * j + y]
+            cell = pltpu.roll(cell, STRIP * j, 1) if j else cell
+            left = cell if left is None else jnp.where(lane_group == j, cell, left)
+            right = cell if right is None else jnp.where(lane_group == j - 1, cell, right)
+        to_pair[y, z, :] = jnp.where(left_first, left, right)
+        to_next[y, z, :] = jnp.where(left_first, right, left)
+
+
+def tiles(depth, body):
+    def one(t, _):
+        body(pl.ds(pl.multiple_of(8 * t, 8), 8))
+        return 0
+
+    lax.fori_loop(0, depth // 8, one, 0)
 
 
 def join_kernel(me, *rest):
@@ -76,7 +80,11 @@
         y0 = pl.multiple_of(yl * rows, rows)
         z0 = pl.multiple_of((2 * zh + zl) * depth, depth)
         cells[pl.ds(y0, rows), pl.ds(z0, depth), :] = pieces[d][...]
-    pack_strips(me, cells, to_pair, to_next)
+
+    def tile(z):
+        pack_tile(me, z, [cells[y, z, :] for y in range(2 * rows)], to_pair, to_next)
+
+    tiles(4 * depth, tile)
 
 
 def weights_kernel(me, rows, columns, axial, *outs):
@@ -121,9 +129,11 @@
         for k, first in ((0, me[2] == 0), (1, me[2] == 1)):
             source = iota(dims, 0) + jnp.where(first, nx, -STRIP)
             both = jnp.concatenate(halves(toeplitz(columns, offsets(source, iota(dims, 1), radius))), 1)
-            for j in range(nx // STRIP):
+            groups = nx // STRIP
+            for j in range(groups):
                 ref, at = place(j, wh_edge, wh_inner)
-                ref[at, k * nx + STRIP * j : k * nx + STRIP * (j + 1), :] = both
+                group = jnp.where(first, j, (j + groups - 1) % groups)
+                ref[at, pl.ds(pl.multiple_of(k * nx + STRIP * group, STRIP), STRIP), :] = both
         for i in range(rows.shape[1]):
             k = rows.shape[1] - 1 - i if flip else i
             wy[i] = jnp.full((8, LANES), rows[channel, k], F32)
@@ -150,27 +160,13 @@
 
 def own_kernel(cells, wz, wx, edge, inner):
     rows, depth = cells.shape[:2]
-
-    def one(g, _):
-        slabs = blur_z(wz[...], [cells[4 * g + i] for i in range(4)])
-        out = dot(jnp.concatenate(halves(jnp.concatenate(slabs, 0)), 1), wx[...])
-        out = (out[:, :LANES] + out[:, LANES:]).reshape(4, depth, LANES)
-
-        @pl.when(g < rows // 16)
-        def _():
-            edge[pl.ds(4 * g, 4)] = out
-
-        @pl.when(g >= 3 * rows // 16)
-        def _():
-            edge[pl.ds(4 * g - rows // 2, 4)] = out
-
-        @pl.when((g >= rows // 16) & (g < 3 * rows // 16))
-        def _():
-            inner[pl.ds(4 * g - rows // 4, 4)] = out
-
-        return 0
-
-    lax.fori_loop(0, rows // 4, one, 0)
+    quarter = rows // 4
+    for first, out, at in ((0, edge, 0), (3 * quarter, edge, quarter), (quarter, inner, 0), (2 * quarter, inner, quarter)):
+        slabs = []
+        for g in range(quarter // 4):
+            slabs += blur_z(wz[...], [cells[first + 4 * g + i] for i in range(4)])
+        both = dot(jnp.concatenate(halves(jnp.concatenate(slabs, 0)), 1), wx[...])
+        out[at : at + quarter] = (both[:, :LANES] + both[:, LANES:]).reshape(quarter, depth, LANES)
 
 
 def strip_terms(strips, weights):
@@ -244,75 +240,61 @@
     lax.fori_loop(0, depth // 8, one, 0)
 
 
-def add_halo(me, part, recv_a, recv_b, wy, halo, blurred):
+def with_halo(me, part, recv_a, recv_b, wy, halo, body):
     rows, depth = part.shape[:2]
     radius = wy.shape[0] // 2
     even = me[3] == 0
     halo[jnp.where(even, 1, 0)] = recv_a[...]
     halo[jnp.where(even, 0, 1)] = recv_b[...]
 
-    def one(t, _):
-        z = pl.ds(pl.multiple_of(8 * t, 8), 8)
+    def tile(z):
         taps = [wy[i] for i in range(wy.shape[0])]
+        sums = [part[y, z, :] for y in range(rows)]
         for side in range(2):
-            sums = {}
             for h in range(radius):
                 y = h - radius if side == 0 else rows + h
                 cell = halo[side, h, z, :]
                 for o in range(radius) if side == 0 else range(rows - radius, rows):
                     i = y - o + radius
                     if 0 <= i < len(taps):
-                        term = taps[i] * cell
-                        sums[o] = sums[o] + term if o in sums else term
-            for o in sums:
-                blurred[o, z, :] = part[o, z, :] + sums[o]
-        return 0
-
-    lax.fori_loop(0, depth // 8, one, 0)
-
-
-def each_row(rows, radius, part, blurred, do):
-    def one(y, _):
-        do(y, part[y])
-        return 0
-
-    def edge(y, _):
-        do(y, blurred[y])
-        return 0
-
-    lax.fori_loop(0, radius, edge, 0)
-    lax.fori_loop(radius, rows - radius, one, 0)
-    lax.fori_loop(rows - radius, rows, edge, 0)
-
-
-def quotient_kernel(me, part, recv_a, recv_b, wy, observed, live, out, to_pair, to_next, halo, blurred):
-    add_halo(me, part, recv_a, recv_b, wy, halo, blurred)
-    rows = part.shape[0]
-
-    def do(y, value):
-        out[y] = jnp.where(live[y // BY] != 0, observed[y] / value, 1.0)
-
-    each_row(rows, wy.shape[0] // 2, part, blurred, do)
-    pack_strips(me, out, to_pair, to_next)
-
-
-def correct(me, part, recv_a, recv_b, wy, estimate, live, out, halo, blurred):
-    add_halo(me, part, recv_a, recv_b, wy, halo, blurred)
-
-    def do(y, value):
-        out[y] = jnp.where(live[y // BY] != 0, estimate[y] * value, estimate[y])
-
-    each_row(part.shape[0], wy.shape[0] // 2, part, blurred, do)
-
-
-def estimate_kernel(me, part, recv_a, recv_b, wy, estimate, live, out, to_pair, to_next, halo, blurred):
-    correct(me, part, recv_a, recv_b, wy, estimate, live, out, halo, blurred)
-    pack_strips(me, out, to_pair, to_next)
+                        sums[o] = sums[o] + taps[i] * cell
+        body(z, sums)
+
+    tiles(depth, tile)
+
+
+def quotient_kernel(me, part, recv_a, recv_b, wy, observed, live, out, to_pair, to_next, halo):
+    def body(z, blurred):
+        cells = []
+        for y in range(len(blurred)):
+            cells.append(jnp.where(live[y // BY, z, :] != 0, observed[y, z, :] / blurred[y], 1.0))
+            out[y, z, :] = cells[y]
+        pack_tile(me, z, cells, to_pair, to_next)
+
+    with_halo(me, part, recv_a, recv_b, wy, halo, body)
+
+
+def estimate_kernel(me, part, recv_a, recv_b, wy, estimate, live, out, to_pair, to_next, halo):
+    def body(z, blurred):
+        cells = []
+        for y in range(len(blurred)):
+            cell = estimate[y, z, :]
+            cells.append(jnp.where(live[y // BY, z, :] != 0, cell * blurred[y], cell))
+            out[y, z, :] = cells[y]
+        pack_tile(me, z, cells, to_pair, to_next)
+
+    with_halo(me, part, recv_a, recv_b, wy, halo, body)
 
 
 def last_kernel(me, part, recv_a, recv_b, wy, estimate, live, *rest):
-    pieces, out, halo, blurred = rest[:8], rest[8], rest[9], rest[10]
-    correct(me, part, recv_a, recv_b, wy, estimate, live, out, halo, blurred)
+    pieces, out, halo = rest[:8], rest[8], rest[9]
+
+    def body(z, blurred):
+        for y in range(len(blurred)):
+            cell = estimate[y, z, :]
+            out[y, z, :] = jnp.where(live[y // BY, z, :] != 0, cell * blurred[y], cell)
+
+    with_halo(me, part, recv_a, recv_b, wy, halo, body)
     rows, depth = pieces[0].shape[:2]
     for d in range(8):
         yl, zh, zl = other((me[0], me[1], me[2]), d)
@@ -387,6 +369,7 @@
     half = shape((ny // 2, nz, LANES))
     strip = shape((LANES // STRIP, nz, LANES))
     halo = shape((radius, nz, LANES))
+    pieces, weights, live = lax.optimization_barrier((pieces, weights, live))
     taken, to_pair, to_next = call(
         join_kernel, [whole, strip, strip], [SMEM] + [VMEM] * 8, us=4, name="join"
     )(me, *pieces)
@@ -414,7 +397,7 @@
         )(own_inner, edge, strips, wh_inner, wy)
         return part, recv_a, recv_b, wy
 
-    scratch = [pltpu.VMEM((2,) + halo.shape, F32), pltpu.VMEM(whole.shape, F32)]
+    scratch = [pltpu.VMEM((2,) + halo.shape, F32)]
     estimate = taken
     for iteration in range(ITERS):
         found = blur(estimate, to_pair, to_next, weights[:5])

time: 199 us -> 157 us (0.79)
  Pallas kernels: 78.6 us -> 51.5 us
  waiting for transfers between devices: 53.5 us -> 38.6 us
  starting transfers between devices: 44.8 us -> 58.9 us
  local copies, waits for them, and re-layouts: 18.6 us -> 4.64 us
    pallas_call x4, Pallas kernels: 24.6 us -> 6.11 us  [blur(): call(own_kernel, [half, half], [VMEM] * 3, us=6, name='own')(cells, wz, wx)]
    unnamed x56 -> x16, local copies, waits for them, and re-layouts: 16.3 us -> 3.71 us
    ppermute x4, starting transfers between devices: 5.47 us -> 15.6 us  [blur(): pair = lax.ppermute(to_pair, 'zl', [(0, 1), (1, 0)])]
    ppermute x4, waiting for transfers between devices: 12.7 us -> 4.53 us  [blur(): recv_a = lax.ppermute(send_a, 'yh', evens)]
    ppermute x14, waiting for transfers between devices: 39.3 us -> 34 us  [trade(): lax.ppermute(pieces[d], group, [(i, i ^ d) for i in range(8)])]
    pallas_call x2, Pallas kernels: 9.27 us -> 4.35 us  [per_device(): call(quotient_kernel, [whole, strip, strip], [SMEM] + [VMEM] * 6, scratch...]
    ppermute x14, starting transfers between devices: 16.7 us -> 20.5 us  [trade(): lax.ppermute(pieces[d], group, [(i, i ^ d) for i in range(8)])]
    pallas_call x1, Pallas kernels: 4.15 us -> 2.13 us  [per_device(): call(estimate_kernel, [whole, strip, strip], [SMEM] + [VMEM] * 6, scratch...]
  transfers between devices with their start and end apart: 31 -> 31, of which waited for: 10 -> 9; matrix products, arithmetic and copies ran while one was open for 1% -> 1% of each run, Pallas kernels for 25% -> 21%
where the time goes in v2:
time: 157 us; the launch traced here: 155 us
  starting transfers between devices  58.9 us (38%)
  Pallas kernels  51.5 us (33%)
  waiting for transfers between devices  38.6 us (25%)
  local copies, waits for them, and re-layouts  4.64 us (3%)
    ppermute x14, waiting for transfers between devices, trade(): lax.ppermute(pieces[d], group, [(i, i ^ d) for i in range(8)])  34 us
    pallas_call x4, Pallas kernels, blur(): call(inner_kernel, whole, [VMEM] * 5, [pltpu.VMEM(half.shape, F32)], us=5...  20.7 us
    ppermute x14, starting transfers between devices, trade(): lax.ppermute(pieces[d], group, [(i, i ^ d) for i in range(8)])  20.5 us
    ppermute x4, starting transfers between devices, blur(): pair = lax.ppermute(to_pair, 'zl', [(0, 1), (1, 0)])  15.6 us
    ppermute x4, starting transfers between devices, blur(): recv_a = lax.ppermute(send_a, 'yh', evens)  14.3 us
    pallas_call x4, Pallas kernels, blur(): call(own_kernel, [half, half], [VMEM] * 3, us=6, name='own')(cells, wz, wx)  6.11 us
    pallas_call x4, Pallas kernels, blur(): call(edge_kernel, [half, shape((2 * strip.shape[0] * nz, 2 * LANES), BF16...  6.05 us
    ppermute x4, waiting for transfers between devices, blur(): recv_a = lax.ppermute(send_a, 'yh', evens)  4.53 us
  transfers between devices with their start and end apart: 31, of which 9 were waited for; matrix products, arithmetic and copies ran while one was open for 1% of the time, Pallas kernels for 21%

profile of v2, /device:TPU:0, one launch (start us, length us, event | category | flops | bytes accessed | tf_op | source)
XLA Modules:
  0.0 154.8 jit_solution(494715696868833130)
XLA Ops:
  0.0 3.0 %collective-permute-start.7 = (s32[4,32]{1,0:T(4,128)}, s32[4,32]{1,0:T(4,128)S(1)}, u32[]{:S(2)}, u32[]{:S(2)}) collective-permute-start(s32[4,32]{1,0:T(4,128)} %bitcast.17), channel_id=1, source_target_pairs={{0,4},{4,0},{1,5},{5,1},{2,6},{6,2},{3,7},{7,3},{8,12},{12,8},{9,1... | collective-permute-start | bytes 1544 | tf_op jit(solution)/shard_map/ppermute | solution.py:353
  3.1 1.6 %copy-done = f32[2,32,16,512]{3,2,1,0:T(8,128)S(1)} copy-done((f32[2,32,16,512]{3,2,1,0:T(8,128)S(1)}, f32[2,32,16,512]{3,2,1,0:T(8,128)}, u32[]{:S(2)}) %copy-start) | copy-done | bytes 2097176
  4.7 1.7 %deal.1 = (f32[32,16,128]{2,1,0:T(8,128)S(1)}, f32[32,16,128]{2,1,0:T(8,128)}, f32[32,16,128]{2,1,0:T(8,128)}, f32[32,16,128]{2,1,0:T(8,128)}, f32[32,16,128]{2,...) custom-call(s32[4]{0:T(128)S(1)} %pad_add_fusion.me, ...), custom_call_target="tpu_custom_call" | custom-call | bytes 9000000 | tf_op jit(solution)/shard_map/deal/pallas_call | solution.py:335
  6.4 0.7 copy-done.1
  7.1 0.7 copy-done.2
  7.8 0.7 copy-done.3
  8.5 1.5 collective-permute-start.1
  10.0 0.4 collective-permute-start.2
  10.4 0.3 collective-permute-start.3
  11.4 3.8 %weights.1 = (bf16[256,256]{1,0:T(8,128)(2,1)S(1)}, bf16[256,256]{1,0:T(8,128)(2,1)S(1)}, bf16[4,256,256]{2,1,0:T(8,128)(2,1)S(1)}, bf16[4,256,256]{2,1,0:T(8,12...) custom-call(s32[4]{0:T(128)S(1)} %pad_add_fusion.me, ...), custom_call_target="tpu_custom_call" | custom-call | bytes 12000000 | tf_op jit(solution)/shard_map/weights/pallas_call | solution.py:348
  15.2 1.4 collective-permute-start.4
  16.6 1.4 collective-permute-start.5
  18.1 1.3 collective-permute-start.6
  19.6 0.1 copy.21
  19.8 0.1 copy.20
  20.2 2.6 %collective-permute-done.2.rest_3_ = f32[32,16,128]{2,1,0:T(8,128)} collective-permute-done((f32[32,16,128]{2,1,0:T(8,128)}, f32[32,16,128]{2,1,0:T(8,128)}, u32[]{:S(2)}, u32[]{:S(2)}) %collective-permute-start.2) | collective-permute-done | bytes 262176 | tf_op jit(solution)/shard_map/ppermute | solution.py:331
  22.8 12.7 %collective-permute-done.4.rest_5_ = f32[32,16,128]{2,1,0:T(8,128)} collective-permute-done((f32[32,16,128]{2,1,0:T(8,128)}, f32[32,16,128]{2,1,0:T(8,128)}, u32[]{:S(2)}, u32[]{:S(2)}) %collective-permute-start.4) | collective-permute-done | bytes 262176 | tf_op jit(solution)/shard_map/ppermute | solution.py:331
  35.5 0.1 broadcast_in_dim.5.live
  35.6 2.5 %join.1 = (f32[64,64,128]{2,1,0:T(8,128)S(1)}, f32[8,64,128]{2,1,0:T(8,128)S(1)}, f32[8,64,128]{2,1,0:T(8,128)S(1)}) custom-call(s32[4]{0:T(128)S(1)} %pad_add_fusion.me, f32[32,16,128]{2,1,0:T(8,128)S(1)} %get-tuple-element.104.rest_0_, f32[32,16,128]{2,1,0:T(8,128)S(1)} %collective-permute-done.rest_1_, f32[32,16,128]{2,1,0:T(8,128)} %collective-permute-done.1.rest_2_, ...), custom_call_target="tpu_custom_call" | custom-call | bytes 12000000 | tf_op jit(solution)/shard_map/join/pallas_call | solution.py:373
  38.2 0.5 collective-permute-start.8
  38.6 0.7 collective-permute-start.9
  39.3 1.5 own.4
  40.9 1.5 edge.4
  42.4 1.6 %collective-permute-start.10 = (f32[15,64,128]{2,1,0:T(8,128)S(1)}, f32[15,64,128]{2,1,0:T(8,128)S(1)}, u32[]{:S(2)}, u32[]{:S(2)}) collective-permute-start(f32[15,64,128]{2,1,0:T(8,128)S(1)} %get-tuple-element.124), channel_id=1, source_target_pairs={{0,8},{8,0},{16,24},{24,16},{1,9},{9,1},{17,25},{25,17},{2,10},{10... | collective-permute-start | bytes 1474568 | tf_op jit(solution)/shard_map/ppermute | solution.py:392
  44.0 0.7 collective-permute-start.11
  44.7 5.1 %inner.4.part = f32[64,64,128]{2,1,0:T(8,128)S(1)} custom-call(f32[32,64,128]{2,1,0:T(8,128)S(1)} %get-tuple-element.115.own_inner, f32[32,64,128]{2,1,0:T(8,128)S(1)} %get-tuple-element.120.edge, bf16[1024,256]{1,0:T(8,128)(2,1)S(1)} %get-tuple-element.121.strips, bf16[4,256,256]{2,1,0:T(8,128)(2,1)S(1)} %get-tuple-element.122.wh, ...), custom_call_target="tpu_custom_call" | custom-call | bytes 15000000 | tf_op jit(solution)/shard_map/inner/pallas_call | solution.py:394
  49.8 1.7 %collective-permute-done.10.recv_a = f32[15,64,128]{2,1,0:T(8,128)S(1)} collective-permute-done((f32[15,64,128]{2,1,0:T(8,128)S(1)}, f32[15,64,128]{2,1,0:T(8,128)S(1)}, u32[]{:S(2)}, u32[]{:S(2)}) %collective-permute-start.10) | collective-permute-done | bytes 491552 | tf_op jit(solution)/shard_map/ppermute | solution.py:392
  51.5 2.2 %quotient.2 = (f32[64,64,128]{2,1,0:T(8,128)S(1)}, f32[8,64,128]{2,1,0:T(8,128)S(1)}, f32[8,64,128]{2,1,0:T(8,128)S(1)}) custom-call(s32[4]{0:T(128)S(1)} %pad_add_fusion.me, f32[64,64,128]{2,1,0:T(8,128)S(1)} %inner.4.part, f32[15,64,128]{2,1,0:T(8,128)S(1)} %collective-permute-done.10.recv_a, f32[15,64,128]{2,1,0:T(8,128)S(1)} %collective-permute-done.11.recv_b, ...), custom_call_target="tpu_custom_call" | custom-call | bytes 12000000 | tf_op jit(solution)/shard_map/quotient/pallas_call | solution.py:404
  53.7 4.9 %collective-permute-start.12 = (f32[8,64,128]{2,1,0:T(8,128)S(1)}, f32[8,64,128]{2,1,0:T(8,128)S(1)}, u32[]{:S(2)}, u32[]{:S(2)}) collective-permute-start(f32[8,64,128]{2,1,0:T(8,128)S(1)} %get-tuple-element.132), channel_id=1, source_target_pairs={{0,1},{1,0},{2,3},{3,2},{4,5},{5,4},{6,7},{7,6},{8,9},{9,8},{10,11... | collective-permute-start | bytes 786440 | tf_op jit(solution)/shard_map/ppermute | solution.py:384
  58.6 0.7 collective-permute-start.13
  59.3 1.5 own.5
  60.8 1.5 edge.5
  62.4 4.7 %collective-permute-start.14 = (f32[15,64,128]{2,1,0:T(8,128)S(1)}, f32[15,64,128]{2,1,0:T(8,128)S(1)}, u32[]{:S(2)}, u32[]{:S(2)}) collective-permute-start(f32[15,64,128]{2,1,0:T(8,128)S(1)} %get-tuple-element.139), channel_id=1, source_target_pairs={{0,8},{8,0},{16,24},{24,16},{1,9},{9,1},{17,25},{25,17},{2,10},{10... | collective-permute-start | bytes 1474568 | tf_op jit(solution)/shard_map/ppermute | solution.py:392
  67.0 0.7 collective-permute-start.15
  67.7 5.2 %inner.5.part = f32[64,64,128]{2,1,0:T(8,128)S(1)} custom-call(f32[32,64,128]{2,1,0:T(8,128)S(1)} %get-tuple-element.130.own_inner, f32[32,64,128]{2,1,0:T(8,128)S(1)} %get-tuple-element.135.edge, bf16[1024,256]{1,0:T(8,128)(2,1)S(1)} %get-tuple-element.136.strips, bf16[4,256,256]{2,1,0:T(8,128)(2,1)S(1)} %get-tuple-element.137.wh, ...), custom_call_target="tpu_custom_call" | custom-call | bytes 15000000 | tf_op jit(solution)/shard_map/inner/pallas_call | solution.py:394
  73.0 1.0 collective-permute-done.14.recv_a
  74.0 2.1 %estimate.1 = (f32[64,64,128]{2,1,0:T(8,128)S(1)}, f32[8,64,128]{2,1,0:T(8,128)S(1)}, f32[8,64,128]{2,1,0:T(8,128)S(1)}) custom-call(s32[4]{0:T(128)S(1)} %pad_add_fusion.me, f32[64,64,128]{2,1,0:T(8,128)S(1)} %inner.5.part, f32[15,64,128]{2,1,0:T(8,128)S(1)} %collective-permute-done.14.recv_a, f32[15,64,128]{2,1,0:T(8,128)S(1)} %collective-permute-done.15.recv_b, ...), custom_call_target="tpu_custom_call" | custom-call | bytes 12000000 | tf_op jit(solution)/shard_map/estimate/pallas_call | solution.py:409
  76.1 5.0 %collective-permute-start.16 = (f32[8,64,128]{2,1,0:T(8,128)S(1)}, f32[8,64,128]{2,1,0:T(8,128)S(1)}, u32[]{:S(2)}, u32[]{:S(2)}) collective-permute-start(f32[8,64,128]{2,1,0:T(8,128)S(1)} %get-tuple-element.144), channel_id=1, source_target_pairs={{0,1},{1,0},{2,3},{3,2},{4,5},{5,4},{6,7},{7,6},{8,9},{9,8},{10,11... | collective-permute-start | bytes 786440 | tf_op jit(solution)/shard_map/ppermute | solution.py:384
  81.1 0.8 collective-permute-start.17
  82.0 1.5 own.6
  83.5 1.5 edge.6
  85.1 4.0 %collective-permute-start.18 = (f32[15,64,128]{2,1,0:T(8,128)S(1)}, f32[15,64,128]{2,1,0:T(8,128)S(1)}, u32[]{:S(2)}, u32[]{:S(2)}) collective-permute-start(f32[15,64,128]{2,1,0:T(8,128)S(1)} %get-tuple-element.148), channel_id=1, source_target_pairs={{0,8},{8,0},{16,24},{24,16},{1,9},{9,1},{17,25},{25,17},{2,10},{10... | collective-permute-start | bytes 1474568 | tf_op jit(solution)/shard_map/ppermute | solution.py:392
  89.0 0.7 collective-permute-start.19
  89.7 5.1 %inner.6.part = f32[64,64,128]{2,1,0:T(8,128)S(1)} custom-call(f32[32,64,128]{2,1,0:T(8,128)S(1)} %get-tuple-element.142.own_inner, f32[32,64,128]{2,1,0:T(8,128)S(1)} %get-tuple-element.146.edge, bf16[1024,256]{1,0:T(8,128)(2,1)S(1)} %get-tuple-element.147.strips, bf16[4,256,256]{2,1,0:T(8,128)(2,1)S(1)} %get-tuple-element.122.wh, ...), custom_call_target="tpu_custom_call" | custom-call | bytes 15000000 | tf_op jit(solution)/shard_map/inner/pallas_call | solution.py:394
  94.8 1.0 collective-permute-done.18.recv_a
  95.9 2.2 %quotient.3 = (f32[64,64,128]{2,1,0:T(8,128)S(1)}, f32[8,64,128]{2,1,0:T(8,128)S(1)}, f32[8,64,128]{2,1,0:T(8,128)S(1)}) custom-call(s32[4]{0:T(128)S(1)} %pad_add_fusion.me, f32[64,64,128]{2,1,0:T(8,128)S(1)} %inner.6.part, f32[15,64,128]{2,1,0:T(8,128)S(1)} %collective-permute-done.18.recv_a, f32[15,64,128]{2,1,0:T(8,128)S(1)} %collective-permute-done.19.recv_b, ...), custom_call_target="tpu_custom_call" | custom-call | bytes 12000000 | tf_op jit(solution)/shard_map/quotient/pallas_call | solution.py:404
  98.0 5.2 %collective-permute-start.20 = (f32[8,64,128]{2,1,0:T(8,128)S(1)}, f32[8,64,128]{2,1,0:T(8,128)S(1)}, u32[]{:S(2)}, u32[]{:S(2)}) collective-permute-start(f32[8,64,128]{2,1,0:T(8,128)S(1)} %get-tuple-element.153), channel_id=1, source_target_pairs={{0,1},{1,0},{2,3},{3,2},{4,5},{5,4},{6,7},{7,6},{8,9},{9,8},{10,11... | collective-permute-start | bytes 786440 | tf_op jit(solution)/shard_map/ppermute | solution.py:384
  103.2 0.7 collective-permute-start.21
  103.9 1.5 own.7
  105.4 1.5 edge.7
  106.9 4.0 %collective-permute-start.22 = (f32[15,64,128]{2,1,0:T(8,128)S(1)}, f32[15,64,128]{2,1,0:T(8,128)S(1)}, u32[]{:S(2)}, u32[]{:S(2)}) collective-permute-start(f32[15,64,128]{2,1,0:T(8,128)S(1)} %get-tuple-element.157), channel_id=1, source_target_pairs={{0,8},{8,0},{16,24},{24,16},{1,9},{9,1},{17,25},{25,17},{2,10},{10... | collective-permute-start | bytes 1474568 | tf_op jit(solution)/shard_map/ppermute | solution.py:392
  110.9 0.7 collective-permute-start.23
  111.6 5.2 %inner.7.part = f32[64,64,128]{2,1,0:T(8,128)S(1)} custom-call(f32[32,64,128]{2,1,0:T(8,128)S(1)} %get-tuple-element.151.own_inner, f32[32,64,128]{2,1,0:T(8,128)S(1)} %get-tuple-element.155.edge, bf16[1024,256]{1,0:T(8,128)(2,1)S(1)} %get-tuple-element.156.strips, bf16[4,256,256]{2,1,0:T(8,128)(2,1)S(1)} %get-tuple-element.137.wh, ...), custom_call_target="tpu_custom_call" | custom-call | bytes 15000000 | tf_op jit(solution)/shard_map/inner/pallas_call | solution.py:394
  116.9 0.9 collective-permute-done.22.recv_a
  117.7 2.0 %last.1 = (f32[32,16,128]{2,1,0:T(8,128)S(1)}, f32[32,16,128]{2,1,0:T(8,128)S(1)}, f32[32,16,128]{2,1,0:T(8,128)S(1)}, f32[32,16,128]{2,1,0:T(8,128)S(1)}, f32[3...) custom-call(s32[4]{0:T(128)S(1)} %pad_add_fusion.me, ...), custom_call_target="tpu_custom_call" | custom-call | bytes 6000000 | tf_op jit(solution)/shard_map/last/pallas_call | solution.py:412
  119.7 5.5 %collective-permute-start.24 = (f32[32,16,128]{2,1,0:T(8,128)S(1)}, f32[32,16,128]{2,1,0:T(8,128)S(1)}, u32[]{:S(2)}, u32[]{:S(2)}) collective-permute-start(f32[32,16,128]{2,1,0:T(8,128)S(1)} %get-tuple-element.160), channel_id=1, source_target_pairs={{0,1},{1,0},{2,3},{3,2},{4,5},{5,4},{6,7},{7,6},{8,9},{9,8},{10,11... | collective-permute-start | bytes 786440 | tf_op jit(solution)/shard_map/ppermute | solution.py:331
  125.2 1.5 collective-permute-start.25
  126.7 2.6 %collective-permute-start.27 = (f32[32,16,128]{2,1,0:T(8,128)S(1)}, f32[32,16,128]{2,1,0:T(8,128)S(1)}, u32[]{:S(2)}, u32[]{:S(2)}) collective-permute-start(f32[32,16,128]{2,1,0:T(8,128)S(1)} %get-tuple-element.163), channel_id=1, source_target_pairs={{0,4},{1,5},{2,6},{3,7},{4,0},{5,1},{6,2},{7,3},{8,12},{9,13},{10,... | collective-permute-start | bytes 786440 | tf_op jit(solution)/shard_map/ppermute | solution.py:331
  129.3 2.6 %collective-permute-start.29 = (f32[32,16,128]{2,1,0:T(8,128)S(1)}, f32[32,16,128]{2,1,0:T(8,128)S(1)}, u32[]{:S(2)}, u32[]{:S(2)}) collective-permute-start(f32[32,16,128]{2,1,0:T(8,128)S(1)} %get-tuple-element.165), channel_id=1, source_target_pairs={{0,6},{1,7},{2,4},{3,5},{4,2},{5,3},{6,0},{7,1},{8,14},{9,15},{10,... | collective-permute-start | bytes 786440 | tf_op jit(solution)/shard_map/ppermute | solution.py:331
  131.9 2.5 %collective-permute-done.25.rest_2_ = f32[32,16,128]{2,1,0:T(8,128)S(1)} collective-permute-done((f32[32,16,128]{2,1,0:T(8,128)S(1)}, f32[32,16,128]{2,1,0:T(8,128)S(1)}, u32[]{:S(2)}, u32[]{:S(2)}) %collective-permute-start.25) | collective-permute-done | bytes 262176 | tf_op jit(solution)/shard_map/ppermute | solution.py:331
  134.4 2.0 %collective-permute-start.30 = (f32[32,16,128]{2,1,0:T(8,128)S(1)}, f32[32,16,128]{2,1,0:T(8,128)S(1)}, u32[]{:S(2)}, u32[]{:S(2)}) collective-permute-start(f32[32,16,128]{2,1,0:T(8,128)S(1)} %get-tuple-element.166), channel_id=1, source_target_pairs={{0,7},{1,6},{2,5},{3,4},{4,3},{5,2},{6,1},{7,0},{8,15},{9,14},{10,... | collective-permute-start | bytes 786440 | tf_op jit(solution)/shard_map/ppermute | solution.py:331
  136.4 2.7 %collective-permute-done.26.rest_3_ = f32[32,16,128]{2,1,0:T(8,128)S(1)} collective-permute-done((f32[32,16,128]{2,1,0:T(8,128)S(1)}, f32[32,16,128]{2,1,0:T(8,128)S(1)}, u32[]{:S(2)}, u32[]{:S(2)}) %collective-permute-start.26) | collective-permute-done | bytes 262176 | tf_op jit(solution)/shard_map/ppermute | solution.py:331
  139.0 13.6 %collective-permute-done.28.rest_5_ = f32[32,16,128]{2,1,0:T(8,128)S(1)} collective-permute-done((f32[32,16,128]{2,1,0:T(8,128)S(1)}, f32[32,16,128]{2,1,0:T(8,128)S(1)}, u32[]{:S(2)}, u32[]{:S(2)}) %collective-permute-start.28) | collective-permute-done | bytes 262176 | tf_op jit(solution)/shard_map/ppermute | solution.py:331
  152.6 2.1 %gather.1 = f32[2,32,16,512]{3,2,1,0:T(8,128)} custom-call(s32[4]{0:T(128)S(1)} %pad_add_fusion.me, f32[32,16,128]{2,1,0:T(8,128)S(1)} %get-tuple-element.159.rest_0_, f32[32,16,128]{2,1,0:T(8,128)S(1)} %collective-permute-done.24.rest_1_, f32[32,16,128]{2,1,0:T(8,128)S(1)} %collective-permute-done.25.rest_2_, ...), custom_call_target="tpu_custom_call" | custom-call | bytes 9000000 | tf_op jit(solution)/shard_map/gather/pallas_call | solution.py:416
  (53 shorter events, 1.4 us)
Async XLA Ops:
  0.0 10.9 %copy-start.7 = (s32[1,4,32]{2,1,0:T(4,128)S(1)}, s32[1,4,32]{2,1,0:T(4,128)}, u32[]{:S(2)}) copy-start(s32[1,4,32]{2,1,0:T(4,128)} %param.9) | copy-start | bytes 1540
  0.0 10.7 %copy-start.6 = (f32[2,101]{1,0:T(2,128)S(1)}, f32[2,101]{1,0:T(2,128)}, u32[]{:S(2)}) copy-start(f32[2,101]{1,0:T(2,128)} %param.8) | copy-start | bytes 2428
  0.0 11.0 %copy-start.5 = (f32[2,31]{1,0:T(2,128)S(1)}, f32[2,31]{1,0:T(2,128)}, u32[]{:S(2)}) copy-start(f32[2,31]{1,0:T(2,128)} %param.6) | copy-start | bytes 748
  0.0 11.1 %copy-start.4 = (f32[2,31]{1,0:T(2,128)S(1)}, f32[2,31]{1,0:T(2,128)}, u32[]{:S(2)}) copy-start(f32[2,31]{1,0:T(2,128)} %param.7) | copy-start | bytes 748
  0.0 15.2 %collective-permute-start.7 = (s32[4,32]{1,0:T(4,128)}, s32[4,32]{1,0:T(4,128)S(1)}, u32[]{:S(2)}, u32[]{:S(2)}) collective-permute-start(s32[4,32]{1,0:T(4,128)} %bitcast.17), channel_id=1, source_target_pairs={{0,4},{4,0},{1,5},{5,1},{2,6},{6,2},{3,7},{7,3},{8,12},{12,8},{9,1... | collective-permute-start | bytes 1544 | tf_op jit(solution)/shard_map/ppermute | solution.py:353
  3.1 1.6 %copy-start = (f32[2,32,16,512]{3,2,1,0:T(8,128)S(1)}, f32[2,32,16,512]{3,2,1,0:T(8,128)}, u32[]{:S(2)}) copy-start(f32[2,32,16,512]{3,2,1,0:T(8,128)} %observed.1) | copy-start | bytes 6291460
  6.4 0.7 copy-start.1
  7.1 0.7 copy-start.2
  7.8 0.7 copy-start.3
  8.5 8.1 %collective-permute-start = (f32[32,16,128]{2,1,0:T(8,128)}, f32[32,16,128]{2,1,0:T(8,128)S(1)}, u32[]{:S(2)}, u32[]{:S(2)}) collective-permute-start(f32[32,16,128]{2,1,0:T(8,128)} %get-tuple-element.87), channel_id=1, source_target_pairs={{0,1},{1,0},{2,3},{3,2},{4,5},{5,4},{6,7},{7,6},{8,9},{9,8},{10,11... | collective-permute-start | bytes 786440 | tf_op jit(solution)/shard_map/ppermute | solution.py:331
  8.5 9.5 %collective-permute-start.1 = (f32[32,16,128]{2,1,0:T(8,128)}, f32[32,16,128]{2,1,0:T(8,128)}, u32[]{:S(2)}, u32[]{:S(2)}) collective-permute-start(f32[32,16,128]{2,1,0:T(8,128)} %get-tuple-element.88), channel_id=1, source_target_pairs={{0,2},{1,3},{2,0},{3,1},{4,6},{5,7},{6,4},{7,5},{8,10},{9,11},{10,... | collective-permute-start | bytes 786440 | tf_op jit(solution)/shard_map/ppermute | solution.py:331
  10.0 12.8 %collective-permute-start.2 = (f32[32,16,128]{2,1,0:T(8,128)}, f32[32,16,128]{2,1,0:T(8,128)}, u32[]{:S(2)}, u32[]{:S(2)}) collective-permute-start(f32[32,16,128]{2,1,0:T(8,128)} %get-tuple-element.89), channel_id=1, source_target_pairs={{0,3},{1,2},{2,1},{3,0},{4,7},{5,6},{6,5},{7,4},{8,11},{9,10},{10,... | collective-permute-start | bytes 786440 | tf_op jit(solution)/shard_map/ppermute | solution.py:331
  10.4 12.4 %collective-permute-start.3 = (f32[32,16,128]{2,1,0:T(8,128)}, f32[32,16,128]{2,1,0:T(8,128)}, u32[]{:S(2)}, u32[]{:S(2)}) collective-permute-start(f32[32,16,128]{2,1,0:T(8,128)} %get-tuple-element.90), channel_id=1, source_target_pairs={{0,4},{1,5},{2,6},{3,7},{4,0},{5,1},{6,2},{7,3},{8,12},{9,13},{10,... | collective-permute-start | bytes 786440 | tf_op jit(solution)/shard_map/ppermute | solution.py:331
  15.2 20.3 %collective-permute-start.4 = (f32[32,16,128]{2,1,0:T(8,128)}, f32[32,16,128]{2,1,0:T(8,128)}, u32[]{:S(2)}, u32[]{:S(2)}) collective-permute-start(f32[32,16,128]{2,1,0:T(8,128)} %copy-done.3), channel_id=1, source_target_pairs={{0,5},{1,4},{2,7},{3,6},{4,1},{5,0},{6,3},{7,2},{8,13},{9,12},{10,... | collective-permute-start | bytes 786440 | tf_op jit(solution)/shard_map/ppermute | solution.py:331
  16.6 18.9 %collective-permute-start.5 = (f32[32,16,128]{2,1,0:T(8,128)}, f32[32,16,128]{2,1,0:T(8,128)}, u32[]{:S(2)}, u32[]{:S(2)}) collective-permute-start(f32[32,16,128]{2,1,0:T(8,128)} %copy-done.2), channel_id=1, source_target_pairs={{0,6},{1,7},{2,4},{3,5},{4,2},{5,3},{6,0},{7,1},{8,14},{9,15},{10,... | collective-permute-start | bytes 786440 | tf_op jit(solution)/shard_map/ppermute | solution.py:331
  18.1 17.4 %collective-permute-start.6 = (f32[32,16,128]{2,1,0:T(8,128)}, f32[32,16,128]{2,1,0:T(8,128)}, u32[]{:S(2)}, u32[]{:S(2)}) collective-permute-start(f32[32,16,128]{2,1,0:T(8,128)} %copy-done.1), channel_id=1, source_target_pairs={{0,7},{1,6},{2,5},{3,4},{4,3},{5,2},{6,1},{7,0},{8,15},{9,14},{10,... | collective-permute-start | bytes 786440 | tf_op jit(solution)/shard_map/ppermute | solution.py:331
  38.2 2.7 %collective-permute-start.8 = (f32[8,64,128]{2,1,0:T(8,128)S(1)}, f32[8,64,128]{2,1,0:T(8,128)S(1)}, u32[]{:S(2)}, u32[]{:S(2)}) collective-permute-start(f32[8,64,128]{2,1,0:T(8,128)S(1)} %get-tuple-element.117), channel_id=1, source_target_pairs={{0,1},{1,0},{2,3},{3,2},{4,5},{5,4},{6,7},{7,6},{8,9},{9,8},{10,11... | collective-permute-start | bytes 786440 | tf_op jit(solution)/shard_map/ppermute | solution.py:384
  38.6 2.2 %collective-permute-start.9 = (f32[8,64,128]{2,1,0:T(8,128)S(1)}, f32[8,64,128]{2,1,0:T(8,128)S(1)}, u32[]{:S(2)}, u32[]{:S(2)}) collective-permute-start(f32[8,64,128]{2,1,0:T(8,128)S(1)} %get-tuple-element.118), channel_id=1, source_target_pairs={{1,4},{4,1},{3,6},{6,3},{9,12},{12,9},{11,14},{14,11},{17,20},{20,... | collective-permute-start | bytes 786440 | tf_op jit(solution)/shard_map/ppermute | solution.py:383
  42.4 9.1 %collective-permute-start.10 = (f32[15,64,128]{2,1,0:T(8,128)S(1)}, f32[15,64,128]{2,1,0:T(8,128)S(1)}, u32[]{:S(2)}, u32[]{:S(2)}) collective-permute-start(f32[15,64,128]{2,1,0:T(8,128)S(1)} %get-tuple-element.124), channel_id=1, source_target_pairs={{0,8},{8,0},{16,24},{24,16},{1,9},{9,1},{17,25},{25,17},{2,10},{10... | collective-permute-start | bytes 1474568 | tf_op jit(solution)/shard_map/ppermute | solution.py:392
  44.0 7.5 %collective-permute-start.11 = (f32[15,64,128]{2,1,0:T(8,128)S(1)}, f32[15,64,128]{2,1,0:T(8,128)S(1)}, u32[]{:S(2)}, u32[]{:S(2)}) collective-permute-start(f32[15,64,128]{2,1,0:T(8,128)S(1)} %get-tuple-element.125), channel_id=1, source_target_pairs={{8,16},{16,8},{9,17},{17,9},{10,18},{18,10},{11,19},{19,11},{12,20... | collective-permute-start | bytes 1474568 | tf_op jit(solution)/shard_map/ppermute | solution.py:393
  53.7 7.1 %collective-permute-start.12 = (f32[8,64,128]{2,1,0:T(8,128)S(1)}, f32[8,64,128]{2,1,0:T(8,128)S(1)}, u32[]{:S(2)}, u32[]{:S(2)}) collective-permute-start(f32[8,64,128]{2,1,0:T(8,128)S(1)} %get-tuple-element.132), channel_id=1, source_target_pairs={{0,1},{1,0},{2,3},{3,2},{4,5},{5,4},{6,7},{7,6},{8,9},{9,8},{10,11... | collective-permute-start | bytes 786440 | tf_op jit(solution)/shard_map/ppermute | solution.py:384
  58.6 2.2 %collective-permute-start.13 = (f32[8,64,128]{2,1,0:T(8,128)S(1)}, f32[8,64,128]{2,1,0:T(8,128)S(1)}, u32[]{:S(2)}, u32[]{:S(2)}) collective-permute-start(f32[8,64,128]{2,1,0:T(8,128)S(1)} %get-tuple-element.133), channel_id=1, source_target_pairs={{1,4},{4,1},{3,6},{6,3},{9,12},{12,9},{11,14},{14,11},{17,20},{20,... | collective-permute-start | bytes 786440 | tf_op jit(solution)/shard_map/ppermute | solution.py:383
  62.4 11.6 %collective-permute-start.14 = (f32[15,64,128]{2,1,0:T(8,128)S(1)}, f32[15,64,128]{2,1,0:T(8,128)S(1)}, u32[]{:S(2)}, u32[]{:S(2)}) collective-permute-start(f32[15,64,128]{2,1,0:T(8,128)S(1)} %get-tuple-element.139), channel_id=1, source_target_pairs={{0,8},{8,0},{16,24},{24,16},{1,9},{9,1},{17,25},{25,17},{2,10},{10... | collective-permute-start | bytes 1474568 | tf_op jit(solution)/shard_map/ppermute | solution.py:392
  67.0 6.9 %collective-permute-start.15 = (f32[15,64,128]{2,1,0:T(8,128)S(1)}, f32[15,64,128]{2,1,0:T(8,128)S(1)}, u32[]{:S(2)}, u32[]{:S(2)}) collective-permute-start(f32[15,64,128]{2,1,0:T(8,128)S(1)} %get-tuple-element.140), channel_id=1, source_target_pairs={{8,16},{16,8},{9,17},{17,9},{10,18},{18,10},{11,19},{19,11},{12,20... | collective-permute-start | bytes 1474568 | tf_op jit(solution)/shard_map/ppermute | solution.py:393
  76.1 7.4 %collective-permute-start.16 = (f32[8,64,128]{2,1,0:T(8,128)S(1)}, f32[8,64,128]{2,1,0:T(8,128)S(1)}, u32[]{:S(2)}, u32[]{:S(2)}) collective-permute-start(f32[8,64,128]{2,1,0:T(8,128)S(1)} %get-tuple-element.144), channel_id=1, source_target_pairs={{0,1},{1,0},{2,3},{3,2},{4,5},{5,4},{6,7},{7,6},{8,9},{9,8},{10,11... | collective-permute-start | bytes 786440 | tf_op jit(solution)/shard_map/ppermute | solution.py:384
  81.1 2.4 %collective-permute-start.17 = (f32[8,64,128]{2,1,0:T(8,128)S(1)}, f32[8,64,128]{2,1,0:T(8,128)S(1)}, u32[]{:S(2)}, u32[]{:S(2)}) collective-permute-start(f32[8,64,128]{2,1,0:T(8,128)S(1)} %get-tuple-element.145), channel_id=1, source_target_pairs={{1,4},{4,1},{3,6},{6,3},{9,12},{12,9},{11,14},{14,11},{17,20},{20,... | collective-permute-start | bytes 786440 | tf_op jit(solution)/shard_map/ppermute | solution.py:383
  85.1 10.8 %collective-permute-start.18 = (f32[15,64,128]{2,1,0:T(8,128)S(1)}, f32[15,64,128]{2,1,0:T(8,128)S(1)}, u32[]{:S(2)}, u32[]{:S(2)}) collective-permute-start(f32[15,64,128]{2,1,0:T(8,128)S(1)} %get-tuple-element.148), channel_id=1, source_target_pairs={{0,8},{8,0},{16,24},{24,16},{1,9},{9,1},{17,25},{25,17},{2,10},{10... | collective-permute-start | bytes 1474568 | tf_op jit(solution)/shard_map/ppermute | solution.py:392
  89.0 6.8 %collective-permute-start.19 = (f32[15,64,128]{2,1,0:T(8,128)S(1)}, f32[15,64,128]{2,1,0:T(8,128)S(1)}, u32[]{:S(2)}, u32[]{:S(2)}) collective-permute-start(f32[15,64,128]{2,1,0:T(8,128)S(1)} %get-tuple-element.149), channel_id=1, source_target_pairs={{8,16},{16,8},{9,17},{17,9},{10,18},{18,10},{11,19},{19,11},{12,20... | collective-permute-start | bytes 1474568 | tf_op jit(solution)/shard_map/ppermute | solution.py:393
  98.0 7.4 %collective-permute-start.20 = (f32[8,64,128]{2,1,0:T(8,128)S(1)}, f32[8,64,128]{2,1,0:T(8,128)S(1)}, u32[]{:S(2)}, u32[]{:S(2)}) collective-permute-start(f32[8,64,128]{2,1,0:T(8,128)S(1)} %get-tuple-element.153), channel_id=1, source_target_pairs={{0,1},{1,0},{2,3},{3,2},{4,5},{5,4},{6,7},{7,6},{8,9},{9,8},{10,11... | collective-permute-start | bytes 786440 | tf_op jit(solution)/shard_map/ppermute | solution.py:384
  103.2 2.2 %collective-permute-start.21 = (f32[8,64,128]{2,1,0:T(8,128)S(1)}, f32[8,64,128]{2,1,0:T(8,128)S(1)}, u32[]{:S(2)}, u32[]{:S(2)}) collective-permute-start(f32[8,64,128]{2,1,0:T(8,128)S(1)} %get-tuple-element.154), channel_id=1, source_target_pairs={{1,4},{4,1},{3,6},{6,3},{9,12},{12,9},{11,14},{14,11},{17,20},{20,... | collective-permute-start | bytes 786440 | tf_op jit(solution)/shard_map/ppermute | solution.py:383
  106.9 10.8 %collective-permute-start.22 = (f32[15,64,128]{2,1,0:T(8,128)S(1)}, f32[15,64,128]{2,1,0:T(8,128)S(1)}, u32[]{:S(2)}, u32[]{:S(2)}) collective-permute-start(f32[15,64,128]{2,1,0:T(8,128)S(1)} %get-tuple-element.157), channel_id=1, source_target_pairs={{0,8},{8,0},{16,24},{24,16},{1,9},{9,1},{17,25},{25,17},{2,10},{10... | collective-permute-start | bytes 1474568 | tf_op jit(solution)/shard_map/ppermute | solution.py:392
  110.9 6.8 %collective-permute-start.23 = (f32[15,64,128]{2,1,0:T(8,128)S(1)}, f32[15,64,128]{2,1,0:T(8,128)S(1)}, u32[]{:S(2)}, u32[]{:S(2)}) collective-permute-start(f32[15,64,128]{2,1,0:T(8,128)S(1)} %get-tuple-element.158), channel_id=1, source_target_pairs={{8,16},{16,8},{9,17},{17,9},{10,18},{18,10},{11,19},{19,11},{12,20... | collective-permute-start | bytes 1474568 | tf_op jit(solution)/shard_map/ppermute | solution.py:393
  119.7 9.6 %collective-permute-start.24 = (f32[32,16,128]{2,1,0:T(8,128)S(1)}, f32[32,16,128]{2,1,0:T(8,128)S(1)}, u32[]{:S(2)}, u32[]{:S(2)}) collective-permute-start(f32[32,16,128]{2,1,0:T(8,128)S(1)} %get-tuple-element.160), channel_id=1, source_target_pairs={{0,1},{1,0},{2,3},{3,2},{4,5},{5,4},{6,7},{7,6},{8,9},{9,8},{10,11... | collective-permute-start | bytes 786440 | tf_op jit(solution)/shard_map/ppermute | solution.py:331
  125.2 9.2 %collective-permute-start.25 = (f32[32,16,128]{2,1,0:T(8,128)S(1)}, f32[32,16,128]{2,1,0:T(8,128)S(1)}, u32[]{:S(2)}, u32[]{:S(2)}) collective-permute-start(f32[32,16,128]{2,1,0:T(8,128)S(1)} %get-tuple-element.161), channel_id=1, source_target_pairs={{0,2},{1,3},{2,0},{3,1},{4,6},{5,7},{6,4},{7,5},{8,10},{9,11},{10,... | collective-permute-start | bytes 786440 | tf_op jit(solution)/shard_map/ppermute | solution.py:331
  126.7 12.3 %collective-permute-start.26 = (f32[32,16,128]{2,1,0:T(8,128)S(1)}, f32[32,16,128]{2,1,0:T(8,128)S(1)}, u32[]{:S(2)}, u32[]{:S(2)}) collective-permute-start(f32[32,16,128]{2,1,0:T(8,128)S(1)} %get-tuple-element.162), channel_id=1, source_target_pairs={{0,3},{1,2},{2,1},{3,0},{4,7},{5,6},{6,5},{7,4},{8,11},{9,10},{10,... | collective-permute-start | bytes 786440 | tf_op jit(solution)/shard_map/ppermute | solution.py:331
  126.7 12.3 %collective-permute-start.27 = (f32[32,16,128]{2,1,0:T(8,128)S(1)}, f32[32,16,128]{2,1,0:T(8,128)S(1)}, u32[]{:S(2)}, u32[]{:S(2)}) collective-permute-start(f32[32,16,128]{2,1,0:T(8,128)S(1)} %get-tuple-element.163), channel_id=1, source_target_pairs={{0,4},{1,5},{2,6},{3,7},{4,0},{5,1},{6,2},{7,3},{8,12},{9,13},{10,... | collective-permute-start | bytes 786440 | tf_op jit(solution)/shard_map/ppermute | solution.py:331
  129.3 23.3 %collective-permute-start.28 = (f32[32,16,128]{2,1,0:T(8,128)S(1)}, f32[32,16,128]{2,1,0:T(8,128)S(1)}, u32[]{:S(2)}, u32[]{:S(2)}) collective-permute-start(f32[32,16,128]{2,1,0:T(8,128)S(1)} %get-tuple-element.164), channel_id=1, source_target_pairs={{0,5},{1,4},{2,7},{3,6},{4,1},{5,0},{6,3},{7,2},{8,13},{9,12},{10,... | collective-permute-start | bytes 786440 | tf_op jit(solution)/shard_map/ppermute | solution.py:331
  129.3 23.3 %collective-permute-start.29 = (f32[32,16,128]{2,1,0:T(8,128)S(1)}, f32[32,16,128]{2,1,0:T(8,128)S(1)}, u32[]{:S(2)}, u32[]{:S(2)}) collective-permute-start(f32[32,16,128]{2,1,0:T(8,128)S(1)} %get-tuple-element.165), channel_id=1, source_target_pairs={{0,6},{1,7},{2,4},{3,5},{4,2},{5,3},{6,0},{7,1},{8,14},{9,15},{10,... | collective-permute-start | bytes 786440 | tf_op jit(solution)/shard_map/ppermute | solution.py:331
  134.4 18.2 %collective-permute-start.30 = (f32[32,16,128]{2,1,0:T(8,128)S(1)}, f32[32,16,128]{2,1,0:T(8,128)S(1)}, u32[]{:S(2)}, u32[]{:S(2)}) collective-permute-start(f32[32,16,128]{2,1,0:T(8,128)S(1)} %get-tuple-element.166), channel_id=1, source_target_pairs={{0,7},{1,6},{2,5},{3,4},{4,3},{5,2},{6,1},{7,0},{8,15},{9,14},{10,... | collective-permute-start | bytes 786440 | tf_op jit(solution)/shard_map/ppermute | solution.py:331

commit v3 on v2

v3 whole, which is shorter than its diff:
```python
import functools

import jax
import jax.numpy as jnp
from jax import lax
from jax.experimental import pallas as pl
from jax.experimental.pallas import tpu as pltpu
from jax.sharding import Mesh, PartitionSpec as P

ITERS = 2
BY = 8
BZ = 8
LANES = 128
STRIP = 16
F32, BF16 = jnp.float32, jnp.bfloat16
VMEM = pl.BlockSpec(memory_space=pltpu.VMEM)
SMEM = pl.BlockSpec(memory_space=pltpu.SMEM)
MIB = 1024 * 1024


def shape(dims, dtype=F32):
    return jax.ShapeDtypeStruct(dims, dtype)


def halves(cells):
    high = cells.astype(BF16)
    return high, (cells - high.astype(F32)).astype(BF16)


def dot(a, b):
    return jnp.dot(a, b, preferred_element_type=F32)


def chip(me, e):
    return tuple(jnp.where((e >> s) & 1, 1 - b, b) for b, s in ((me[0], 1), (me[1], 0)))


def slots(start, size):
    return pl.ds(pl.multiple_of(start * size, size), size)


def deal_kernel(me, observed, kept, sent):
    channels, rows, depth, columns = observed.shape
    lane_group = lax.broadcasted_iota(jnp.int32, (8, LANES), 1) // STRIP
    upper = jnp.full((8, LANES), me[0], jnp.int32) == 1
    for c in range(channels):
        for q in range(columns // LANES):
            cells = observed[c, :, :, q * LANES : (q + 1) * LANES]
            strips = {}
            for part in range(2):
                for y in range(4):
                    for t in range(depth // 8):
                        z = slice(8 * t, 8 * t + 8)
                        total = jnp.zeros((8, LANES), F32)
                        for g in range(4):
                            row = 16 * part + 4 * g + y
                            if (q + 1) * LANES < columns:
                                cell = observed[c, row, z, (q + 1) * LANES : (q + 2) * LANES]
                                total = jnp.where(lane_group == g, pltpu.roll(cell, STRIP * g, 1) if g else cell, total)
                            if q:
                                cell = observed[c, row, z, (q - 1) * LANES : q * LANES]
                                cell = pltpu.roll(cell, STRIP * (g + 5), 1)
                                total = jnp.where(lane_group == g + 4, cell, total)
                        strips[part, y, t] = jnp.where(upper, pltpu.roll(total, LANES // 2, 1), total)

            def put(out):
                out[c, q // 2, :rows] = cells
                for (part, y, t), value in strips.items():
                    out[c, q // 2, rows + 4 * part + y, 8 * t : 8 * t + 8, :] = value

            own = me[2] == (q % 2) ^ (q // 2)

            @pl.when(own)
            def _():
                put(kept)

            @pl.when(jnp.logical_not(own))
            def _():
                put(sent)


def mix_kernel(me, kept, swapped, *outs):
    rows, depth = outs[0].shape[0] - 4, kept.shape[3]
    for part in range(2):
        half = me[0] if part == 0 else 1 - me[0]
        for e in range(4):
            yl, zh = chip(me, e)
            out = outs[4 * part + e]
            for z, cells in ((me[2], kept), (1 - me[2], swapped)):
                out[:rows, slots(z, depth), :] = cells[zh, yl, slots(half, rows)]
                out[rows:, slots(z, depth), :] = cells[zh, yl, pl.ds(2 * rows + 4 * half, 4)]


def join_kernel(me, *rest):
    pieces, cells, pair, after, strips = rest[:4], rest[4], rest[5], rest[6], rest[7]
    rows, depth = pieces[0].shape[0] - 4, pieces[0].shape[1]
    for e in range(4):
        yl, zh = chip(me, e)
        z = slots(zh, depth)
        cells[slots(yl, rows), z, :] = pieces[e][:rows]
        strips[yl, :, z, :] = pieces[e][rows:]
    low = lax.broadcasted_iota(jnp.int32, (8, LANES), 1) < LANES // 2
    right_first = jnp.full((8, LANES), me[4], jnp.int32) == 0

    def tile(z):
        for y in range(4):
            first, second = strips[0, y, z, :], strips[1, y, z, :]
            right = jnp.where(low, first, second)
            left = pltpu.roll(jnp.where(low, second, first), 3 * STRIP, 1)
            pair[y, z, :] = jnp.where(right_first, right, left)
            after[y, z, :] = jnp.where(right_first, left, right)

    tiles(cells.shape[1], tile)


def split_depth_kernel(me, *rest):
    pieces, out = rest[:4], rest[4]
    for e in range(4):
        out[e] = pieces[e][:, slots(1 - me[2], out.shape[2]), :]


def gather_kernel(me, *rest):
    out = rest[10]
    for part in range(2):
        pieces, swapped = rest[5 * part : 5 * part + 4], rest[5 * part + 4]
        rows, depth = swapped.shape[1:3]
        y = slots(me[0] if part == 0 else 1 - me[0], rows)
        for e in range(4):
            yl, zh = chip(me, e)
            side = me[2] ^ yl
            out[zh, y, :, slots(2 * yl + side, LANES)] = pieces[e][:, slots(me[2], depth), :]
            out[zh, y, :, slots(2 * yl + 1 - side, LANES)] = swapped[e]


def pack_tile(me, z, cells, to_pair, to_next):
    groups = LANES // STRIP
    deep = len(cells) // groups
    lane_group = lax.broadcasted_iota(jnp.int32, (8, LANES), 1) // STRIP
    left_first = jnp.full((8, LANES), me[4], jnp.int32) == 1
    for y in range(deep):
        left = right = None
        for j in range(groups):
            cell = cells[deep * j + y]
            cell = pltpu.roll(cell, STRIP * j, 1) if j else cell
            left = cell if left is None else jnp.where(lane_group == j, cell, left)
            right = cell if right is None else jnp.where(lane_group == j - 1, cell, right)
        to_pair[y, z, :] = jnp.where(left_first, left, right)
        to_next[y, z, :] = jnp.where(left_first, right, left)


def tiles(depth, body):
    def one(t, _):
        body(pl.ds(pl.multiple_of(8 * t, 8), 8))
        return 0

    lax.fori_loop(0, depth // 8, one, 0)


def weights_kernel(me, rows, columns, axial, listed, theirs, *outs):
    live = outs[-1]
    tall, deep = live.shape[0] // 2, live.shape[1] // listed.shape[0] // BZ
    wide = listed.shape[1] // tall // deep
    for lists, half in ((listed, me[0]), (theirs, 1 - me[0])):
        for g in range(lists.shape[0]):
            bits = jnp.int32(0)
            for i in range(lists.shape[1]):
                number = lists[g, i]
                bits = bits | jnp.where(number < 0, 0, jnp.left_shift(jnp.int32(1), jnp.maximum(number, 0)))
            for t in range(tall):
                for b in range(deep):
                    number = (t * deep + b) * wide + 2 * me[0] + me[4]
                    z = (g * deep + b) * BZ
                    hit = jnp.right_shift(bits, number) & 1
                    live[half * tall + t, z : z + BZ, :] = jnp.full((BZ, LANES), hit, jnp.int32).astype(F32)
    channel = me[1]
    nx, nz = LANES, outs[0].shape[0] // 4
    radius, reach = columns.shape[1] // 2, axial.shape[1] // 2

    totals = {}
    for taps in (rows, columns, axial):
        total = taps[channel, 0]
        for k in range(1, taps.shape[1]):
            total = total + taps[channel, k]
        totals[id(taps)] = total

    def toeplitz(taps, offsets):
        total = jnp.zeros(offsets.shape, F32)
        for k in range(taps.shape[1]):
            total = jnp.where(offsets == k, taps[channel, k], total)
        return total / totals[id(taps)]

    for flip in (False, True):
        wz, wx, wh, wy = outs[4 * flip : 4 * flip + 4]

        def offsets(source, target, half):
            return (target - source if flip else source - target) + half

        def iota(dims, axis):
            return lax.broadcasted_iota(jnp.int32, dims, axis)

        dims = (nz, 2 * nz)
        high, low = halves(toeplitz(axial, offsets(iota(dims, 1) % nz, iota(dims, 0), reach)))
        zero = jnp.zeros(dims, BF16)
        wz[...] = jnp.concatenate(
            [
                jnp.concatenate([high, zero], 1),
                jnp.concatenate([low, zero], 1),
                jnp.concatenate([zero, high], 1),
                jnp.concatenate([zero, low], 1),
            ],
            0,
        )
        dims = (nx, nx)
        high, low = halves(toeplitz(columns, offsets(iota(dims, 0), iota(dims, 1), radius)))
        both = jnp.concatenate([high, low], 1)
        wx[...] = jnp.concatenate([both, both], 0)
        dims = (STRIP, 2 * nx)
        lanes = iota(dims, 1)
        edge = lanes % (2 * STRIP)
        target = jnp.where(edge < STRIP, nx - STRIP + edge, edge - STRIP)
        groups = nx // STRIP
        for k, first in ((0, me[4] == 0), (1, me[4] == 1)):
            source = iota(dims, 0) + jnp.where(first, nx, -STRIP)
            high, low = halves(toeplitz(columns, offsets(source, target, radius)))
            for g in range(groups):
                here = lanes // (2 * STRIP) == jnp.where(first, g, (g + 1) % groups)
                at = k * nx + STRIP * g
                both = [jnp.where(here, part.astype(F32), 0.0).astype(BF16) for part in (high, low)]
                wh[at : at + STRIP, :] = jnp.concatenate(both, 1)
        for i in range(rows.shape[1]):
            k = rows.shape[1] - 1 - i if flip else i
            wy[i] = jnp.full((8, LANES), rows[channel, k], F32) / totals[id(rows)]


def blur_z(weights, slabs):
    depth = slabs[0].shape[0]
    parts = [jnp.concatenate(halves(slab), 0) for slab in slabs]
    stacked = jnp.concatenate(
        [jnp.concatenate(parts[:2], 0), jnp.concatenate(parts[2:], 0)], 1
    )
    out = dot(weights, stacked)
    return [
        out[2 * a * depth : (2 * a + 1) * depth, b * LANES : (b + 1) * LANES]
        + out[(2 * a + 1) * depth : (2 * a + 2) * depth, b * LANES : (b + 1) * LANES]
        for b in range(2)
        for a in range(2)
    ]


def own_columns(cells, wz, wx, out):
    rows, depth = cells.shape[:2]
    count = 16
    for first in range(0, rows, count):
        slabs = []
        for y in range(first, first + count, 4):
            slabs += blur_z(wz[...], [cells[y + i] for i in range(4)])
        both = dot(jnp.concatenate(halves(jnp.concatenate(slabs, 0)), 1), wx[...])
        out[first : first + count] = (both[:, :LANES] + both[:, LANES:]).reshape(count, depth, LANES)


def near_columns(own, pair, after, wz, wh, out):
    deep, depth = pair.shape[:2]
    a = blur_z(wz[...], [pair[i] for i in range(deep)])
    b = blur_z(wz[...], [after[i] for i in range(deep)])
    high_a, low_a = halves(jnp.concatenate(a, 0))
    high_b, low_b = halves(jnp.concatenate(b, 0))
    strips = jnp.concatenate(
        [jnp.concatenate([high_a, high_b], 1), jnp.concatenate([low_a, low_b], 1)], 0
    )
    both = dot(strips, wh[...])
    count, wide = deep * depth, both.shape[1] // 2
    both = both[:, :wide] + both[:, wide:]
    both = both[:count] + both[count:]
    lane = lax.broadcasted_iota(jnp.int32, (count, LANES), 1)
    near = (lane < STRIP) | (lane >= LANES - STRIP)
    per = LANES // (2 * STRIP)
    for j in range(LANES // STRIP):
        add = both[:, j // per * LANES : (j // per + 1) * LANES]
        add = pltpu.roll(add, (LANES - STRIP - 2 * STRIP * (j % per)) % LANES, 1)
        add = jnp.where(near, add, 0.0).reshape(deep, depth, LANES)
        out[deep * j : deep * (j + 1)] = own[deep * j : deep * (j + 1)] + add


def own_kernel(cells, wz, wx, out):
    own_columns(cells, wz, wx, out)


def outer_kernel(me, own, pair, after, wz, wh, out, send_a, send_b):
    near_columns(own, pair, after, wz, wh, out)
    rows, count = out.shape[0], send_a.shape[0]
    even = me[3] == 0

    @pl.when(even)
    def _():
        send_a[...] = out[rows - count :]
        send_b[...] = out[:count]

    @pl.when(jnp.logical_not(even))
    def _():
        send_a[...] = out[:count]
        send_b[...] = out[rows - count :]


def ratio(observed, blurred, live):
    return jnp.where(live != 0, observed / blurred, 1.0)


def product(estimate, correction, live):
    return jnp.where(live != 0, estimate * correction, estimate)


def inner_blur(me, cells, pair, after, outer, wz, wx, wh, wy, part, inner, body):
    own_columns(cells, wz, wx, inner)
    near_columns(inner, pair, after, wz, wh, inner)
    quarter, depth = outer.shape[0] // 2, outer.shape[1]
    rows = 4 * quarter
    radius = wy.shape[0] // 2

    def source(y):
        if y < quarter:
            return outer, y
        if y < 3 * quarter:
            return inner, y - quarter
        return outer, y - 2 * quarter

    def tile(z):
        taps = [wy[i] for i in range(wy.shape[0])]
        blurred = []
        for first in range(0, rows, quarter):
            sums = [None] * quarter
            for y in range(max(0, first - radius), min(rows, first + quarter + radius)):
                ref, at = source(y)
                cell = ref[at, z, :]
                for o in range(quarter):
                    i = y - (first + o) + radius
                    if 0 <= i < len(taps):
                        term = taps[i] * cell
                        sums[o] = term if sums[o] is None else sums[o] + term
            for o in range(quarter):
                ref, at = source(first + o)
                if ref is outer:
                    part[at, z, :] = sums[o]
                else:
                    blurred.append(sums[o])
        body(z, blurred)

    tiles(depth, tile)


def outer_blur(me, part, recv_a, recv_b, wy, halo, body):
    rows, depth = part.shape[:2]
    radius = wy.shape[0] // 2
    even = me[3] == 0
    halo[jnp.where(even, 1, 0)] = recv_a[...]
    halo[jnp.where(even, 0, 1)] = recv_b[...]

    def tile(z):
        taps = [wy[i] for i in range(wy.shape[0])]
        sums = [part[y, z, :] for y in range(rows)]
        for side in range(2):
            for h in range(radius):
                y = h - radius if side == 0 else rows + h
                cell = halo[side, h, z, :]
                for o in range(radius) if side == 0 else range(rows - radius, rows):
                    i = y - o + radius
                    if 0 <= i < len(taps):
                        sums[o] = sums[o] + taps[i] * cell
        body(z, sums)

    tiles(depth, tile)


def bricks_of(outer, y):
    return y // BY if outer and y < 16 else y // BY + (4 if outer else 2)


def update(me, outer, rule, base, live, out, strips):
    def body(z, blurred):
        cells = []
        for y in range(len(blurred)):
            cells.append(rule(base[y, z, :], blurred[y], live[bricks_of(outer, y), z, :]))
            out[y, z, :] = cells[y]
        if strips:
            pack_tile(me, z, cells, *strips)

    return body


def deal_out(me, cells, pieces):
    rows, depth = pieces[0].shape[:2]
    for e in range(4):
        yl, zh = chip(me, e)
        pieces[e][...] = cells[slots(yl, rows), slots(zh, depth), :]


def inner_kernel(rule, me, cells, pair, after, outer, wz, wx, wh, wy, base, live, part, out, to_pair, to_next, inner):
    body = update(me, False, rule, base, live, out, (to_pair, to_next))
    inner_blur(me, cells, pair, after, outer, wz, wx, wh, wy, part, inner, body)


def last_inner_kernel(me, cells, pair, after, outer, wz, wx, wh, wy, base, live, part, *rest):
    pieces, inner, out = rest[:4], rest[4], rest[5]
    body = update(me, False, product, base, live, out, ())
    inner_blur(me, cells, pair, after, outer, wz, wx, wh, wy, part, inner, body)
    deal_out(me, out, pieces)


def final_kernel(rule, me, part, recv_a, recv_b, wy, base, live, out, to_pair, to_next, halo):
    outer_blur(me, part, recv_a, recv_b, wy, halo, update(me, True, rule, base, live, out, (to_pair, to_next)))


def last_final_kernel(me, part, recv_a, recv_b, wy, base, live, *rest):
    pieces, halo, out = rest[:4], rest[4], rest[5]
    outer_blur(me, part, recv_a, recv_b, wy, halo, update(me, True, product, base, live, out, ()))
    deal_out(me, out, pieces)


def call(kernel, out, ins, scratch=(), us=1, name=None, mib=6):
    many = isinstance(out, (tuple, list))
    return pl.pallas_call(
        kernel,
        out_shape=out,
        in_specs=ins,
        out_specs=[VMEM] * len(out) if many else VMEM,
        scratch_shapes=list(scratch),
        compiler_params=pltpu.CompilerParams(vmem_limit_bytes=mib * MIB),
        cost_estimate=pl.CostEstimate(flops=int(us * 1.0e9), bytes_accessed=0, transcendentals=0),
        name=name,
    )


def per_device(observed, psf_rows, psf_columns, psf_axial, live_list):
    yh = lax.axis_index("yh")
    yl, zh, zl = lax.axis_index("yl"), lax.axis_index("zh"), lax.axis_index("zl")
    side = zl ^ yl
    me = jnp.stack([yl, zh, zl, yh % 2, side]).astype(jnp.int32)
    channels, rows, depth, columns = observed.shape
    ny, nz = 2 * rows, 4 * depth
    radius = psf_rows.shape[1] // 2
    swaps = [(0, 1), (1, 0)]

    def trade(pieces):
        return [pieces[0]] + [
            lax.ppermute(pieces[e], ("yl", "zh"), [(i, i ^ e) for i in range(4)]) for e in range(1, 4)
        ]

    half = shape((ny // 2, nz, LANES))
    strip = shape((ny // 2 // (LANES // STRIP), nz, LANES))
    halo = shape((radius, nz, LANES))
    swapped = shape((4, rows // 2, depth, LANES))
    along = shape((rows // 2, 2 * depth, LANES))

    listed = live_list[0]
    theirs = lax.ppermute(listed, "yl", swaps)
    mine = shape((channels, 2, rows + 8, depth, LANES))
    kept, sent = call(deal_kernel, [mine] * 2, [SMEM, VMEM], us=0, name="deal")(me, observed)
    swapped_in = lax.ppermute(sent, "zl", swaps)
    tall = shape((rows // 2 + 4, 2 * depth, LANES))

    dealt = call(mix_kernel, [tall] * 8, [SMEM] + [VMEM] * 2, us=0, name="mix")(me, kept, swapped_in)
    dealt, theirs = lax.optimization_barrier((dealt, theirs))
    outer_pieces = trade(dealt[:4])
    inner_pieces = trade(dealt[4:])

    wide = [
        shape((4 * nz, 4 * nz), BF16),
        shape((2 * LANES, 2 * LANES), BF16),
        shape((2 * LANES, 4 * LANES), BF16),
        shape((psf_rows.shape[1], 8, LANES)),
    ]
    later, _ = lax.optimization_barrier((me, dealt))
    *weights, live = call(
        weights_kernel, wide * 2 + [shape((ny // BY, nz, LANES))], [SMEM] * 6, us=1, name="weights", mib=8
    )(later, psf_rows, psf_columns, psf_axial, listed, theirs)
    outer_pieces, weights, live = lax.optimization_barrier((outer_pieces, weights, live))

    def take(pieces):
        room = pltpu.VMEM((2,) + strip.shape, F32)
        return call(join_kernel, [half, strip, strip], [SMEM] + [VMEM] * 4, [room], us=0.3, name="join")(me, *pieces)

    high = lax.axis_size("yh")
    evens = [p for i in range(0, high - 1, 2) for p in ((i, i + 1), (i + 1, i))]
    odds = [p for i in range(1, high - 1, 2) for p in ((i, i + 1), (i + 1, i))]

    def exchange(to_pair, to_next):
        after = lax.ppermute(to_next, ("yl", "zl"), [(1, 3), (3, 1)])
        return lax.ppermute(to_pair, "zl", swaps), after

    def send_outer(cells, beside, w, near):
        wz, wx, wh, wy = w
        pair, after = beside
        cells, near = lax.optimization_barrier((cells, near))
        own = call(own_kernel, half, [VMEM] * 3, us=0.3, name="own", mib=8)(cells, wz, wx)
        outer, send_a, send_b = call(
            outer_kernel, [half, halo, halo], [SMEM] + [VMEM] * 5, us=0.3, name="outer", mib=8
        )(me, own, pair, after, wz, wh)
        return outer, lax.ppermute(send_a, "yh", evens), lax.ppermute(send_b, "yh", odds), near

    room, beyond = pltpu.VMEM(half.shape, F32), pltpu.VMEM((2,) + halo.shape, F32)
    taken = [take(outer_pieces), None]
    estimate = [taken[0][0], None]
    cells, strips = list(estimate), [taken[0][1:], None]
    for step in range(2 * ITERS):
        w = weights[:4] if step % 2 == 0 else weights[4:]
        near = exchange(*strips[1]) if step else ()
        beside = exchange(*strips[0]) if step else strips[0]
        outer, recv_a, recv_b, near = send_outer(cells[0], beside, w, near)
        if step == 0:
            inner_pieces, outer = lax.optimization_barrier((inner_pieces, outer))
            taken[1] = take(inner_pieces)
            estimate[1] = cells[1] = taken[1][0]
            near = taken[1][1:]
        base = [taken[0][0], taken[1][0]] if step % 2 == 0 else estimate
        ins = (me, cells[1], *near, outer, *w, base[1], live)
        if step == 2 * ITERS - 1:
            part, *pieces = call(
                last_inner_kernel, [half] + [along] * 4, [SMEM] + [VMEM] * 10, [room, room], us=3, name="last_inner", mib=16
            )(*ins)
            inner_out = trade(pieces)
            outer_out = trade(
                call(last_final_kernel, [along] * 4, [SMEM] + [VMEM] * 6, [beyond, room], us=2, name="last", mib=8)(
                    me, part, recv_a, recv_b, w[3], base[0], live
                )
            )
            continue
        rule = ratio if step % 2 == 0 else product
        part, inner, *inner_strips = call(
            functools.partial(inner_kernel, rule), [half, half, strip, strip], [SMEM] + [VMEM] * 10, [room], us=3,
            name="inner", mib=16,
        )(*ins)
        outer, *outer_strips = call(
            functools.partial(final_kernel, rule), [half, strip, strip], [SMEM] + [VMEM] * 6, [beyond], us=2,
            name="final", mib=8,
        )(me, part, recv_a, recv_b, w[3], base[0], live)
        cells, strips = [outer, inner], [outer_strips, inner_strips]
        if step % 2 == 1:
            estimate = cells

    def back(pieces):
        sent = call(split_depth_kernel, swapped, [SMEM] + [VMEM] * 4, us=1, name="split_back")(me, *pieces)
        return (*pieces, lax.ppermute(sent, "zl", swaps))

    return call(gather_kernel, shape(observed.shape), [SMEM] + [VMEM] * 10, us=2, name="gather", mib=8)(
        me, *back(outer_out), *back(inner_out)
    )


def solution(mesh):
    fine = Mesh(
        mesh.devices.reshape(mesh.devices.shape[0] // 2, 2, 2, mesh.devices.shape[1] // 2),
        ("yh", "yl", "zh", "zl"),
    )
    spread = P(None, ("yh", "yl"), ("zh", "zl"), None)
    placed = (spread, P(), P(), P(), P(("yh", "yl"), None, None))
    return jax.shard_map(per_device, mesh=fine, in_specs=placed, out_specs=spread, check_vma=False)
```

time: 157 us -> 142 us (0.904); the launches traced: 155 us -> 142 us
  waiting for transfers between devices: 38.6 us -> 26 us
  local copies, waits for them, and re-layouts: 4.64 us -> 1.69 us
  Pallas kernels: 51.5 us -> 53.3 us
    ppermute x31 -> x36, waiting for transfers between devices: 38.6 us -> 26 us  [the longest x12 23.5 us: trade(): lax.ppermute(pieces[e], ('yl', 'zh'), [(i, i ^ e) for i in range(4)])]
    unnamed x16 -> x10, local copies, waits for them, and re-layouts: 3.71 us -> 1.61 us
    pallas_call x20 -> x24, Pallas kernels: 51.5 us -> 53.3 us  [the longest x3 19.8 us: per_device(): call(functools.partial(inner_kernel, rule), [half, half, strip, strip], [...]
    ppermute x31 -> x36, starting transfers between devices: 58.9 us -> 60.3 us  [the longest x12 17.3 us: trade(): lax.ppermute(pieces[e], ('yl', 'zh'), [(i, i ^ e) for i in range(4)])]
  transfers between devices with their start and end apart: 31 -> 36, of which waited for: 9 -> 8; matrix products, arithmetic and copies ran while one was open for 1% -> 0% of each run, Pallas kernels for 21% -> 32%
where the time goes in v3:
time: 142 us
  starting transfers between devices  60.3 us (42%)
  Pallas kernels  53.3 us (38%)
  waiting for transfers between devices  26 us (18%)
  local copies, waits for them, and re-layouts  1.69 us (1%)
    ppermute x12, waiting for transfers between devices, trade(): lax.ppermute(pieces[e], ('yl', 'zh'), [(i, i ^ e) for i in range(4)])  23.5 us
    pallas_call x3, Pallas kernels, per_device(): call(functools.partial(inner_kernel, rule), [half, half, strip, strip], [...  19.8 us
    ppermute x12, starting transfers between devices, trade(): lax.ppermute(pieces[e], ('yl', 'zh'), [(i, i ^ e) for i in range(4)])  17.3 us
    ppermute x6, starting transfers between devices, exchange(): return (lax.ppermute(to_pair, 'zl', swaps), after)  14.9 us
    ppermute x4, starting transfers between devices, send_outer(): lax.ppermute(send_a, 'yh', evens)  9.26 us
    ppermute x2, starting transfers between devices, back(): return (*pieces, lax.ppermute(sent, 'zl', swaps))  8.93 us
    pallas_call x1, Pallas kernels, per_device(): call(last_inner_kernel, [half] + [along] * 4, [SMEM] + [VMEM] * 10, [room...  6.17 us
    pallas_call x3, Pallas kernels, per_device(): call(functools.partial(final_kernel, rule), [half, strip, strip], [SMEM]...  5.47 us
  transfers between devices with their start and end apart: 36, of which 8 were waited for; matrix products, arithmetic and copies ran while one was open for 0% of the time, Pallas kernels for 32%

profile of v3, /device:TPU:0, one launch (start us, length us, event | category | flops | bytes accessed | tf_op | source)
XLA Modules:
  0.0 141.6 jit_solution(16533341511858567987)
XLA Ops:
  0.1 1.6 %copy-done = f32[2,32,16,512]{3,2,1,0:T(8,128)S(1)} copy-done((f32[2,32,16,512]{3,2,1,0:T(8,128)S(1)}, f32[2,32,16,512]{3,2,1,0:T(8,128)}, u32[]{:S(2)}) %copy-start) | copy-done | bytes 2097176
  1.7 2.5 %deal.1 = (f32[2,2,40,16,128]{4,3,2,1,0:T(8,128)S(1)}, f32[2,2,40,16,128]{4,3,2,1,0:T(8,128)S(1)}) custom-call(s32[5]{0:T(128)S(1)} %stack.23.me, f32[2,32,16,512]{3,2,1,0:T(8,128)S(1)} %copy-done), custom_call_target="tpu_custom_call" | custom-call | tf_op jit(solution)/shard_map/deal/pallas_call | solution.py:456
  4.7 2.6 %collective-permute-start.1 = (s32[4,32]{1,0:T(4,128)S(1)}, s32[4,32]{1,0:T(4,128)S(1)}, u32[]{:S(2)}, u32[]{:S(2)}) collective-permute-start(s32[4,32]{1,0:T(4,128)S(1)} %bitcast.6), channel_id=1, source_target_pairs={{0,4},{4,0},{1,5},{5,1},{2,6},{6,2},{3,7},{7,3},{8,12},{12,8},{9,1... | collective-permute-start | bytes 1544 | tf_op jit(solution)/shard_map/ppermute | solution.py:454
  7.3 0.7 mix.1
  8.1 0.8 collective-permute-done.1.theirs
  8.9 2.2 %collective-permute-start.5 = (f32[20,32,128]{2,1,0:T(8,128)S(1)}, f32[20,32,128]{2,1,0:T(8,128)S(1)}, u32[]{:S(2)}, u32[]{:S(2)}) collective-permute-start(f32[20,32,128]{2,1,0:T(8,128)S(1)} %get-tuple-element.124), channel_id=1, source_target_pairs={{0,2},{2,0},{4,6},{6,4},{1,3},{3,1},{5,7},{7,5},{8,10},{10,8},{12,... | collective-permute-start | bytes 983048 | tf_op jit(solution)/shard_map/ppermute | solution.py:444
  11.0 1.5 %collective-permute-start.6 = (f32[20,32,128]{2,1,0:T(8,128)S(1)}, f32[20,32,128]{2,1,0:T(8,128)S(1)}, u32[]{:S(2)}, u32[]{:S(2)}) collective-permute-start(f32[20,32,128]{2,1,0:T(8,128)S(1)} %get-tuple-element.125), channel_id=1, source_target_pairs={{0,4},{2,6},{4,0},{6,2},{1,5},{3,7},{5,1},{7,3},{8,12},{10,14},{12... | collective-permute-start | bytes 983048 | tf_op jit(solution)/shard_map/ppermute | solution.py:444
  12.6 1.9 %collective-permute-start.2 = (f32[20,32,128]{2,1,0:T(8,128)S(1)}, f32[20,32,128]{2,1,0:T(8,128)S(1)}, u32[]{:S(2)}, u32[]{:S(2)}) collective-permute-start(f32[20,32,128]{2,1,0:T(8,128)S(1)} %get-tuple-element.120), channel_id=1, source_target_pairs={{0,2},{2,0},{4,6},{6,4},{1,3},{3,1},{5,7},{7,5},{8,10},{10,8},{12,... | collective-permute-start | bytes 983048 | tf_op jit(solution)/shard_map/ppermute | solution.py:444
  14.5 1.5 %collective-permute-start.3 = (f32[20,32,128]{2,1,0:T(8,128)S(1)}, f32[20,32,128]{2,1,0:T(8,128)S(1)}, u32[]{:S(2)}, u32[]{:S(2)}) collective-permute-start(f32[20,32,128]{2,1,0:T(8,128)S(1)} %get-tuple-element.121), channel_id=1, source_target_pairs={{0,4},{2,6},{4,0},{6,2},{1,5},{3,7},{5,1},{7,3},{8,12},{10,14},{12... | collective-permute-start | bytes 983048 | tf_op jit(solution)/shard_map/ppermute | solution.py:444
  16.0 3.5 %collective-permute-done.5.rest_1_ = f32[20,32,128]{2,1,0:T(8,128)S(1)} collective-permute-done((f32[20,32,128]{2,1,0:T(8,128)S(1)}, f32[20,32,128]{2,1,0:T(8,128)S(1)}, u32[]{:S(2)}, u32[]{:S(2)}) %collective-permute-start.5) | collective-permute-done | bytes 327712 | tf_op jit(solution)/shard_map/ppermute | solution.py:444
  19.5 3.0 %collective-permute-start.4 = (f32[20,32,128]{2,1,0:T(8,128)S(1)}, f32[20,32,128]{2,1,0:T(8,128)S(1)}, u32[]{:S(2)}, u32[]{:S(2)}) collective-permute-start(f32[20,32,128]{2,1,0:T(8,128)S(1)} %get-tuple-element.122), channel_id=1, source_target_pairs={{0,6},{2,4},{4,2},{6,0},{1,7},{3,5},{5,3},{7,1},{8,14},{10,12},{12... | collective-permute-start | bytes 983048 | tf_op jit(solution)/shard_map/ppermute | solution.py:444
  22.6 2.2 %weights.1 = (bf16[256,256]{1,0:T(8,128)(2,1)S(1)}, bf16[256,256]{1,0:T(8,128)(2,1)S(1)}, bf16[256,512]{1,0:T(8,128)(2,1)S(1)}, f32[31,8,128]{2,1,0:T(8,128)S(1)...) custom-call(s32[5]{0:T(128)S(1)} %stack.23.me, ...), custom_call_target="tpu_custom_call" | custom-call | flops 1000000000 | tf_op jit(solution)/shard_map/weights/pallas_call | solution.py:472
  24.8 3.9 %collective-permute-done.6.rest_2_ = f32[20,32,128]{2,1,0:T(8,128)S(1)} collective-permute-done((f32[20,32,128]{2,1,0:T(8,128)S(1)}, f32[20,32,128]{2,1,0:T(8,128)S(1)}, u32[]{:S(2)}, u32[]{:S(2)}) %collective-permute-start.6) | collective-permute-done | bytes 327712 | tf_op jit(solution)/shard_map/ppermute | solution.py:444
  28.7 1.2 join.2
  29.9 1.0 own.4
  30.9 1.3 outer.4
  32.2 1.7 %collective-permute-start.8 = (f32[15,64,128]{2,1,0:T(8,128)S(1)}, f32[15,64,128]{2,1,0:T(8,128)S(1)}, u32[]{:S(2)}, u32[]{:S(2)}) collective-permute-start(f32[15,64,128]{2,1,0:T(8,128)S(1)} %get-tuple-element.161), channel_id=1, source_target_pairs={{0,8},{8,0},{16,24},{24,16},{1,9},{9,1},{17,25},{25,17},{2,10},{10... | collective-permute-start | bytes 1474568 | tf_op jit(solution)/shard_map/ppermute | solution.py:497
  33.8 0.7 collective-permute-start.9
  34.5 7.0 %collective-permute-done.3.rest_2_ = f32[20,32,128]{2,1,0:T(8,128)S(1)} collective-permute-done((f32[20,32,128]{2,1,0:T(8,128)S(1)}, f32[20,32,128]{2,1,0:T(8,128)S(1)}, u32[]{:S(2)}, u32[]{:S(2)}) %collective-permute-start.3) | collective-permute-done | bytes 327712 | tf_op jit(solution)/shard_map/ppermute | solution.py:444
  41.6 1.2 join.3
  42.8 6.6 %inner.3 = (f32[32,64,128]{2,1,0:T(8,128)S(1)}, f32[32,64,128]{2,1,0:T(8,128)S(1)}, f32[4,64,128]{2,1,0:T(8,128)S(1)}, f32[4,64,128]{2,1,0:T(8,128)S(1)}) custom-call(s32[5]{0:T(128)S(1)} %stack.23.me, f32[32,64,128]{2,1,0:T(8,128)S(1)} %get-tuple-element.153.cells.base, f32[4,64,128]{2,1,0:T(8,128)S(1)} %get-tuple-element.154.pair, ...), custom_call_target="tpu_custom_call" | custom-call | flops 3000000000 | tf_op jit(solution)/shard_map/inner/pallas_call | solution.py:527
  49.5 0.7 collective-permute-start.11
  50.2 1.8 %final.3 = (f32[32,64,128]{2,1,0:T(8,128)S(1)}, f32[4,64,128]{2,1,0:T(8,128)S(1)}, f32[4,64,128]{2,1,0:T(8,128)S(1)}) custom-call(s32[5]{0:T(128)S(1)} %stack.23.me, f32[32,64,128]{2,1,0:T(8,128)S(1)} %get-tuple-element.160.part, f32[15,64,128]{2,1,0:T(8,128)S(1)} %collective-permute-done.8.recv_a, f32[15,64,128]{2,1,0:T(8,128)S(1)} %collective-permute-done.9.recv_b, ...), custom_call_target="tpu_custom_call" | custom-call | flops 2000000000 | tf_op jit(solution)/shard_map/final/pallas_call | solution.py:531
  52.1 3.0 %collective-permute-start.12 = (f32[4,64,128]{2,1,0:T(8,128)S(1)}, f32[4,64,128]{2,1,0:T(8,128)S(1)}, u32[]{:S(2)}, u32[]{:S(2)}) collective-permute-start(f32[4,64,128]{2,1,0:T(8,128)S(1)} %get-tuple-element.171), channel_id=1, source_target_pairs={{0,1},{1,0},{2,3},{3,2},{4,5},{5,4},{6,7},{7,6},{8,9},{9,8},{10,11... | collective-permute-start | bytes 393224 | tf_op jit(solution)/shard_map/ppermute | solution.py:487
  55.1 0.7 collective-permute-start.13
  55.8 1.0 own.5
  56.8 1.3 outer.5
  58.1 1.6 %collective-permute-start.14 = (f32[15,64,128]{2,1,0:T(8,128)S(1)}, f32[15,64,128]{2,1,0:T(8,128)S(1)}, u32[]{:S(2)}, u32[]{:S(2)}) collective-permute-start(f32[15,64,128]{2,1,0:T(8,128)S(1)} %get-tuple-element.178), channel_id=1, source_target_pairs={{0,8},{8,0},{16,24},{24,16},{1,9},{9,1},{17,25},{25,17},{2,10},{10... | collective-permute-start | bytes 1474568 | tf_op jit(solution)/shard_map/ppermute | solution.py:497
  59.8 0.7 collective-permute-start.15
  60.4 6.5 %inner.4 = (f32[32,64,128]{2,1,0:T(8,128)S(1)}, f32[32,64,128]{2,1,0:T(8,128)S(1)}, f32[4,64,128]{2,1,0:T(8,128)S(1)}, f32[4,64,128]{2,1,0:T(8,128)S(1)}) custom-call(s32[5]{0:T(128)S(1)} %stack.23.me, f32[32,64,128]{2,1,0:T(8,128)S(1)} %get-tuple-element.159.cells, f32[4,64,128]{2,1,0:T(8,128)S(1)} %collective-permute-done.10.pair, ...), custom_call_target="tpu_custom_call" | custom-call | flops 3000000000 | tf_op jit(solution)/shard_map/inner/pallas_call | solution.py:527
  66.9 3.8 %collective-permute-start.16 = (f32[4,64,128]{2,1,0:T(8,128)S(1)}, f32[4,64,128]{2,1,0:T(8,128)S(1)}, u32[]{:S(2)}, u32[]{:S(2)}) collective-permute-start(f32[4,64,128]{2,1,0:T(8,128)S(1)} %get-tuple-element.181), channel_id=1, source_target_pairs={{0,1},{1,0},{2,3},{3,2},{4,5},{5,4},{6,7},{7,6},{8,9},{9,8},{10,11... | collective-permute-start | bytes 393224 | tf_op jit(solution)/shard_map/ppermute | solution.py:487
  70.8 0.8 collective-permute-start.17
  71.6 1.8 %final.4 = (f32[32,64,128]{2,1,0:T(8,128)S(1)}, f32[4,64,128]{2,1,0:T(8,128)S(1)}, f32[4,64,128]{2,1,0:T(8,128)S(1)}) custom-call(s32[5]{0:T(128)S(1)} %stack.23.me, f32[32,64,128]{2,1,0:T(8,128)S(1)} %get-tuple-element.177.part, f32[15,64,128]{2,1,0:T(8,128)S(1)} %collective-permute-done.14.recv_a, f32[15,64,128]{2,1,0:T(8,128)S(1)} %collective-permute-done.15.recv_b, ...), custom_call_target="tpu_custom_call" | custom-call | flops 2000000000 | tf_op jit(solution)/shard_map/final/pallas_call | solution.py:531
  73.4 1.6 %collective-permute-start.18 = (f32[4,64,128]{2,1,0:T(8,128)S(1)}, f32[4,64,128]{2,1,0:T(8,128)S(1)}, u32[]{:S(2)}, u32[]{:S(2)}) collective-permute-start(f32[4,64,128]{2,1,0:T(8,128)S(1)} %get-tuple-element.186), channel_id=1, source_target_pairs={{0,1},{1,0},{2,3},{3,2},{4,5},{5,4},{6,7},{7,6},{8,9},{9,8},{10,11... | collective-permute-start | bytes 393224 | tf_op jit(solution)/shard_map/ppermute | solution.py:487
  75.0 0.7 collective-permute-start.19
  75.7 1.0 own.6
  76.7 1.3 outer.6
  78.0 4.2 %collective-permute-start.20 = (f32[15,64,128]{2,1,0:T(8,128)S(1)}, f32[15,64,128]{2,1,0:T(8,128)S(1)}, u32[]{:S(2)}, u32[]{:S(2)}) collective-permute-start(f32[15,64,128]{2,1,0:T(8,128)S(1)} %get-tuple-element.191), channel_id=1, source_target_pairs={{0,8},{8,0},{16,24},{24,16},{1,9},{9,1},{17,25},{25,17},{2,10},{10... | collective-permute-start | bytes 1474568 | tf_op jit(solution)/shard_map/ppermute | solution.py:497
  82.2 0.7 collective-permute-start.21
  82.8 6.6 %inner.5 = (f32[32,64,128]{2,1,0:T(8,128)S(1)}, f32[32,64,128]{2,1,0:T(8,128)S(1)}, f32[4,64,128]{2,1,0:T(8,128)S(1)}, f32[4,64,128]{2,1,0:T(8,128)S(1)}) custom-call(s32[5]{0:T(128)S(1)} %stack.23.me, f32[32,64,128]{2,1,0:T(8,128)S(1)} %get-tuple-element.176.cells.base, f32[4,64,128]{2,1,0:T(8,128)S(1)} %collective-permute-done.16.pair, ...), custom_call_target="tpu_custom_call" | custom-call | flops 3000000000 | tf_op jit(solution)/shard_map/inner/pallas_call | solution.py:527
  89.5 3.8 %collective-permute-start.22 = (f32[4,64,128]{2,1,0:T(8,128)S(1)}, f32[4,64,128]{2,1,0:T(8,128)S(1)}, u32[]{:S(2)}, u32[]{:S(2)}) collective-permute-start(f32[4,64,128]{2,1,0:T(8,128)S(1)} %get-tuple-element.194), channel_id=1, source_target_pairs={{0,1},{1,0},{2,3},{3,2},{4,5},{5,4},{6,7},{7,6},{8,9},{9,8},{10,11... | collective-permute-start | bytes 393224 | tf_op jit(solution)/shard_map/ppermute | solution.py:487
  93.3 0.7 collective-permute-start.23
  94.0 1.8 %final.5 = (f32[32,64,128]{2,1,0:T(8,128)S(1)}, f32[4,64,128]{2,1,0:T(8,128)S(1)}, f32[4,64,128]{2,1,0:T(8,128)S(1)}) custom-call(s32[5]{0:T(128)S(1)} %stack.23.me, f32[32,64,128]{2,1,0:T(8,128)S(1)} %get-tuple-element.190.part, f32[15,64,128]{2,1,0:T(8,128)S(1)} %collective-permute-done.20.recv_a, f32[15,64,128]{2,1,0:T(8,128)S(1)} %collective-permute-done.21.recv_b, ...), custom_call_target="tpu_custom_call" | custom-call | flops 2000000000 | tf_op jit(solution)/shard_map/final/pallas_call | solution.py:531
  95.8 2.6 %collective-permute-start.24 = (f32[4,64,128]{2,1,0:T(8,128)S(1)}, f32[4,64,128]{2,1,0:T(8,128)S(1)}, u32[]{:S(2)}, u32[]{:S(2)}) collective-permute-start(f32[4,64,128]{2,1,0:T(8,128)S(1)} %get-tuple-element.199), channel_id=1, source_target_pairs={{0,1},{1,0},{2,3},{3,2},{4,5},{5,4},{6,7},{7,6},{8,9},{9,8},{10,11... | collective-permute-start | bytes 393224 | tf_op jit(solution)/shard_map/ppermute | solution.py:487
  98.4 0.7 collective-permute-start.25
  99.1 1.0 own.7
  100.1 1.3 outer.7
  101.4 1.8 %collective-permute-start.26 = (f32[15,64,128]{2,1,0:T(8,128)S(1)}, f32[15,64,128]{2,1,0:T(8,128)S(1)}, u32[]{:S(2)}, u32[]{:S(2)}) collective-permute-start(f32[15,64,128]{2,1,0:T(8,128)S(1)} %get-tuple-element.203), channel_id=1, source_target_pairs={{0,8},{8,0},{16,24},{24,16},{1,9},{9,1},{17,25},{25,17},{2,10},{10... | collective-permute-start | bytes 1474568 | tf_op jit(solution)/shard_map/ppermute | solution.py:497
  103.2 0.7 collective-permute-start.27
  103.9 6.2 %last_inner.1 = (f32[32,64,128]{2,1,0:T(8,128)S(1)}, f32[16,32,128]{2,1,0:T(8,128)S(1)}, f32[16,32,128]{2,1,0:T(8,128)S(1)}, f32[16,32,128]{2,1,0:T(8,128)S(1)}, f32[16,32,128]{2,1,0:T(8,128)S(1)}) custom-call(s32[5]{0:T(128)S(1)} %stack.23.me, f32[32,64,128]{2,1,0:T(8,128)S(1)} %get-tuple-element.189.cells, f32[4,64,128]{2,1,0:T(8,128)S(1)} %collective-permute-done.22.pair, ...), custom_call_target="tpu_custom_call" | custom-call | flops 3000000000 | tf_op jit(solution)/shard_map/last_inner/pallas_call | solution.py:516
  110.1 1.3 collective-permute-start.32
  111.4 0.8 collective-permute-start.33
  112.2 1.4 %collective-permute-start.34 = (f32[16,32,128]{2,1,0:T(8,128)S(1)}, f32[16,32,128]{2,1,0:T(8,128)S(1)}, u32[]{:S(2)}, u32[]{:S(2)}) collective-permute-start(f32[16,32,128]{2,1,0:T(8,128)S(1)} %get-tuple-element.212), channel_id=1, source_target_pairs={{0,6},{2,4},{4,2},{6,0},{1,7},{3,5},{5,3},{7,1},{8,14},{10,12},{12... | collective-permute-start | bytes 786440 | tf_op jit(solution)/shard_map/ppermute | solution.py:444
  113.7 1.5 %last.1 = (f32[16,32,128]{2,1,0:T(8,128)S(1)}, f32[16,32,128]{2,1,0:T(8,128)S(1)}, f32[16,32,128]{2,1,0:T(8,128)S(1)}, f32[16,32,128]{2,1,0:T(8,128)S(1)}) custom-call(s32[5]{0:T(128)S(1)} %stack.23.me, f32[32,64,128]{2,1,0:T(8,128)S(1)} %get-tuple-element.202.part, f32[15,64,128]{2,1,0:T(8,128)S(1)} %collective-permute-done.26.recv_a, ...), custom_call_target="tpu_custom_call" | custom-call | flops 2000000000 | tf_op jit(solution)/shard_map/last/pallas_call | solution.py:521
  115.1 1.3 collective-permute-start.28
  116.5 0.8 collective-permute-start.29
  117.3 1.4 %collective-permute-start.30 = (f32[16,32,128]{2,1,0:T(8,128)S(1)}, f32[16,32,128]{2,1,0:T(8,128)S(1)}, u32[]{:S(2)}, u32[]{:S(2)}) collective-permute-start(f32[16,32,128]{2,1,0:T(8,128)S(1)} %get-tuple-element.208), channel_id=1, source_target_pairs={{0,6},{2,4},{4,2},{6,0},{1,7},{3,5},{5,3},{7,1},{8,14},{10,12},{12... | collective-permute-start | bytes 786440 | tf_op jit(solution)/shard_map/ppermute | solution.py:444
  118.7 4.4 %collective-permute-done.34.rest_3_.rest_8_ = f32[16,32,128]{2,1,0:T(8,128)S(1)} collective-permute-done((f32[16,32,128]{2,1,0:T(8,128)S(1)}, f32[16,32,128]{2,1,0:T(8,128)S(1)}, u32[]{:S(2)}, u32[]{:S(2)}) %collective-permute-start.34) | collective-permute-done | bytes 262176 | tf_op jit(solution)/shard_map/ppermute | solution.py:444
  123.7 5.9 %collective-permute-start.35 = (f32[4,16,16,128]{3,2,1,0:T(8,128)S(1)}, f32[4,16,16,128]{3,2,1,0:T(8,128)S(1)}, u32[]{:S(2)}, u32[]{:S(2)}) collective-permute-start(f32[4,16,16,128]{3,2,1,0:T(8,128)S(1)} %split_back.3), channel_id=1, source_target_pairs={{0,1},{1,0},{2,3},{3,2},{4,5},{5,4},{6,7},{7,6},{8,9},{9,8},{10,11... | collective-permute-start | bytes 1572872 | tf_op jit(solution)/shard_map/ppermute | solution.py:541
  129.5 1.9 %collective-permute-done.29.rest_2_ = f32[16,32,128]{2,1,0:T(8,128)S(1)} collective-permute-done((f32[16,32,128]{2,1,0:T(8,128)S(1)}, f32[16,32,128]{2,1,0:T(8,128)S(1)}, u32[]{:S(2)}, u32[]{:S(2)}) %collective-permute-start.29) | collective-permute-done | bytes 262176 | tf_op jit(solution)/shard_map/ppermute | solution.py:444
  131.4 2.9 %collective-permute-done.30.rest_3_ = f32[16,32,128]{2,1,0:T(8,128)S(1)} collective-permute-done((f32[16,32,128]{2,1,0:T(8,128)S(1)}, f32[16,32,128]{2,1,0:T(8,128)S(1)}, u32[]{:S(2)}, u32[]{:S(2)}) %collective-permute-start.30) | collective-permute-done | bytes 262176 | tf_op jit(solution)/shard_map/ppermute | solution.py:444
  134.9 3.1 %collective-permute-start.31 = (f32[4,16,16,128]{3,2,1,0:T(8,128)S(1)}, f32[4,16,16,128]{3,2,1,0:T(8,128)S(1)}, u32[]{:S(2)}, u32[]{:S(2)}) collective-permute-start(f32[4,16,16,128]{3,2,1,0:T(8,128)S(1)} %split_back.2), channel_id=1, source_target_pairs={{0,1},{1,0},{2,3},{3,2},{4,5},{5,4},{6,7},{7,6},{8,9},{9,8},{10,11... | collective-permute-start | bytes 1572872 | tf_op jit(solution)/shard_map/ppermute | solution.py:541
  138.0 1.5 %collective-permute-done.31.rest_4_ = f32[4,16,16,128]{3,2,1,0:T(8,128)S(1)} collective-permute-done((f32[4,16,16,128]{3,2,1,0:T(8,128)S(1)}, f32[4,16,16,128]{3,2,1,0:T(8,128)S(1)}, u32[]{:S(2)}, u32[]{:S(2)}) %collective-permute-start.31) | collective-permute-done | bytes 524320 | tf_op jit(solution)/shard_map/ppermute | solution.py:541
  139.5 2.1 %gather.1 = f32[2,32,16,512]{3,2,1,0:T(8,128)} custom-call(s32[5]{0:T(128)S(1)} %stack.23.me, f32[16,32,128]{2,1,0:T(8,128)S(1)} %get-tuple-element.205.rest_0_, f32[16,32,128]{2,1,0:T(8,128)S(1)} %collective-permute-done.28.rest_1_, f32[16,32,128]{2,1,0:T(8,128)S(1)} %collective-permute-done.29.rest_2_, f32[16,32,128]{2,1,0:T(8,128)S(1)} %collective-permute-done.30.rest_3_, ...), custom_call_target="tpu_custom_call" | custom-call | flops 2000000000 | tf_op jit(solution)/shard_map/gather/pallas_call | solution.py:543
  (43 shorter events, 2.0 us)
Async XLA Ops:
  0.0 4.7 %copy-start.1 = (s32[1,4,32]{2,1,0:T(4,128)S(1)}, s32[1,4,32]{2,1,0:T(4,128)}, u32[]{:S(2)}) copy-start(s32[1,4,32]{2,1,0:T(4,128)} %param.9) | copy-start | bytes 1540
  0.1 1.6 %copy-start = (f32[2,32,16,512]{3,2,1,0:T(8,128)S(1)}, f32[2,32,16,512]{3,2,1,0:T(8,128)}, u32[]{:S(2)}) copy-start(f32[2,32,16,512]{3,2,1,0:T(8,128)} %observed.1) | copy-start | bytes 6291460
  4.2 3.2 %collective-permute-start = (f32[2,2,40,16,128]{4,3,2,1,0:T(8,128)S(1)}, f32[2,2,40,16,128]{4,3,2,1,0:T(8,128)S(1)}, u32[]{:S(2)}, u32[]{:S(2)}) collective-permute-start(f32[2,2,40,16,128]{4,3,2,1,0:T(8,128)S(1)} %get-tuple-element.110), channel_id=1, source_target_pairs={{0,1},{1,0},{2,3},{3,2},{4,5},{5,4},{6,7},{7,6},{8,9},{9,8},{10,11... | collective-permute-start | bytes 3932168 | tf_op jit(solution)/shard_map/ppermute | solution.py:457
  4.7 4.2 %collective-permute-start.1 = (s32[4,32]{1,0:T(4,128)S(1)}, s32[4,32]{1,0:T(4,128)S(1)}, u32[]{:S(2)}, u32[]{:S(2)}) collective-permute-start(s32[4,32]{1,0:T(4,128)S(1)} %bitcast.6), channel_id=1, source_target_pairs={{0,4},{4,0},{1,5},{5,1},{2,6},{6,2},{3,7},{7,3},{8,12},{12,8},{9,1... | collective-permute-start | bytes 1544 | tf_op jit(solution)/shard_map/ppermute | solution.py:454
  7.3 15.2 %copy-start.2 = (f32[2,31]{1,0:T(2,128)S(1)}, f32[2,31]{1,0:T(2,128)}, u32[]{:S(2)}) copy-start(f32[2,31]{1,0:T(2,128)} %rows.1) | copy-start | bytes 748
  7.3 15.2 %copy-start.3 = (f32[2,31]{1,0:T(2,128)S(1)}, f32[2,31]{1,0:T(2,128)}, u32[]{:S(2)}) copy-start(f32[2,31]{1,0:T(2,128)} %columns.1) | copy-start | bytes 748
  7.3 15.2 %copy-start.4 = (f32[2,101]{1,0:T(2,128)S(1)}, f32[2,101]{1,0:T(2,128)}, u32[]{:S(2)}) copy-start(f32[2,101]{1,0:T(2,128)} %axial.1) | copy-start | bytes 2428
  8.9 10.7 %collective-permute-start.5 = (f32[20,32,128]{2,1,0:T(8,128)S(1)}, f32[20,32,128]{2,1,0:T(8,128)S(1)}, u32[]{:S(2)}, u32[]{:S(2)}) collective-permute-start(f32[20,32,128]{2,1,0:T(8,128)S(1)} %get-tuple-element.124), channel_id=1, source_target_pairs={{0,2},{2,0},{4,6},{6,4},{1,3},{3,1},{5,7},{7,5},{8,10},{10,8},{12,... | collective-permute-start | bytes 983048 | tf_op jit(solution)/shard_map/ppermute | solution.py:444
  11.0 17.6 %collective-permute-start.6 = (f32[20,32,128]{2,1,0:T(8,128)S(1)}, f32[20,32,128]{2,1,0:T(8,128)S(1)}, u32[]{:S(2)}, u32[]{:S(2)}) collective-permute-start(f32[20,32,128]{2,1,0:T(8,128)S(1)} %get-tuple-element.125), channel_id=1, source_target_pairs={{0,4},{2,6},{4,0},{6,2},{1,5},{3,7},{5,1},{7,3},{8,12},{10,14},{12... | collective-permute-start | bytes 983048 | tf_op jit(solution)/shard_map/ppermute | solution.py:444
  12.6 16.1 %collective-permute-start.7 = (f32[20,32,128]{2,1,0:T(8,128)S(1)}, f32[20,32,128]{2,1,0:T(8,128)S(1)}, u32[]{:S(2)}, u32[]{:S(2)}) collective-permute-start(f32[20,32,128]{2,1,0:T(8,128)S(1)} %get-tuple-element.126), channel_id=1, source_target_pairs={{0,6},{2,4},{4,2},{6,0},{1,7},{3,5},{5,3},{7,1},{8,14},{10,12},{12... | collective-permute-start | bytes 983048 | tf_op jit(solution)/shard_map/ppermute | solution.py:444
  12.6 22.0 %collective-permute-start.2 = (f32[20,32,128]{2,1,0:T(8,128)S(1)}, f32[20,32,128]{2,1,0:T(8,128)S(1)}, u32[]{:S(2)}, u32[]{:S(2)}) collective-permute-start(f32[20,32,128]{2,1,0:T(8,128)S(1)} %get-tuple-element.120), channel_id=1, source_target_pairs={{0,2},{2,0},{4,6},{6,4},{1,3},{3,1},{5,7},{7,5},{8,10},{10,8},{12,... | collective-permute-start | bytes 983048 | tf_op jit(solution)/shard_map/ppermute | solution.py:444
  14.5 27.1 %collective-permute-start.3 = (f32[20,32,128]{2,1,0:T(8,128)S(1)}, f32[20,32,128]{2,1,0:T(8,128)S(1)}, u32[]{:S(2)}, u32[]{:S(2)}) collective-permute-start(f32[20,32,128]{2,1,0:T(8,128)S(1)} %get-tuple-element.121), channel_id=1, source_target_pairs={{0,4},{2,6},{4,0},{6,2},{1,5},{3,7},{5,1},{7,3},{8,12},{10,14},{12... | collective-permute-start | bytes 983048 | tf_op jit(solution)/shard_map/ppermute | solution.py:444
  19.5 22.0 %collective-permute-start.4 = (f32[20,32,128]{2,1,0:T(8,128)S(1)}, f32[20,32,128]{2,1,0:T(8,128)S(1)}, u32[]{:S(2)}, u32[]{:S(2)}) collective-permute-start(f32[20,32,128]{2,1,0:T(8,128)S(1)} %get-tuple-element.122), channel_id=1, source_target_pairs={{0,6},{2,4},{4,2},{6,0},{1,7},{3,5},{5,3},{7,1},{8,14},{10,12},{12... | collective-permute-start | bytes 983048 | tf_op jit(solution)/shard_map/ppermute | solution.py:444
  32.2 18.0 %collective-permute-start.8 = (f32[15,64,128]{2,1,0:T(8,128)S(1)}, f32[15,64,128]{2,1,0:T(8,128)S(1)}, u32[]{:S(2)}, u32[]{:S(2)}) collective-permute-start(f32[15,64,128]{2,1,0:T(8,128)S(1)} %get-tuple-element.161), channel_id=1, source_target_pairs={{0,8},{8,0},{16,24},{24,16},{1,9},{9,1},{17,25},{25,17},{2,10},{10... | collective-permute-start | bytes 1474568 | tf_op jit(solution)/shard_map/ppermute | solution.py:497
  33.8 16.4 %collective-permute-start.9 = (f32[15,64,128]{2,1,0:T(8,128)S(1)}, f32[15,64,128]{2,1,0:T(8,128)S(1)}, u32[]{:S(2)}, u32[]{:S(2)}) collective-permute-start(f32[15,64,128]{2,1,0:T(8,128)S(1)} %get-tuple-element.162), channel_id=1, source_target_pairs={{8,16},{16,8},{9,17},{17,9},{10,18},{18,10},{11,19},{19,11},{12,20... | collective-permute-start | bytes 1474568 | tf_op jit(solution)/shard_map/ppermute | solution.py:497
  49.4 6.3 %collective-permute-start.10 = (f32[4,64,128]{2,1,0:T(8,128)S(1)}, f32[4,64,128]{2,1,0:T(8,128)S(1)}, u32[]{:S(2)}, u32[]{:S(2)}) collective-permute-start(f32[4,64,128]{2,1,0:T(8,128)S(1)} %get-tuple-element.164), channel_id=1, source_target_pairs={{0,1},{1,0},{2,3},{3,2},{4,5},{5,4},{6,7},{7,6},{8,9},{9,8},{10,11... | collective-permute-start | bytes 393224 | tf_op jit(solution)/shard_map/ppermute | solution.py:487
  49.5 6.2 %collective-permute-start.11 = (f32[4,64,128]{2,1,0:T(8,128)S(1)}, f32[4,64,128]{2,1,0:T(8,128)S(1)}, u32[]{:S(2)}, u32[]{:S(2)}) collective-permute-start(f32[4,64,128]{2,1,0:T(8,128)S(1)} %get-tuple-element.165), channel_id=1, source_target_pairs={{1,5},{5,1},{3,7},{7,3},{9,13},{13,9},{11,15},{15,11},{17,21},{21,... | collective-permute-start | bytes 393224 | tf_op jit(solution)/shard_map/ppermute | solution.py:486
  52.1 4.7 %collective-permute-start.12 = (f32[4,64,128]{2,1,0:T(8,128)S(1)}, f32[4,64,128]{2,1,0:T(8,128)S(1)}, u32[]{:S(2)}, u32[]{:S(2)}) collective-permute-start(f32[4,64,128]{2,1,0:T(8,128)S(1)} %get-tuple-element.171), channel_id=1, source_target_pairs={{0,1},{1,0},{2,3},{3,2},{4,5},{5,4},{6,7},{7,6},{8,9},{9,8},{10,11... | collective-permute-start | bytes 393224 | tf_op jit(solution)/shard_map/ppermute | solution.py:487
  55.1 1.7 %collective-permute-start.13 = (f32[4,64,128]{2,1,0:T(8,128)S(1)}, f32[4,64,128]{2,1,0:T(8,128)S(1)}, u32[]{:S(2)}, u32[]{:S(2)}) collective-permute-start(f32[4,64,128]{2,1,0:T(8,128)S(1)} %get-tuple-element.172), channel_id=1, source_target_pairs={{1,5},{5,1},{3,7},{7,3},{9,13},{13,9},{11,15},{15,11},{17,21},{21,... | collective-permute-start | bytes 393224 | tf_op jit(solution)/shard_map/ppermute | solution.py:486
  58.1 13.5 %collective-permute-start.14 = (f32[15,64,128]{2,1,0:T(8,128)S(1)}, f32[15,64,128]{2,1,0:T(8,128)S(1)}, u32[]{:S(2)}, u32[]{:S(2)}) collective-permute-start(f32[15,64,128]{2,1,0:T(8,128)S(1)} %get-tuple-element.178), channel_id=1, source_target_pairs={{0,8},{8,0},{16,24},{24,16},{1,9},{9,1},{17,25},{25,17},{2,10},{10... | collective-permute-start | bytes 1474568 | tf_op jit(solution)/shard_map/ppermute | solution.py:497
  59.8 11.9 %collective-permute-start.15 = (f32[15,64,128]{2,1,0:T(8,128)S(1)}, f32[15,64,128]{2,1,0:T(8,128)S(1)}, u32[]{:S(2)}, u32[]{:S(2)}) collective-permute-start(f32[15,64,128]{2,1,0:T(8,128)S(1)} %get-tuple-element.179), channel_id=1, source_target_pairs={{8,16},{16,8},{9,17},{17,9},{10,18},{18,10},{11,19},{19,11},{12,20... | collective-permute-start | bytes 1474568 | tf_op jit(solution)/shard_map/ppermute | solution.py:497
  66.9 8.7 %collective-permute-start.16 = (f32[4,64,128]{2,1,0:T(8,128)S(1)}, f32[4,64,128]{2,1,0:T(8,128)S(1)}, u32[]{:S(2)}, u32[]{:S(2)}) collective-permute-start(f32[4,64,128]{2,1,0:T(8,128)S(1)} %get-tuple-element.181), channel_id=1, source_target_pairs={{0,1},{1,0},{2,3},{3,2},{4,5},{5,4},{6,7},{7,6},{8,9},{9,8},{10,11... | collective-permute-start | bytes 393224 | tf_op jit(solution)/shard_map/ppermute | solution.py:487
  70.8 4.9 %collective-permute-start.17 = (f32[4,64,128]{2,1,0:T(8,128)S(1)}, f32[4,64,128]{2,1,0:T(8,128)S(1)}, u32[]{:S(2)}, u32[]{:S(2)}) collective-permute-start(f32[4,64,128]{2,1,0:T(8,128)S(1)} %get-tuple-element.182), channel_id=1, source_target_pairs={{1,5},{5,1},{3,7},{7,3},{9,13},{13,9},{11,15},{15,11},{17,21},{21,... | collective-permute-start | bytes 393224 | tf_op jit(solution)/shard_map/ppermute | solution.py:486
  73.4 3.2 %collective-permute-start.18 = (f32[4,64,128]{2,1,0:T(8,128)S(1)}, f32[4,64,128]{2,1,0:T(8,128)S(1)}, u32[]{:S(2)}, u32[]{:S(2)}) collective-permute-start(f32[4,64,128]{2,1,0:T(8,128)S(1)} %get-tuple-element.186), channel_id=1, source_target_pairs={{0,1},{1,0},{2,3},{3,2},{4,5},{5,4},{6,7},{7,6},{8,9},{9,8},{10,11... | collective-permute-start | bytes 393224 | tf_op jit(solution)/shard_map/ppermute | solution.py:487
  75.0 1.7 %collective-permute-start.19 = (f32[4,64,128]{2,1,0:T(8,128)S(1)}, f32[4,64,128]{2,1,0:T(8,128)S(1)}, u32[]{:S(2)}, u32[]{:S(2)}) collective-permute-start(f32[4,64,128]{2,1,0:T(8,128)S(1)} %get-tuple-element.187), channel_id=1, source_target_pairs={{1,5},{5,1},{3,7},{7,3},{9,13},{13,9},{11,15},{15,11},{17,21},{21,... | collective-permute-start | bytes 393224 | tf_op jit(solution)/shard_map/ppermute | solution.py:486
  78.0 16.0 %collective-permute-start.20 = (f32[15,64,128]{2,1,0:T(8,128)S(1)}, f32[15,64,128]{2,1,0:T(8,128)S(1)}, u32[]{:S(2)}, u32[]{:S(2)}) collective-permute-start(f32[15,64,128]{2,1,0:T(8,128)S(1)} %get-tuple-element.191), channel_id=1, source_target_pairs={{0,8},{8,0},{16,24},{24,16},{1,9},{9,1},{17,25},{25,17},{2,10},{10... | collective-permute-start | bytes 1474568 | tf_op jit(solution)/shard_map/ppermute | solution.py:497
  82.2 11.8 %collective-permute-start.21 = (f32[15,64,128]{2,1,0:T(8,128)S(1)}, f32[15,64,128]{2,1,0:T(8,128)S(1)}, u32[]{:S(2)}, u32[]{:S(2)}) collective-permute-start(f32[15,64,128]{2,1,0:T(8,128)S(1)} %get-tuple-element.192), channel_id=1, source_target_pairs={{8,16},{16,8},{9,17},{17,9},{10,18},{18,10},{11,19},{19,11},{12,20... | collective-permute-start | bytes 1474568 | tf_op jit(solution)/shard_map/ppermute | solution.py:497
  89.5 9.6 %collective-permute-start.22 = (f32[4,64,128]{2,1,0:T(8,128)S(1)}, f32[4,64,128]{2,1,0:T(8,128)S(1)}, u32[]{:S(2)}, u32[]{:S(2)}) collective-permute-start(f32[4,64,128]{2,1,0:T(8,128)S(1)} %get-tuple-element.194), channel_id=1, source_target_pairs={{0,1},{1,0},{2,3},{3,2},{4,5},{5,4},{6,7},{7,6},{8,9},{9,8},{10,11... | collective-permute-start | bytes 393224 | tf_op jit(solution)/shard_map/ppermute | solution.py:487
  93.3 5.8 %collective-permute-start.23 = (f32[4,64,128]{2,1,0:T(8,128)S(1)}, f32[4,64,128]{2,1,0:T(8,128)S(1)}, u32[]{:S(2)}, u32[]{:S(2)}) collective-permute-start(f32[4,64,128]{2,1,0:T(8,128)S(1)} %get-tuple-element.195), channel_id=1, source_target_pairs={{1,5},{5,1},{3,7},{7,3},{9,13},{13,9},{11,15},{15,11},{17,21},{21,... | collective-permute-start | bytes 393224 | tf_op jit(solution)/shard_map/ppermute | solution.py:486
  95.8 4.2 %collective-permute-start.24 = (f32[4,64,128]{2,1,0:T(8,128)S(1)}, f32[4,64,128]{2,1,0:T(8,128)S(1)}, u32[]{:S(2)}, u32[]{:S(2)}) collective-permute-start(f32[4,64,128]{2,1,0:T(8,128)S(1)} %get-tuple-element.199), channel_id=1, source_target_pairs={{0,1},{1,0},{2,3},{3,2},{4,5},{5,4},{6,7},{7,6},{8,9},{9,8},{10,11... | collective-permute-start | bytes 393224 | tf_op jit(solution)/shard_map/ppermute | solution.py:487
  98.4 1.7 %collective-permute-start.25 = (f32[4,64,128]{2,1,0:T(8,128)S(1)}, f32[4,64,128]{2,1,0:T(8,128)S(1)}, u32[]{:S(2)}, u32[]{:S(2)}) collective-permute-start(f32[4,64,128]{2,1,0:T(8,128)S(1)} %get-tuple-element.200), channel_id=1, source_target_pairs={{1,5},{5,1},{3,7},{7,3},{9,13},{13,9},{11,15},{15,11},{17,21},{21,... | collective-permute-start | bytes 393224 | tf_op jit(solution)/shard_map/ppermute | solution.py:486
  101.4 12.2 %collective-permute-start.26 = (f32[15,64,128]{2,1,0:T(8,128)S(1)}, f32[15,64,128]{2,1,0:T(8,128)S(1)}, u32[]{:S(2)}, u32[]{:S(2)}) collective-permute-start(f32[15,64,128]{2,1,0:T(8,128)S(1)} %get-tuple-element.203), channel_id=1, source_target_pairs={{0,8},{8,0},{16,24},{24,16},{1,9},{9,1},{17,25},{25,17},{2,10},{10... | collective-permute-start | bytes 1474568 | tf_op jit(solution)/shard_map/ppermute | solution.py:497
  103.2 10.4 %collective-permute-start.27 = (f32[15,64,128]{2,1,0:T(8,128)S(1)}, f32[15,64,128]{2,1,0:T(8,128)S(1)}, u32[]{:S(2)}, u32[]{:S(2)}) collective-permute-start(f32[15,64,128]{2,1,0:T(8,128)S(1)} %get-tuple-element.204), channel_id=1, source_target_pairs={{8,16},{16,8},{9,17},{17,9},{10,18},{18,10},{11,19},{19,11},{12,20... | collective-permute-start | bytes 1474568 | tf_op jit(solution)/shard_map/ppermute | solution.py:497
  110.1 7.1 %collective-permute-start.32 = (f32[16,32,128]{2,1,0:T(8,128)S(1)}, f32[16,32,128]{2,1,0:T(8,128)S(1)}, u32[]{:S(2)}, u32[]{:S(2)}) collective-permute-start(f32[16,32,128]{2,1,0:T(8,128)S(1)} %get-tuple-element.210), channel_id=1, source_target_pairs={{0,2},{2,0},{4,6},{6,4},{1,3},{3,1},{5,7},{7,5},{8,10},{10,8},{12,... | collective-permute-start | bytes 786440 | tf_op jit(solution)/shard_map/ppermute | solution.py:444
  111.4 7.2 %collective-permute-start.33 = (f32[16,32,128]{2,1,0:T(8,128)S(1)}, f32[16,32,128]{2,1,0:T(8,128)S(1)}, u32[]{:S(2)}, u32[]{:S(2)}) collective-permute-start(f32[16,32,128]{2,1,0:T(8,128)S(1)} %get-tuple-element.211), channel_id=1, source_target_pairs={{0,4},{2,6},{4,0},{6,2},{1,5},{3,7},{5,1},{7,3},{8,12},{10,14},{12... | collective-permute-start | bytes 786440 | tf_op jit(solution)/shard_map/ppermute | solution.py:444
  112.2 10.8 %collective-permute-start.34 = (f32[16,32,128]{2,1,0:T(8,128)S(1)}, f32[16,32,128]{2,1,0:T(8,128)S(1)}, u32[]{:S(2)}, u32[]{:S(2)}) collective-permute-start(f32[16,32,128]{2,1,0:T(8,128)S(1)} %get-tuple-element.212), channel_id=1, source_target_pairs={{0,6},{2,4},{4,2},{6,0},{1,7},{3,5},{5,3},{7,1},{8,14},{10,12},{12... | collective-permute-start | bytes 786440 | tf_op jit(solution)/shard_map/ppermute | solution.py:444
  115.1 14.4 %collective-permute-start.28 = (f32[16,32,128]{2,1,0:T(8,128)S(1)}, f32[16,32,128]{2,1,0:T(8,128)S(1)}, u32[]{:S(2)}, u32[]{:S(2)}) collective-permute-start(f32[16,32,128]{2,1,0:T(8,128)S(1)} %get-tuple-element.206), channel_id=1, source_target_pairs={{0,2},{2,0},{4,6},{6,4},{1,3},{3,1},{5,7},{7,5},{8,10},{10,8},{12,... | collective-permute-start | bytes 786440 | tf_op jit(solution)/shard_map/ppermute | solution.py:444
  116.5 14.9 %collective-permute-start.29 = (f32[16,32,128]{2,1,0:T(8,128)S(1)}, f32[16,32,128]{2,1,0:T(8,128)S(1)}, u32[]{:S(2)}, u32[]{:S(2)}) collective-permute-start(f32[16,32,128]{2,1,0:T(8,128)S(1)} %get-tuple-element.207), channel_id=1, source_target_pairs={{0,4},{2,6},{4,0},{6,2},{1,5},{3,7},{5,1},{7,3},{8,12},{10,14},{12... | collective-permute-start | bytes 786440 | tf_op jit(solution)/shard_map/ppermute | solution.py:444
  117.3 17.1 %collective-permute-start.30 = (f32[16,32,128]{2,1,0:T(8,128)S(1)}, f32[16,32,128]{2,1,0:T(8,128)S(1)}, u32[]{:S(2)}, u32[]{:S(2)}) collective-permute-start(f32[16,32,128]{2,1,0:T(8,128)S(1)} %get-tuple-element.208), channel_id=1, source_target_pairs={{0,6},{2,4},{4,2},{6,0},{1,7},{3,5},{5,3},{7,1},{8,14},{10,12},{12... | collective-permute-start | bytes 786440 | tf_op jit(solution)/shard_map/ppermute | solution.py:444
  123.7 14.3 %collective-permute-start.35 = (f32[4,16,16,128]{3,2,1,0:T(8,128)S(1)}, f32[4,16,16,128]{3,2,1,0:T(8,128)S(1)}, u32[]{:S(2)}, u32[]{:S(2)}) collective-permute-start(f32[4,16,16,128]{3,2,1,0:T(8,128)S(1)} %split_back.3), channel_id=1, source_target_pairs={{0,1},{1,0},{2,3},{3,2},{4,5},{5,4},{6,7},{7,6},{8,9},{9,8},{10,11... | collective-permute-start | bytes 1572872 | tf_op jit(solution)/shard_map/ppermute | solution.py:541
  134.9 4.6 %collective-permute-start.31 = (f32[4,16,16,128]{3,2,1,0:T(8,128)S(1)}, f32[4,16,16,128]{3,2,1,0:T(8,128)S(1)}, u32[]{:S(2)}, u32[]{:S(2)}) collective-permute-start(f32[4,16,16,128]{3,2,1,0:T(8,128)S(1)} %split_back.2), channel_id=1, source_target_pairs={{0,1},{1,0},{2,3},{3,2},{4,5},{5,4},{6,7},{7,6},{8,9},{9,8},{10,11... | collective-permute-start | bytes 1572872 | tf_op jit(solution)/shard_map/ppermute | solution.py:541

commit v4 on v3

--- a/solution.py
+++ b/solution.py
@@ -309,10 +309,7 @@
     return jnp.where(live != 0, estimate * correction, estimate)
 
 
-def inner_blur(me, cells, pair, after, outer, wz, wx, wh, wy, part, inner, body):
-    own_columns(cells, wz, wx, inner)
-    near_columns(inner, pair, after, wz, wh, inner)
-    quarter, depth = outer.shape[0] // 2, outer.shape[1]
+def blur_rows(wy, quarter, depth, outer, inner, pre, take):
     rows = 4 * quarter
     radius = wy.shape[0] // 2
 
@@ -325,11 +322,12 @@
 
     def tile(z):
         taps = [wy[i] for i in range(wy.shape[0])]
-        blurred = []
         for first in range(0, rows, quarter):
-            sums = [None] * quarter
+            sums = [None if pre is None else pre[first + o, z, :] for o in range(quarter)]
             for y in range(max(0, first - radius), min(rows, first + quarter + radius)):
                 ref, at = source(y)
+                if ref is None:
+                    continue
                 cell = ref[at, z, :]
                 for o in range(quarter):
                     i = y - (first + o) + radius
@@ -337,14 +335,34 @@
                         term = taps[i] * cell
                         sums[o] = term if sums[o] is None else sums[o] + term
             for o in range(quarter):
-                ref, at = source(first + o)
-                if ref is outer:
-                    part[at, z, :] = sums[o]
-                else:
-                    blurred.append(sums[o])
-        body(z, blurred)
+                take(first + o, z, jnp.zeros((8, LANES), F32) if sums[o] is None else sums[o])
 
     tiles(depth, tile)
+
+
+def ahead_kernel(outer, wy, pre):
+    def take(y, z, value):
+        pre[y, z, :] = value
+
+    blur_rows(wy, outer.shape[0] // 2, outer.shape[1], outer, None, None, take)
+
+
+def inner_blur(me, cells, pair, after, outer, pre, wz, wx, wh, wy, part, inner, body):
+    own_columns(cells, wz, wx, inner)
+    near_columns(inner, pair, after, wz, wh, inner)
+    quarter, depth = inner.shape[0] // 2, inner.shape[1]
+    blurred = []
+
+    def take(y, z, value):
+        if quarter <= y < 3 * quarter:
+            blurred.append(value)
+        else:
+            part[y if y < quarter else y - 2 * quarter, z, :] = value
+        if y == 4 * quarter - 1:
+            body(z, blurred)
+            blurred.clear()
+
+    blur_rows(wy, quarter, depth, outer, inner, pre, take)
 
 
 def outer_blur(me, part, recv_a, recv_b, wy, halo, body):
@@ -393,15 +411,16 @@
         pieces[e][...] = cells[slots(yl, rows), slots(zh, depth), :]
 
 
-def inner_kernel(rule, me, cells, pair, after, outer, wz, wx, wh, wy, base, live, part, out, to_pair, to_next, inner):
+def inner_kernel(first, rule, me, cells, pair, after, known, wz, wx, wh, wy, base, live, part, out, to_pair, to_next, inner):
     body = update(me, False, rule, base, live, out, (to_pair, to_next))
-    inner_blur(me, cells, pair, after, outer, wz, wx, wh, wy, part, inner, body)
+    outer, pre = (None, known) if first else (known, None)
+    inner_blur(me, cells, pair, after, outer, pre, wz, wx, wh, wy, part, inner, body)
 
 
 def last_inner_kernel(me, cells, pair, after, outer, wz, wx, wh, wy, base, live, part, *rest):
     pieces, inner, out = rest[:4], rest[4], rest[5]
     body = update(me, False, product, base, live, out, ())
-    inner_blur(me, cells, pair, after, outer, wz, wx, wh, wy, part, inner, body)
+    inner_blur(me, cells, pair, after, outer, None, wz, wx, wh, wy, part, inner, body)
     deal_out(me, out, pieces)
 
 
@@ -506,6 +525,8 @@
         beside = exchange(*strips[0]) if step else strips[0]
         outer, recv_a, recv_b, near = send_outer(cells[0], beside, w, near)
         if step == 0:
+            whole = shape((ny, nz, LANES))
+            outer = call(ahead_kernel, whole, [VMEM] * 2, us=0.3, name="ahead")(outer, w[3])
             inner_pieces, outer = lax.optimization_barrier((inner_pieces, outer))
             taken[1] = take(inner_pieces)
             estimate[1] = cells[1] = taken[1][0]
@@ -525,7 +546,7 @@
             continue
         rule = ratio if step % 2 == 0 else product
         part, inner, *inner_strips = call(
-            functools.partial(inner_kernel, rule), [half, half, strip, strip], [SMEM] + [VMEM] * 10, [room], us=3,
+            functools.partial(inner_kernel, step == 0, rule), [half, half, strip, strip], [SMEM] + [VMEM] * 10, [room], us=3,
             name="inner", mib=16,
         )(*ins)
         outer, *outer_strips = call(

time: 142 us -> 140 us (0.986)
  waiting for transfers between devices: 26 us -> 24.3 us
    ppermute x12, waiting for transfers between devices: 23.5 us -> 21.9 us  [trade(): lax.ppermute(pieces[e], ('yl', 'zh'), [(i, i ^ e) for i in range(4)])]
    pallas_call x3 -> x4, Pallas kernels: 19.8 us -> 19.7 us  [the longest x3 18 us: per_device(): call(functools.partial(inner_kernel, step == 0, rule), [half, half, strip...]
where the time goes in v4:
time: 140 us
  starting transfers between devices  60.3 us (43%)
  Pallas kernels  53.2 us (38%)
  waiting for transfers between devices  24.3 us (17%)
  local copies, waits for them, and re-layouts  1.69 us (1%)
    ppermute x12, waiting for transfers between devices, trade(): lax.ppermute(pieces[e], ('yl', 'zh'), [(i, i ^ e) for i in range(4)])  21.9 us
    pallas_call x3, Pallas kernels, per_device(): call(functools.partial(inner_kernel, step == 0, rule), [half, half, strip...  18 us
    ppermute x12, starting transfers between devices, trade(): lax.ppermute(pieces[e], ('yl', 'zh'), [(i, i ^ e) for i in range(4)])  17.3 us
    ppermute x6, starting transfers between devices, exchange(): return (lax.ppermute(to_pair, 'zl', swaps), after)  14.9 us
    ppermute x4, starting transfers between devices, send_outer(): lax.ppermute(send_a, 'yh', evens)  9.23 us
    ppermute x2, starting transfers between devices, back(): return (*pieces, lax.ppermute(sent, 'zl', swaps))  8.93 us
    pallas_call x1, Pallas kernels, per_device(): call(last_inner_kernel, [half] + [along] * 4, [SMEM] + [VMEM] * 10, [room...  6.17 us
    pallas_call x3, Pallas kernels, per_device(): call(functools.partial(final_kernel, rule), [half, strip, strip], [SMEM]...  5.46 us
  transfers between devices with their start and end apart: 36, of which 8 were waited for; matrix products, arithmetic and copies ran while one was open for 0% of the time, Pallas kernels for 32%

profile of v4, /device:TPU:0, one launch (start us, length us, event | category | flops | bytes accessed | tf_op | source)
XLA Modules:
  0.0 139.9 jit_solution(10464276309027916476)
XLA Ops:
  0.1 1.6 %copy-done = f32[2,32,16,512]{3,2,1,0:T(8,128)S(1)} copy-done((f32[2,32,16,512]{3,2,1,0:T(8,128)S(1)}, f32[2,32,16,512]{3,2,1,0:T(8,128)}, u32[]{:S(2)}) %copy-start) | copy-done | bytes 2097176
  1.7 2.5 %deal.1 = (f32[2,2,40,16,128]{4,3,2,1,0:T(8,128)S(1)}, f32[2,2,40,16,128]{4,3,2,1,0:T(8,128)S(1)}) custom-call(s32[5]{0:T(128)S(1)} %stack.23.me, f32[2,32,16,512]{3,2,1,0:T(8,128)S(1)} %copy-done), custom_call_target="tpu_custom_call" | custom-call | tf_op jit(solution)/shard_map/deal/pallas_call | solution.py:475
  4.7 2.6 %collective-permute-start.1 = (s32[4,32]{1,0:T(4,128)S(1)}, s32[4,32]{1,0:T(4,128)S(1)}, u32[]{:S(2)}, u32[]{:S(2)}) collective-permute-start(s32[4,32]{1,0:T(4,128)S(1)} %bitcast.6), channel_id=1, source_target_pairs={{0,4},{4,0},{1,5},{5,1},{2,6},{6,2},{3,7},{7,3},{8,12},{12,8},{9,1... | collective-permute-start | bytes 1544 | tf_op jit(solution)/shard_map/ppermute | solution.py:473
  7.3 0.7 mix.1
  8.1 0.8 collective-permute-done.1.theirs
  8.9 2.2 %collective-permute-start.5 = (f32[20,32,128]{2,1,0:T(8,128)S(1)}, f32[20,32,128]{2,1,0:T(8,128)S(1)}, u32[]{:S(2)}, u32[]{:S(2)}) collective-permute-start(f32[20,32,128]{2,1,0:T(8,128)S(1)} %get-tuple-element.124), channel_id=1, source_target_pairs={{0,2},{2,0},{4,6},{6,4},{1,3},{3,1},{5,7},{7,5},{8,10},{10,8},{12,... | collective-permute-start | bytes 983048 | tf_op jit(solution)/shard_map/ppermute | solution.py:463
  11.0 1.5 %collective-permute-start.6 = (f32[20,32,128]{2,1,0:T(8,128)S(1)}, f32[20,32,128]{2,1,0:T(8,128)S(1)}, u32[]{:S(2)}, u32[]{:S(2)}) collective-permute-start(f32[20,32,128]{2,1,0:T(8,128)S(1)} %get-tuple-element.125), channel_id=1, source_target_pairs={{0,4},{2,6},{4,0},{6,2},{1,5},{3,7},{5,1},{7,3},{8,12},{10,14},{12... | collective-permute-start | bytes 983048 | tf_op jit(solution)/shard_map/ppermute | solution.py:463
  12.6 1.9 %collective-permute-start.2 = (f32[20,32,128]{2,1,0:T(8,128)S(1)}, f32[20,32,128]{2,1,0:T(8,128)S(1)}, u32[]{:S(2)}, u32[]{:S(2)}) collective-permute-start(f32[20,32,128]{2,1,0:T(8,128)S(1)} %get-tuple-element.120), channel_id=1, source_target_pairs={{0,2},{2,0},{4,6},{6,4},{1,3},{3,1},{5,7},{7,5},{8,10},{10,8},{12,... | collective-permute-start | bytes 983048 | tf_op jit(solution)/shard_map/ppermute | solution.py:463
  14.5 1.5 %collective-permute-start.3 = (f32[20,32,128]{2,1,0:T(8,128)S(1)}, f32[20,32,128]{2,1,0:T(8,128)S(1)}, u32[]{:S(2)}, u32[]{:S(2)}) collective-permute-start(f32[20,32,128]{2,1,0:T(8,128)S(1)} %get-tuple-element.121), channel_id=1, source_target_pairs={{0,4},{2,6},{4,0},{6,2},{1,5},{3,7},{5,1},{7,3},{8,12},{10,14},{12... | collective-permute-start | bytes 983048 | tf_op jit(solution)/shard_map/ppermute | solution.py:463
  16.1 3.5 %collective-permute-done.5.rest_1_ = f32[20,32,128]{2,1,0:T(8,128)S(1)} collective-permute-done((f32[20,32,128]{2,1,0:T(8,128)S(1)}, f32[20,32,128]{2,1,0:T(8,128)S(1)}, u32[]{:S(2)}, u32[]{:S(2)}) %collective-permute-start.5) | collective-permute-done | bytes 327712 | tf_op jit(solution)/shard_map/ppermute | solution.py:463
  19.5 3.0 %collective-permute-start.4 = (f32[20,32,128]{2,1,0:T(8,128)S(1)}, f32[20,32,128]{2,1,0:T(8,128)S(1)}, u32[]{:S(2)}, u32[]{:S(2)}) collective-permute-start(f32[20,32,128]{2,1,0:T(8,128)S(1)} %get-tuple-element.122), channel_id=1, source_target_pairs={{0,6},{2,4},{4,2},{6,0},{1,7},{3,5},{5,3},{7,1},{8,14},{10,12},{12... | collective-permute-start | bytes 983048 | tf_op jit(solution)/shard_map/ppermute | solution.py:463
  22.6 2.2 %weights.1 = (bf16[256,256]{1,0:T(8,128)(2,1)S(1)}, bf16[256,256]{1,0:T(8,128)(2,1)S(1)}, bf16[256,512]{1,0:T(8,128)(2,1)S(1)}, f32[31,8,128]{2,1,0:T(8,128)S(1)...) custom-call(s32[5]{0:T(128)S(1)} %stack.23.me, ...), custom_call_target="tpu_custom_call" | custom-call | flops 1000000000 | tf_op jit(solution)/shard_map/weights/pallas_call | solution.py:491
  24.8 3.9 %collective-permute-done.6.rest_2_ = f32[20,32,128]{2,1,0:T(8,128)S(1)} collective-permute-done((f32[20,32,128]{2,1,0:T(8,128)S(1)}, f32[20,32,128]{2,1,0:T(8,128)S(1)}, u32[]{:S(2)}, u32[]{:S(2)}) %collective-permute-start.6) | collective-permute-done | bytes 327712 | tf_op jit(solution)/shard_map/ppermute | solution.py:463
  28.7 1.2 join.2
  29.9 1.0 own.4
  30.9 1.3 outer.4
  32.2 1.6 %collective-permute-start.8 = (f32[15,64,128]{2,1,0:T(8,128)S(1)}, f32[15,64,128]{2,1,0:T(8,128)S(1)}, u32[]{:S(2)}, u32[]{:S(2)}) collective-permute-start(f32[15,64,128]{2,1,0:T(8,128)S(1)} %get-tuple-element.161), channel_id=1, source_target_pairs={{0,8},{8,0},{16,24},{24,16},{1,9},{9,1},{17,25},{25,17},{2,10},{10... | collective-permute-start | bytes 1474568 | tf_op jit(solution)/shard_map/ppermute | solution.py:516
  33.9 0.7 collective-permute-start.9
  34.5 1.7 %ahead.1.known = f32[64,64,128]{2,1,0:T(8,128)S(1)} custom-call(f32[32,64,128]{2,1,0:T(8,128)S(1)} %get-tuple-element.148.outer, f32[31,8,128]{2,1,0:T(8,128)S(1)} %get-tuple-element.149.wy), custom_call_target="tpu_custom_call" | custom-call | flops 300000000 | tf_op jit(solution)/shard_map/ahead/pallas_call | solution.py:529
  36.2 5.4 %collective-permute-done.3.rest_2_ = f32[20,32,128]{2,1,0:T(8,128)S(1)} collective-permute-done((f32[20,32,128]{2,1,0:T(8,128)S(1)}, f32[20,32,128]{2,1,0:T(8,128)S(1)}, u32[]{:S(2)}, u32[]{:S(2)}) %collective-permute-start.3) | collective-permute-done | bytes 327712 | tf_op jit(solution)/shard_map/ppermute | solution.py:463
  41.6 1.2 join.3
  42.8 5.0 %inner.3 = (f32[32,64,128]{2,1,0:T(8,128)S(1)}, f32[32,64,128]{2,1,0:T(8,128)S(1)}, f32[4,64,128]{2,1,0:T(8,128)S(1)}, f32[4,64,128]{2,1,0:T(8,128)S(1)}) custom-call(s32[5]{0:T(128)S(1)} %stack.23.me, f32[32,64,128]{2,1,0:T(8,128)S(1)} %get-tuple-element.154.cells.base, f32[4,64,128]{2,1,0:T(8,128)S(1)} %get-tuple-element.155.pair, ...), custom_call_target="tpu_custom_call" | custom-call | flops 3000000000 | tf_op jit(solution)/shard_map/inner/pallas_call | solution.py:548
  47.8 0.7 collective-permute-start.11
  48.5 1.8 %final.3 = (f32[32,64,128]{2,1,0:T(8,128)S(1)}, f32[4,64,128]{2,1,0:T(8,128)S(1)}, f32[4,64,128]{2,1,0:T(8,128)S(1)}) custom-call(s32[5]{0:T(128)S(1)} %stack.23.me, f32[32,64,128]{2,1,0:T(8,128)S(1)} %get-tuple-element.160.part, f32[15,64,128]{2,1,0:T(8,128)S(1)} %collective-permute-done.8.recv_a, f32[15,64,128]{2,1,0:T(8,128)S(1)} %collective-permute-done.9.recv_b, ...), custom_call_target="tpu_custom_call" | custom-call | flops 2000000000 | tf_op jit(solution)/shard_map/final/pallas_call | solution.py:552
  50.4 3.0 %collective-permute-start.12 = (f32[4,64,128]{2,1,0:T(8,128)S(1)}, f32[4,64,128]{2,1,0:T(8,128)S(1)}, u32[]{:S(2)}, u32[]{:S(2)}) collective-permute-start(f32[4,64,128]{2,1,0:T(8,128)S(1)} %get-tuple-element.171), channel_id=1, source_target_pairs={{0,1},{1,0},{2,3},{3,2},{4,5},{5,4},{6,7},{7,6},{8,9},{9,8},{10,11... | collective-permute-start | bytes 393224 | tf_op jit(solution)/shard_map/ppermute | solution.py:506
  53.4 0.7 collective-permute-start.13
  54.1 1.0 own.5
  55.1 1.3 outer.5
  56.4 1.6 %collective-permute-start.14 = (f32[15,64,128]{2,1,0:T(8,128)S(1)}, f32[15,64,128]{2,1,0:T(8,128)S(1)}, u32[]{:S(2)}, u32[]{:S(2)}) collective-permute-start(f32[15,64,128]{2,1,0:T(8,128)S(1)} %get-tuple-element.178), channel_id=1, source_target_pairs={{0,8},{8,0},{16,24},{24,16},{1,9},{9,1},{17,25},{25,17},{2,10},{10... | collective-permute-start | bytes 1474568 | tf_op jit(solution)/shard_map/ppermute | solution.py:516
  58.1 0.7 collective-permute-start.15
  58.8 6.5 %inner.4 = (f32[32,64,128]{2,1,0:T(8,128)S(1)}, f32[32,64,128]{2,1,0:T(8,128)S(1)}, f32[4,64,128]{2,1,0:T(8,128)S(1)}, f32[4,64,128]{2,1,0:T(8,128)S(1)}) custom-call(s32[5]{0:T(128)S(1)} %stack.23.me, f32[32,64,128]{2,1,0:T(8,128)S(1)} %get-tuple-element.159.cells, f32[4,64,128]{2,1,0:T(8,128)S(1)} %collective-permute-done.10.pair, ...), custom_call_target="tpu_custom_call" | custom-call | flops 3000000000 | tf_op jit(solution)/shard_map/inner/pallas_call | solution.py:548
  65.3 3.8 %collective-permute-start.16 = (f32[4,64,128]{2,1,0:T(8,128)S(1)}, f32[4,64,128]{2,1,0:T(8,128)S(1)}, u32[]{:S(2)}, u32[]{:S(2)}) collective-permute-start(f32[4,64,128]{2,1,0:T(8,128)S(1)} %get-tuple-element.181), channel_id=1, source_target_pairs={{0,1},{1,0},{2,3},{3,2},{4,5},{5,4},{6,7},{7,6},{8,9},{9,8},{10,11... | collective-permute-start | bytes 393224 | tf_op jit(solution)/shard_map/ppermute | solution.py:506
  69.1 0.8 collective-permute-start.17
  70.0 1.8 %final.4 = (f32[32,64,128]{2,1,0:T(8,128)S(1)}, f32[4,64,128]{2,1,0:T(8,128)S(1)}, f32[4,64,128]{2,1,0:T(8,128)S(1)}) custom-call(s32[5]{0:T(128)S(1)} %stack.23.me, f32[32,64,128]{2,1,0:T(8,128)S(1)} %get-tuple-element.177.part, f32[15,64,128]{2,1,0:T(8,128)S(1)} %collective-permute-done.14.recv_a, f32[15,64,128]{2,1,0:T(8,128)S(1)} %collective-permute-done.15.recv_b, ...), custom_call_target="tpu_custom_call" | custom-call | flops 2000000000 | tf_op jit(solution)/shard_map/final/pallas_call | solution.py:552
  71.7 1.6 %collective-permute-start.18 = (f32[4,64,128]{2,1,0:T(8,128)S(1)}, f32[4,64,128]{2,1,0:T(8,128)S(1)}, u32[]{:S(2)}, u32[]{:S(2)}) collective-permute-start(f32[4,64,128]{2,1,0:T(8,128)S(1)} %get-tuple-element.186), channel_id=1, source_target_pairs={{0,1},{1,0},{2,3},{3,2},{4,5},{5,4},{6,7},{7,6},{8,9},{9,8},{10,11... | collective-permute-start | bytes 393224 | tf_op jit(solution)/shard_map/ppermute | solution.py:506
  73.3 0.7 collective-permute-start.19
  74.0 1.0 own.6
  75.0 1.3 outer.6
  76.3 4.2 %collective-permute-start.20 = (f32[15,64,128]{2,1,0:T(8,128)S(1)}, f32[15,64,128]{2,1,0:T(8,128)S(1)}, u32[]{:S(2)}, u32[]{:S(2)}) collective-permute-start(f32[15,64,128]{2,1,0:T(8,128)S(1)} %get-tuple-element.191), channel_id=1, source_target_pairs={{0,8},{8,0},{16,24},{24,16},{1,9},{9,1},{17,25},{25,17},{2,10},{10... | collective-permute-start | bytes 1474568 | tf_op jit(solution)/shard_map/ppermute | solution.py:516
  80.5 0.7 collective-permute-start.21
  81.2 6.6 %inner.5 = (f32[32,64,128]{2,1,0:T(8,128)S(1)}, f32[32,64,128]{2,1,0:T(8,128)S(1)}, f32[4,64,128]{2,1,0:T(8,128)S(1)}, f32[4,64,128]{2,1,0:T(8,128)S(1)}) custom-call(s32[5]{0:T(128)S(1)} %stack.23.me, f32[32,64,128]{2,1,0:T(8,128)S(1)} %get-tuple-element.176.cells.base, f32[4,64,128]{2,1,0:T(8,128)S(1)} %collective-permute-done.16.pair, ...), custom_call_target="tpu_custom_call" | custom-call | flops 3000000000 | tf_op jit(solution)/shard_map/inner/pallas_call | solution.py:548
  87.7 3.8 %collective-permute-start.22 = (f32[4,64,128]{2,1,0:T(8,128)S(1)}, f32[4,64,128]{2,1,0:T(8,128)S(1)}, u32[]{:S(2)}, u32[]{:S(2)}) collective-permute-start(f32[4,64,128]{2,1,0:T(8,128)S(1)} %get-tuple-element.194), channel_id=1, source_target_pairs={{0,1},{1,0},{2,3},{3,2},{4,5},{5,4},{6,7},{7,6},{8,9},{9,8},{10,11... | collective-permute-start | bytes 393224 | tf_op jit(solution)/shard_map/ppermute | solution.py:506
  91.6 0.7 collective-permute-start.23
  92.3 1.8 %final.5 = (f32[32,64,128]{2,1,0:T(8,128)S(1)}, f32[4,64,128]{2,1,0:T(8,128)S(1)}, f32[4,64,128]{2,1,0:T(8,128)S(1)}) custom-call(s32[5]{0:T(128)S(1)} %stack.23.me, f32[32,64,128]{2,1,0:T(8,128)S(1)} %get-tuple-element.190.part, f32[15,64,128]{2,1,0:T(8,128)S(1)} %collective-permute-done.20.recv_a, f32[15,64,128]{2,1,0:T(8,128)S(1)} %collective-permute-done.21.recv_b, ...), custom_call_target="tpu_custom_call" | custom-call | flops 2000000000 | tf_op jit(solution)/shard_map/final/pallas_call | solution.py:552
  94.1 2.6 %collective-permute-start.24 = (f32[4,64,128]{2,1,0:T(8,128)S(1)}, f32[4,64,128]{2,1,0:T(8,128)S(1)}, u32[]{:S(2)}, u32[]{:S(2)}) collective-permute-start(f32[4,64,128]{2,1,0:T(8,128)S(1)} %get-tuple-element.199), channel_id=1, source_target_pairs={{0,1},{1,0},{2,3},{3,2},{4,5},{5,4},{6,7},{7,6},{8,9},{9,8},{10,11... | collective-permute-start | bytes 393224 | tf_op jit(solution)/shard_map/ppermute | solution.py:506
  97.4 1.0 own.7
  98.4 1.3 outer.7
  99.7 1.8 %collective-permute-start.26 = (f32[15,64,128]{2,1,0:T(8,128)S(1)}, f32[15,64,128]{2,1,0:T(8,128)S(1)}, u32[]{:S(2)}, u32[]{:S(2)}) collective-permute-start(f32[15,64,128]{2,1,0:T(8,128)S(1)} %get-tuple-element.203), channel_id=1, source_target_pairs={{0,8},{8,0},{16,24},{24,16},{1,9},{9,1},{17,25},{25,17},{2,10},{10... | collective-permute-start | bytes 1474568 | tf_op jit(solution)/shard_map/ppermute | solution.py:516
  101.5 0.7 collective-permute-start.27
  102.2 6.2 %last_inner.1 = (f32[32,64,128]{2,1,0:T(8,128)S(1)}, f32[16,32,128]{2,1,0:T(8,128)S(1)}, f32[16,32,128]{2,1,0:T(8,128)S(1)}, f32[16,32,128]{2,1,0:T(8,128)S(1)}, f32[16,32,128]{2,1,0:T(8,128)S(1)}) custom-call(s32[5]{0:T(128)S(1)} %stack.23.me, f32[32,64,128]{2,1,0:T(8,128)S(1)} %get-tuple-element.189.cells, f32[4,64,128]{2,1,0:T(8,128)S(1)} %collective-permute-done.22.pair, ...), custom_call_target="tpu_custom_call" | custom-call | flops 3000000000 | tf_op jit(solution)/shard_map/last_inner/pallas_call | solution.py:537
  108.3 1.4 collective-permute-start.32
  109.7 0.8 collective-permute-start.33
  110.5 1.4 %collective-permute-start.34 = (f32[16,32,128]{2,1,0:T(8,128)S(1)}, f32[16,32,128]{2,1,0:T(8,128)S(1)}, u32[]{:S(2)}, u32[]{:S(2)}) collective-permute-start(f32[16,32,128]{2,1,0:T(8,128)S(1)} %get-tuple-element.212), channel_id=1, source_target_pairs={{0,6},{2,4},{4,2},{6,0},{1,7},{3,5},{5,3},{7,1},{8,14},{10,12},{12... | collective-permute-start | bytes 786440 | tf_op jit(solution)/shard_map/ppermute | solution.py:463
  111.9 1.4 %last.1 = (f32[16,32,128]{2,1,0:T(8,128)S(1)}, f32[16,32,128]{2,1,0:T(8,128)S(1)}, f32[16,32,128]{2,1,0:T(8,128)S(1)}, f32[16,32,128]{2,1,0:T(8,128)S(1)}) custom-call(s32[5]{0:T(128)S(1)} %stack.23.me, f32[32,64,128]{2,1,0:T(8,128)S(1)} %get-tuple-element.202.part, f32[15,64,128]{2,1,0:T(8,128)S(1)} %collective-permute-done.26.recv_a, ...), custom_call_target="tpu_custom_call" | custom-call | flops 2000000000 | tf_op jit(solution)/shard_map/last/pallas_call | solution.py:542
  113.4 1.4 collective-permute-start.28
  114.7 0.8 collective-permute-start.29
  115.5 1.4 %collective-permute-start.30 = (f32[16,32,128]{2,1,0:T(8,128)S(1)}, f32[16,32,128]{2,1,0:T(8,128)S(1)}, u32[]{:S(2)}, u32[]{:S(2)}) collective-permute-start(f32[16,32,128]{2,1,0:T(8,128)S(1)} %get-tuple-element.208), channel_id=1, source_target_pairs={{0,6},{2,4},{4,2},{6,0},{1,7},{3,5},{5,3},{7,1},{8,14},{10,12},{12... | collective-permute-start | bytes 786440 | tf_op jit(solution)/shard_map/ppermute | solution.py:463
  116.9 4.4 %collective-permute-done.34.rest_3_.rest_8_ = f32[16,32,128]{2,1,0:T(8,128)S(1)} collective-permute-done((f32[16,32,128]{2,1,0:T(8,128)S(1)}, f32[16,32,128]{2,1,0:T(8,128)S(1)}, u32[]{:S(2)}, u32[]{:S(2)}) %collective-permute-start.34) | collective-permute-done | bytes 262176 | tf_op jit(solution)/shard_map/ppermute | solution.py:463
  121.9 5.9 %collective-permute-start.35 = (f32[4,16,16,128]{3,2,1,0:T(8,128)S(1)}, f32[4,16,16,128]{3,2,1,0:T(8,128)S(1)}, u32[]{:S(2)}, u32[]{:S(2)}) collective-permute-start(f32[4,16,16,128]{3,2,1,0:T(8,128)S(1)} %split_back.3), channel_id=1, source_target_pairs={{0,1},{1,0},{2,3},{3,2},{4,5},{5,4},{6,7},{7,6},{8,9},{9,8},{10,11... | collective-permute-start | bytes 1572872 | tf_op jit(solution)/shard_map/ppermute | solution.py:562
  127.8 1.9 %collective-permute-done.29.rest_2_ = f32[16,32,128]{2,1,0:T(8,128)S(1)} collective-permute-done((f32[16,32,128]{2,1,0:T(8,128)S(1)}, f32[16,32,128]{2,1,0:T(8,128)S(1)}, u32[]{:S(2)}, u32[]{:S(2)}) %collective-permute-start.29) | collective-permute-done | bytes 262176 | tf_op jit(solution)/shard_map/ppermute | solution.py:463
  129.6 2.9 %collective-permute-done.30.rest_3_ = f32[16,32,128]{2,1,0:T(8,128)S(1)} collective-permute-done((f32[16,32,128]{2,1,0:T(8,128)S(1)}, f32[16,32,128]{2,1,0:T(8,128)S(1)}, u32[]{:S(2)}, u32[]{:S(2)}) %collective-permute-start.30) | collective-permute-done | bytes 262176 | tf_op jit(solution)/shard_map/ppermute | solution.py:463
  133.1 3.1 %collective-permute-start.31 = (f32[4,16,16,128]{3,2,1,0:T(8,128)S(1)}, f32[4,16,16,128]{3,2,1,0:T(8,128)S(1)}, u32[]{:S(2)}, u32[]{:S(2)}) collective-permute-start(f32[4,16,16,128]{3,2,1,0:T(8,128)S(1)} %split_back.2), channel_id=1, source_target_pairs={{0,1},{1,0},{2,3},{3,2},{4,5},{5,4},{6,7},{7,6},{8,9},{9,8},{10,11... | collective-permute-start | bytes 1572872 | tf_op jit(solution)/shard_map/ppermute | solution.py:562
  136.2 1.5 %collective-permute-done.31.rest_4_ = f32[4,16,16,128]{3,2,1,0:T(8,128)S(1)} collective-permute-done((f32[4,16,16,128]{3,2,1,0:T(8,128)S(1)}, f32[4,16,16,128]{3,2,1,0:T(8,128)S(1)}, u32[]{:S(2)}, u32[]{:S(2)}) %collective-permute-start.31) | collective-permute-done | bytes 524320 | tf_op jit(solution)/shard_map/ppermute | solution.py:562
  137.7 2.1 %gather.1 = f32[2,32,16,512]{3,2,1,0:T(8,128)} custom-call(s32[5]{0:T(128)S(1)} %stack.23.me, f32[16,32,128]{2,1,0:T(8,128)S(1)} %get-tuple-element.205.rest_0_, f32[16,32,128]{2,1,0:T(8,128)S(1)} %collective-permute-done.28.rest_1_, f32[16,32,128]{2,1,0:T(8,128)S(1)} %collective-permute-done.29.rest_2_, f32[16,32,128]{2,1,0:T(8,128)S(1)} %collective-permute-done.30.rest_3_, ...), custom_call_target="tpu_custom_call" | custom-call | flops 2000000000 | tf_op jit(solution)/shard_map/gather/pallas_call | solution.py:564
  (44 shorter events, 2.6 us)
Async XLA Ops:
  0.0 4.7 %copy-start.1 = (s32[1,4,32]{2,1,0:T(4,128)S(1)}, s32[1,4,32]{2,1,0:T(4,128)}, u32[]{:S(2)}) copy-start(s32[1,4,32]{2,1,0:T(4,128)} %param.9) | copy-start | bytes 1540
  0.1 1.6 %copy-start = (f32[2,32,16,512]{3,2,1,0:T(8,128)S(1)}, f32[2,32,16,512]{3,2,1,0:T(8,128)}, u32[]{:S(2)}) copy-start(f32[2,32,16,512]{3,2,1,0:T(8,128)} %observed.1) | copy-start | bytes 6291460
  1.7 20.9 %copy-start.2 = (f32[2,31]{1,0:T(2,128)S(1)}, f32[2,31]{1,0:T(2,128)}, u32[]{:S(2)}) copy-start(f32[2,31]{1,0:T(2,128)} %rows.1) | copy-start | bytes 748
  1.7 20.9 %copy-start.3 = (f32[2,31]{1,0:T(2,128)S(1)}, f32[2,31]{1,0:T(2,128)}, u32[]{:S(2)}) copy-start(f32[2,31]{1,0:T(2,128)} %columns.1) | copy-start | bytes 748
  1.7 20.9 %copy-start.4 = (f32[2,101]{1,0:T(2,128)S(1)}, f32[2,101]{1,0:T(2,128)}, u32[]{:S(2)}) copy-start(f32[2,101]{1,0:T(2,128)} %axial.1) | copy-start | bytes 2428
  4.2 3.2 %collective-permute-start = (f32[2,2,40,16,128]{4,3,2,1,0:T(8,128)S(1)}, f32[2,2,40,16,128]{4,3,2,1,0:T(8,128)S(1)}, u32[]{:S(2)}, u32[]{:S(2)}) collective-permute-start(f32[2,2,40,16,128]{4,3,2,1,0:T(8,128)S(1)} %get-tuple-element.110), channel_id=1, source_target_pairs={{0,1},{1,0},{2,3},{3,2},{4,5},{5,4},{6,7},{7,6},{8,9},{9,8},{10,11... | collective-permute-start | bytes 3932168 | tf_op jit(solution)/shard_map/ppermute | solution.py:476
  4.7 4.2 %collective-permute-start.1 = (s32[4,32]{1,0:T(4,128)S(1)}, s32[4,32]{1,0:T(4,128)S(1)}, u32[]{:S(2)}, u32[]{:S(2)}) collective-permute-start(s32[4,32]{1,0:T(4,128)S(1)} %bitcast.6), channel_id=1, source_target_pairs={{0,4},{4,0},{1,5},{5,1},{2,6},{6,2},{3,7},{7,3},{8,12},{12,8},{9,1... | collective-permute-start | bytes 1544 | tf_op jit(solution)/shard_map/ppermute | solution.py:473
  8.9 10.7 %collective-permute-start.5 = (f32[20,32,128]{2,1,0:T(8,128)S(1)}, f32[20,32,128]{2,1,0:T(8,128)S(1)}, u32[]{:S(2)}, u32[]{:S(2)}) collective-permute-start(f32[20,32,128]{2,1,0:T(8,128)S(1)} %get-tuple-element.124), channel_id=1, source_target_pairs={{0,2},{2,0},{4,6},{6,4},{1,3},{3,1},{5,7},{7,5},{8,10},{10,8},{12,... | collective-permute-start | bytes 983048 | tf_op jit(solution)/shard_map/ppermute | solution.py:463
  11.0 17.6 %collective-permute-start.6 = (f32[20,32,128]{2,1,0:T(8,128)S(1)}, f32[20,32,128]{2,1,0:T(8,128)S(1)}, u32[]{:S(2)}, u32[]{:S(2)}) collective-permute-start(f32[20,32,128]{2,1,0:T(8,128)S(1)} %get-tuple-element.125), channel_id=1, source_target_pairs={{0,4},{2,6},{4,0},{6,2},{1,5},{3,7},{5,1},{7,3},{8,12},{10,14},{12... | collective-permute-start | bytes 983048 | tf_op jit(solution)/shard_map/ppermute | solution.py:463
  12.6 16.1 %collective-permute-start.7 = (f32[20,32,128]{2,1,0:T(8,128)S(1)}, f32[20,32,128]{2,1,0:T(8,128)S(1)}, u32[]{:S(2)}, u32[]{:S(2)}) collective-permute-start(f32[20,32,128]{2,1,0:T(8,128)S(1)} %get-tuple-element.126), channel_id=1, source_target_pairs={{0,6},{2,4},{4,2},{6,0},{1,7},{3,5},{5,3},{7,1},{8,14},{10,12},{12... | collective-permute-start | bytes 983048 | tf_op jit(solution)/shard_map/ppermute | solution.py:463
  12.6 23.6 %collective-permute-start.2 = (f32[20,32,128]{2,1,0:T(8,128)S(1)}, f32[20,32,128]{2,1,0:T(8,128)S(1)}, u32[]{:S(2)}, u32[]{:S(2)}) collective-permute-start(f32[20,32,128]{2,1,0:T(8,128)S(1)} %get-tuple-element.120), channel_id=1, source_target_pairs={{0,2},{2,0},{4,6},{6,4},{1,3},{3,1},{5,7},{7,5},{8,10},{10,8},{12,... | collective-permute-start | bytes 983048 | tf_op jit(solution)/shard_map/ppermute | solution.py:463
  14.5 27.1 %collective-permute-start.3 = (f32[20,32,128]{2,1,0:T(8,128)S(1)}, f32[20,32,128]{2,1,0:T(8,128)S(1)}, u32[]{:S(2)}, u32[]{:S(2)}) collective-permute-start(f32[20,32,128]{2,1,0:T(8,128)S(1)} %get-tuple-element.121), channel_id=1, source_target_pairs={{0,4},{2,6},{4,0},{6,2},{1,5},{3,7},{5,1},{7,3},{8,12},{10,14},{12... | collective-permute-start | bytes 983048 | tf_op jit(solution)/shard_map/ppermute | solution.py:463
  19.5 22.0 %collective-permute-start.4 = (f32[20,32,128]{2,1,0:T(8,128)S(1)}, f32[20,32,128]{2,1,0:T(8,128)S(1)}, u32[]{:S(2)}, u32[]{:S(2)}) collective-permute-start(f32[20,32,128]{2,1,0:T(8,128)S(1)} %get-tuple-element.122), channel_id=1, source_target_pairs={{0,6},{2,4},{4,2},{6,0},{1,7},{3,5},{5,3},{7,1},{8,14},{10,12},{12... | collective-permute-start | bytes 983048 | tf_op jit(solution)/shard_map/ppermute | solution.py:463
  32.2 16.3 %collective-permute-start.8 = (f32[15,64,128]{2,1,0:T(8,128)S(1)}, f32[15,64,128]{2,1,0:T(8,128)S(1)}, u32[]{:S(2)}, u32[]{:S(2)}) collective-permute-start(f32[15,64,128]{2,1,0:T(8,128)S(1)} %get-tuple-element.161), channel_id=1, source_target_pairs={{0,8},{8,0},{16,24},{24,16},{1,9},{9,1},{17,25},{25,17},{2,10},{10... | collective-permute-start | bytes 1474568 | tf_op jit(solution)/shard_map/ppermute | solution.py:516
  33.9 14.7 %collective-permute-start.9 = (f32[15,64,128]{2,1,0:T(8,128)S(1)}, f32[15,64,128]{2,1,0:T(8,128)S(1)}, u32[]{:S(2)}, u32[]{:S(2)}) collective-permute-start(f32[15,64,128]{2,1,0:T(8,128)S(1)} %get-tuple-element.162), channel_id=1, source_target_pairs={{8,16},{16,8},{9,17},{17,9},{10,18},{18,10},{11,19},{19,11},{12,20... | collective-permute-start | bytes 1474568 | tf_op jit(solution)/shard_map/ppermute | solution.py:516
  47.8 6.3 %collective-permute-start.10 = (f32[4,64,128]{2,1,0:T(8,128)S(1)}, f32[4,64,128]{2,1,0:T(8,128)S(1)}, u32[]{:S(2)}, u32[]{:S(2)}) collective-permute-start(f32[4,64,128]{2,1,0:T(8,128)S(1)} %get-tuple-element.164), channel_id=1, source_target_pairs={{0,1},{1,0},{2,3},{3,2},{4,5},{5,4},{6,7},{7,6},{8,9},{9,8},{10,11... | collective-permute-start | bytes 393224 | tf_op jit(solution)/shard_map/ppermute | solution.py:506
  47.8 6.2 %collective-permute-start.11 = (f32[4,64,128]{2,1,0:T(8,128)S(1)}, f32[4,64,128]{2,1,0:T(8,128)S(1)}, u32[]{:S(2)}, u32[]{:S(2)}) collective-permute-start(f32[4,64,128]{2,1,0:T(8,128)S(1)} %get-tuple-element.165), channel_id=1, source_target_pairs={{1,5},{5,1},{3,7},{7,3},{9,13},{13,9},{11,15},{15,11},{17,21},{21,... | collective-permute-start | bytes 393224 | tf_op jit(solution)/shard_map/ppermute | solution.py:505
  50.4 4.7 %collective-permute-start.12 = (f32[4,64,128]{2,1,0:T(8,128)S(1)}, f32[4,64,128]{2,1,0:T(8,128)S(1)}, u32[]{:S(2)}, u32[]{:S(2)}) collective-permute-start(f32[4,64,128]{2,1,0:T(8,128)S(1)} %get-tuple-element.171), channel_id=1, source_target_pairs={{0,1},{1,0},{2,3},{3,2},{4,5},{5,4},{6,7},{7,6},{8,9},{9,8},{10,11... | collective-permute-start | bytes 393224 | tf_op jit(solution)/shard_map/ppermute | solution.py:506
  53.4 1.7 %collective-permute-start.13 = (f32[4,64,128]{2,1,0:T(8,128)S(1)}, f32[4,64,128]{2,1,0:T(8,128)S(1)}, u32[]{:S(2)}, u32[]{:S(2)}) collective-permute-start(f32[4,64,128]{2,1,0:T(8,128)S(1)} %get-tuple-element.172), channel_id=1, source_target_pairs={{1,5},{5,1},{3,7},{7,3},{9,13},{13,9},{11,15},{15,11},{17,21},{21,... | collective-permute-start | bytes 393224 | tf_op jit(solution)/shard_map/ppermute | solution.py:505
  56.4 13.5 %collective-permute-start.14 = (f32[15,64,128]{2,1,0:T(8,128)S(1)}, f32[15,64,128]{2,1,0:T(8,128)S(1)}, u32[]{:S(2)}, u32[]{:S(2)}) collective-permute-start(f32[15,64,128]{2,1,0:T(8,128)S(1)} %get-tuple-element.178), channel_id=1, source_target_pairs={{0,8},{8,0},{16,24},{24,16},{1,9},{9,1},{17,25},{25,17},{2,10},{10... | collective-permute-start | bytes 1474568 | tf_op jit(solution)/shard_map/ppermute | solution.py:516
  58.1 11.9 %collective-permute-start.15 = (f32[15,64,128]{2,1,0:T(8,128)S(1)}, f32[15,64,128]{2,1,0:T(8,128)S(1)}, u32[]{:S(2)}, u32[]{:S(2)}) collective-permute-start(f32[15,64,128]{2,1,0:T(8,128)S(1)} %get-tuple-element.179), channel_id=1, source_target_pairs={{8,16},{16,8},{9,17},{17,9},{10,18},{18,10},{11,19},{19,11},{12,20... | collective-permute-start | bytes 1474568 | tf_op jit(solution)/shard_map/ppermute | solution.py:516
  65.3 8.7 %collective-permute-start.16 = (f32[4,64,128]{2,1,0:T(8,128)S(1)}, f32[4,64,128]{2,1,0:T(8,128)S(1)}, u32[]{:S(2)}, u32[]{:S(2)}) collective-permute-start(f32[4,64,128]{2,1,0:T(8,128)S(1)} %get-tuple-element.181), channel_id=1, source_target_pairs={{0,1},{1,0},{2,3},{3,2},{4,5},{5,4},{6,7},{7,6},{8,9},{9,8},{10,11... | collective-permute-start | bytes 393224 | tf_op jit(solution)/shard_map/ppermute | solution.py:506
  69.1 4.9 %collective-permute-start.17 = (f32[4,64,128]{2,1,0:T(8,128)S(1)}, f32[4,64,128]{2,1,0:T(8,128)S(1)}, u32[]{:S(2)}, u32[]{:S(2)}) collective-permute-start(f32[4,64,128]{2,1,0:T(8,128)S(1)} %get-tuple-element.182), channel_id=1, source_target_pairs={{1,5},{5,1},{3,7},{7,3},{9,13},{13,9},{11,15},{15,11},{17,21},{21,... | collective-permute-start | bytes 393224 | tf_op jit(solution)/shard_map/ppermute | solution.py:505
  71.7 3.2 %collective-permute-start.18 = (f32[4,64,128]{2,1,0:T(8,128)S(1)}, f32[4,64,128]{2,1,0:T(8,128)S(1)}, u32[]{:S(2)}, u32[]{:S(2)}) collective-permute-start(f32[4,64,128]{2,1,0:T(8,128)S(1)} %get-tuple-element.186), channel_id=1, source_target_pairs={{0,1},{1,0},{2,3},{3,2},{4,5},{5,4},{6,7},{7,6},{8,9},{9,8},{10,11... | collective-permute-start | bytes 393224 | tf_op jit(solution)/shard_map/ppermute | solution.py:506
  73.3 1.7 %collective-permute-start.19 = (f32[4,64,128]{2,1,0:T(8,128)S(1)}, f32[4,64,128]{2,1,0:T(8,128)S(1)}, u32[]{:S(2)}, u32[]{:S(2)}) collective-permute-start(f32[4,64,128]{2,1,0:T(8,128)S(1)} %get-tuple-element.187), channel_id=1, source_target_pairs={{1,5},{5,1},{3,7},{7,3},{9,13},{13,9},{11,15},{15,11},{17,21},{21,... | collective-permute-start | bytes 393224 | tf_op jit(solution)/shard_map/ppermute | solution.py:505
  76.3 15.9 %collective-permute-start.20 = (f32[15,64,128]{2,1,0:T(8,128)S(1)}, f32[15,64,128]{2,1,0:T(8,128)S(1)}, u32[]{:S(2)}, u32[]{:S(2)}) collective-permute-start(f32[15,64,128]{2,1,0:T(8,128)S(1)} %get-tuple-element.191), channel_id=1, source_target_pairs={{0,8},{8,0},{16,24},{24,16},{1,9},{9,1},{17,25},{25,17},{2,10},{10... | collective-permute-start | bytes 1474568 | tf_op jit(solution)/shard_map/ppermute | solution.py:516
  80.5 11.8 %collective-permute-start.21 = (f32[15,64,128]{2,1,0:T(8,128)S(1)}, f32[15,64,128]{2,1,0:T(8,128)S(1)}, u32[]{:S(2)}, u32[]{:S(2)}) collective-permute-start(f32[15,64,128]{2,1,0:T(8,128)S(1)} %get-tuple-element.192), channel_id=1, source_target_pairs={{8,16},{16,8},{9,17},{17,9},{10,18},{18,10},{11,19},{19,11},{12,20... | collective-permute-start | bytes 1474568 | tf_op jit(solution)/shard_map/ppermute | solution.py:516
  87.7 9.6 %collective-permute-start.22 = (f32[4,64,128]{2,1,0:T(8,128)S(1)}, f32[4,64,128]{2,1,0:T(8,128)S(1)}, u32[]{:S(2)}, u32[]{:S(2)}) collective-permute-start(f32[4,64,128]{2,1,0:T(8,128)S(1)} %get-tuple-element.194), channel_id=1, source_target_pairs={{0,1},{1,0},{2,3},{3,2},{4,5},{5,4},{6,7},{7,6},{8,9},{9,8},{10,11... | collective-permute-start | bytes 393224 | tf_op jit(solution)/shard_map/ppermute | solution.py:506
  91.6 5.8 %collective-permute-start.23 = (f32[4,64,128]{2,1,0:T(8,128)S(1)}, f32[4,64,128]{2,1,0:T(8,128)S(1)}, u32[]{:S(2)}, u32[]{:S(2)}) collective-permute-start(f32[4,64,128]{2,1,0:T(8,128)S(1)} %get-tuple-element.195), channel_id=1, source_target_pairs={{1,5},{5,1},{3,7},{7,3},{9,13},{13,9},{11,15},{15,11},{17,21},{21,... | collective-permute-start | bytes 393224 | tf_op jit(solution)/shard_map/ppermute | solution.py:505
  94.1 4.2 %collective-permute-start.24 = (f32[4,64,128]{2,1,0:T(8,128)S(1)}, f32[4,64,128]{2,1,0:T(8,128)S(1)}, u32[]{:S(2)}, u32[]{:S(2)}) collective-permute-start(f32[4,64,128]{2,1,0:T(8,128)S(1)} %get-tuple-element.199), channel_id=1, source_target_pairs={{0,1},{1,0},{2,3},{3,2},{4,5},{5,4},{6,7},{7,6},{8,9},{9,8},{10,11... | collective-permute-start | bytes 393224 | tf_op jit(solution)/shard_map/ppermute | solution.py:506
  96.7 1.7 %collective-permute-start.25 = (f32[4,64,128]{2,1,0:T(8,128)S(1)}, f32[4,64,128]{2,1,0:T(8,128)S(1)}, u32[]{:S(2)}, u32[]{:S(2)}) collective-permute-start(f32[4,64,128]{2,1,0:T(8,128)S(1)} %get-tuple-element.200), channel_id=1, source_target_pairs={{1,5},{5,1},{3,7},{7,3},{9,13},{13,9},{11,15},{15,11},{17,21},{21,... | collective-permute-start | bytes 393224 | tf_op jit(solution)/shard_map/ppermute | solution.py:505
  99.7 12.2 %collective-permute-start.26 = (f32[15,64,128]{2,1,0:T(8,128)S(1)}, f32[15,64,128]{2,1,0:T(8,128)S(1)}, u32[]{:S(2)}, u32[]{:S(2)}) collective-permute-start(f32[15,64,128]{2,1,0:T(8,128)S(1)} %get-tuple-element.203), channel_id=1, source_target_pairs={{0,8},{8,0},{16,24},{24,16},{1,9},{9,1},{17,25},{25,17},{2,10},{10... | collective-permute-start | bytes 1474568 | tf_op jit(solution)/shard_map/ppermute | solution.py:516
  101.5 10.4 %collective-permute-start.27 = (f32[15,64,128]{2,1,0:T(8,128)S(1)}, f32[15,64,128]{2,1,0:T(8,128)S(1)}, u32[]{:S(2)}, u32[]{:S(2)}) collective-permute-start(f32[15,64,128]{2,1,0:T(8,128)S(1)} %get-tuple-element.204), channel_id=1, source_target_pairs={{8,16},{16,8},{9,17},{17,9},{10,18},{18,10},{11,19},{19,11},{12,20... | collective-permute-start | bytes 1474568 | tf_op jit(solution)/shard_map/ppermute | solution.py:516
  108.3 7.1 %collective-permute-start.32 = (f32[16,32,128]{2,1,0:T(8,128)S(1)}, f32[16,32,128]{2,1,0:T(8,128)S(1)}, u32[]{:S(2)}, u32[]{:S(2)}) collective-permute-start(f32[16,32,128]{2,1,0:T(8,128)S(1)} %get-tuple-element.210), channel_id=1, source_target_pairs={{0,2},{2,0},{4,6},{6,4},{1,3},{3,1},{5,7},{7,5},{8,10},{10,8},{12,... | collective-permute-start | bytes 786440 | tf_op jit(solution)/shard_map/ppermute | solution.py:463
  109.7 7.2 %collective-permute-start.33 = (f32[16,32,128]{2,1,0:T(8,128)S(1)}, f32[16,32,128]{2,1,0:T(8,128)S(1)}, u32[]{:S(2)}, u32[]{:S(2)}) collective-permute-start(f32[16,32,128]{2,1,0:T(8,128)S(1)} %get-tuple-element.211), channel_id=1, source_target_pairs={{0,4},{2,6},{4,0},{6,2},{1,5},{3,7},{5,1},{7,3},{8,12},{10,14},{12... | collective-permute-start | bytes 786440 | tf_op jit(solution)/shard_map/ppermute | solution.py:463
  110.5 10.9 %collective-permute-start.34 = (f32[16,32,128]{2,1,0:T(8,128)S(1)}, f32[16,32,128]{2,1,0:T(8,128)S(1)}, u32[]{:S(2)}, u32[]{:S(2)}) collective-permute-start(f32[16,32,128]{2,1,0:T(8,128)S(1)} %get-tuple-element.212), channel_id=1, source_target_pairs={{0,6},{2,4},{4,2},{6,0},{1,7},{3,5},{5,3},{7,1},{8,14},{10,12},{12... | collective-permute-start | bytes 786440 | tf_op jit(solution)/shard_map/ppermute | solution.py:463
  113.4 14.4 %collective-permute-start.28 = (f32[16,32,128]{2,1,0:T(8,128)S(1)}, f32[16,32,128]{2,1,0:T(8,128)S(1)}, u32[]{:S(2)}, u32[]{:S(2)}) collective-permute-start(f32[16,32,128]{2,1,0:T(8,128)S(1)} %get-tuple-element.206), channel_id=1, source_target_pairs={{0,2},{2,0},{4,6},{6,4},{1,3},{3,1},{5,7},{7,5},{8,10},{10,8},{12,... | collective-permute-start | bytes 786440 | tf_op jit(solution)/shard_map/ppermute | solution.py:463
  114.7 14.9 %collective-permute-start.29 = (f32[16,32,128]{2,1,0:T(8,128)S(1)}, f32[16,32,128]{2,1,0:T(8,128)S(1)}, u32[]{:S(2)}, u32[]{:S(2)}) collective-permute-start(f32[16,32,128]{2,1,0:T(8,128)S(1)} %get-tuple-element.207), channel_id=1, source_target_pairs={{0,4},{2,6},{4,0},{6,2},{1,5},{3,7},{5,1},{7,3},{8,12},{10,14},{12... | collective-permute-start | bytes 786440 | tf_op jit(solution)/shard_map/ppermute | solution.py:463
  115.5 17.1 %collective-permute-start.30 = (f32[16,32,128]{2,1,0:T(8,128)S(1)}, f32[16,32,128]{2,1,0:T(8,128)S(1)}, u32[]{:S(2)}, u32[]{:S(2)}) collective-permute-start(f32[16,32,128]{2,1,0:T(8,128)S(1)} %get-tuple-element.208), channel_id=1, source_target_pairs={{0,6},{2,4},{4,2},{6,0},{1,7},{3,5},{5,3},{7,1},{8,14},{10,12},{12... | collective-permute-start | bytes 786440 | tf_op jit(solution)/shard_map/ppermute | solution.py:463
  121.9 14.3 %collective-permute-start.35 = (f32[4,16,16,128]{3,2,1,0:T(8,128)S(1)}, f32[4,16,16,128]{3,2,1,0:T(8,128)S(1)}, u32[]{:S(2)}, u32[]{:S(2)}) collective-permute-start(f32[4,16,16,128]{3,2,1,0:T(8,128)S(1)} %split_back.3), channel_id=1, source_target_pairs={{0,1},{1,0},{2,3},{3,2},{4,5},{5,4},{6,7},{7,6},{8,9},{9,8},{10,11... | collective-permute-start | bytes 1572872 | tf_op jit(solution)/shard_map/ppermute | solution.py:562
  133.1 4.6 %collective-permute-start.31 = (f32[4,16,16,128]{3,2,1,0:T(8,128)S(1)}, f32[4,16,16,128]{3,2,1,0:T(8,128)S(1)}, u32[]{:S(2)}, u32[]{:S(2)}) collective-permute-start(f32[4,16,16,128]{3,2,1,0:T(8,128)S(1)} %split_back.2), channel_id=1, source_target_pairs={{0,1},{1,0},{2,3},{3,2},{4,5},{5,4},{6,7},{7,6},{8,9},{9,8},{10,11... | collective-permute-start | bytes 1572872 | tf_op jit(solution)/shard_map/ppermute | solution.py:562

commit v5 on v4

--- a/solution.py
+++ b/solution.py
@@ -258,7 +258,9 @@
         out[first : first + count] = (both[:, :LANES] + both[:, LANES:]).reshape(count, depth, LANES)
 
 
-def near_columns(own, pair, after, wz, wh, out):
+def near_columns(outer, own, pair, after, wz, wh, out):
+    if len(pair.shape) == 4:
+        pair, after = pair.at[0 if outer else 1], after.at[0 if outer else 1]
     deep, depth = pair.shape[:2]
     a = blur_z(wz[...], [pair[i] for i in range(deep)])
     b = blur_z(wz[...], [after[i] for i in range(deep)])
@@ -286,7 +288,7 @@
 
 
 def outer_kernel(me, own, pair, after, wz, wh, out, send_a, send_b):
-    near_columns(own, pair, after, wz, wh, out)
+    near_columns(True, own, pair, after, wz, wh, out)
     rows, count = out.shape[0], send_a.shape[0]
     even = me[3] == 0
 
@@ -322,20 +324,40 @@
 
     def tile(z):
         taps = [wy[i] for i in range(wy.shape[0])]
+        pairs = [taps[i] + taps[i + 1] if i + 1 < len(taps) else taps[i] for i in range(0, len(taps), 2)]
+
+        def cell(y):
+            ref, at = source(y) if 0 <= y < rows else (None, 0)
+            return None if ref is None else ref[at, z, :]
+
+        def difference(p, q):
+            if p is None:
+                return None if q is None else -q
+            return p if q is None else p - q
+
+        def add(total, tap, value):
+            if value is None:
+                return total
+            return tap * value if total is None else total + tap * value
+
         for first in range(0, rows, quarter):
-            sums = [None if pre is None else pre[first + o, z, :] for o in range(quarter)]
-            for y in range(max(0, first - radius), min(rows, first + quarter + radius)):
-                ref, at = source(y)
-                if ref is None:
-                    continue
-                cell = ref[at, z, :]
-                for o in range(quarter):
-                    i = y - (first + o) + radius
+            count = quarter // 2
+            shared, even, odd = ([None] * count for _ in range(3))
+            for r in range(first - radius + 1, first + quarter + radius + 1, 2):
+                middle = cell(r)
+                before, behind = difference(cell(r - 1), middle), difference(cell(r + 1), middle)
+                for o in range(count):
+                    i = r - (first + 2 * o) + radius - 1
                     if 0 <= i < len(taps):
-                        term = taps[i] * cell
-                        sums[o] = term if sums[o] is None else sums[o] + term
-            for o in range(quarter):
-                take(first + o, z, jnp.zeros((8, LANES), F32) if sums[o] is None else sums[o])
+                        shared[o] = add(shared[o], pairs[i // 2], middle)
+                        even[o] = add(even[o], taps[i], before)
+                        if i + 1 < len(taps):
+                            odd[o] = add(odd[o], taps[i + 1], behind)
+            for o in range(count):
+                for k, part in enumerate((even[o], odd[o])):
+                    y = first + 2 * o + k
+                    values = [v for v in (None if pre is None else pre[y, z, :], shared[o], part) if v is not None]
+                    take(y, z, functools.reduce(jnp.add, values) if values else jnp.zeros((8, LANES), F32))
 
     tiles(depth, tile)
 
@@ -349,7 +371,7 @@
 
 def inner_blur(me, cells, pair, after, outer, pre, wz, wx, wh, wy, part, inner, body):
     own_columns(cells, wz, wx, inner)
-    near_columns(inner, pair, after, wz, wh, inner)
+    near_columns(False, inner, pair, after, wz, wh, inner)
     quarter, depth = inner.shape[0] // 2, inner.shape[1]
     blurred = []
 
@@ -428,6 +450,12 @@
     outer_blur(me, part, recv_a, recv_b, wy, halo, update(me, True, rule, base, live, out, (to_pair, to_next)))
 
 
+def first_final_kernel(me, part, recv_a, recv_b, wy, base, live, pair, after, out, to_pair, to_next, halo):
+    to_pair[1], to_next[1] = pair[...], after[...]
+    body = update(me, True, ratio, base, live, out, (to_pair.at[0], to_next.at[0]))
+    outer_blur(me, part, recv_a, recv_b, wy, halo, body)
+
+
 def last_final_kernel(me, part, recv_a, recv_b, wy, base, live, *rest):
     pieces, halo, out = rest[:4], rest[4], rest[5]
     outer_blur(me, part, recv_a, recv_b, wy, halo, update(me, True, product, base, live, out, ()))
@@ -521,9 +549,11 @@
     cells, strips = list(estimate), [taken[0][1:], None]
     for step in range(2 * ITERS):
         w = weights[:4] if step % 2 == 0 else weights[4:]
-        near = exchange(*strips[1]) if step else ()
+        near = exchange(*strips[1]) if step > 1 else ()
         beside = exchange(*strips[0]) if step else strips[0]
         outer, recv_a, recv_b, near = send_outer(cells[0], beside, w, near)
+        if step == 1:
+            near = beside
         if step == 0:
             whole = shape((ny, nz, LANES))
             outer = call(ahead_kernel, whole, [VMEM] * 2, us=0.3, name="ahead")(outer, w[3])
@@ -549,10 +579,14 @@
             functools.partial(inner_kernel, step == 0, rule), [half, half, strip, strip], [SMEM] + [VMEM] * 10, [room], us=3,
             name="inner", mib=16,
         )(*ins)
+        ins = (me, part, recv_a, recv_b, w[3], base[0], live)
+        if step == 0:
+            outs, kernel, ins = [half] + [shape((2,) + strip.shape)] * 2, first_final_kernel, ins + tuple(inner_strips)
+        else:
+            outs, kernel = [half, strip, strip], functools.partial(final_kernel, rule)
         outer, *outer_strips = call(
-            functools.partial(final_kernel, rule), [half, strip, strip], [SMEM] + [VMEM] * 6, [beyond], us=2,
-            name="final", mib=8,
-        )(me, part, recv_a, recv_b, w[3], base[0], live)
+            kernel, outs, [SMEM] + [VMEM] * (len(ins) - 1), [beyond], us=2, name="final", mib=8
+        )(*ins)
         cells, strips = [outer, inner], [outer_strips, inner_strips]
         if step % 2 == 1:
             estimate = cells

time: 140 us -> 137 us (0.979)
  Pallas kernels: 53.2 us -> 50.3 us
    pallas_call x3, Pallas kernels: 18 us -> 16.1 us  [per_device(): call(functools.partial(inner_kernel, step == 0, rule), [half, half, strip...]
    ppermute x4, starting transfers between devices: 9.23 us -> 11 us  [send_outer(): lax.ppermute(send_a, 'yh', evens)]
    ppermute x6 -> x5, starting transfers between devices: 14.9 us -> 13.8 us  [exchange(): return (lax.ppermute(to_pair, 'zl', swaps), after)]
    ppermute x6 -> x5, starting transfers between devices: 4.13 us -> 3.49 us  [exchange(): after = lax.ppermute(to_next, ('yl', 'zl'), [(1, 3), (3, 1)])]
  transfers between devices with their start and end apart: 36 -> 34, of which waited for: 8 -> 8; matrix products, arithmetic and copies ran while one was open for 0% -> 0% of each run, Pallas kernels for 32% -> 29%
where the time goes in v5:
time: 137 us
  starting transfers between devices  60.7 us (44%)
  Pallas kernels  50.3 us (37%)
  waiting for transfers between devices  23.5 us (17%)
  local copies, waits for them, and re-layouts  1.69 us (1%)
    ppermute x12, waiting for transfers between devices, trade(): lax.ppermute(pieces[e], ('yl', 'zh'), [(i, i ^ e) for i in range(4)])  21.1 us
    ppermute x12, starting transfers between devices, trade(): lax.ppermute(pieces[e], ('yl', 'zh'), [(i, i ^ e) for i in range(4)])  17.3 us
    pallas_call x3, Pallas kernels, per_device(): call(functools.partial(inner_kernel, step == 0, rule), [half, half, strip...  16.1 us
    ppermute x5, starting transfers between devices, exchange(): return (lax.ppermute(to_pair, 'zl', swaps), after)  13.8 us
    ppermute x4, starting transfers between devices, send_outer(): lax.ppermute(send_a, 'yh', evens)  11 us
    ppermute x2, starting transfers between devices, back(): return (*pieces, lax.ppermute(sent, 'zl', swaps))  9.22 us
    pallas_call x3, Pallas kernels, per_device(): call(kernel, outs, [SMEM] + [VMEM] * (len(ins) - 1), [beyond], us=2, name...  5.48 us
    pallas_call x1, Pallas kernels, per_device(): call(last_inner_kernel, [half] + [along] * 4, [SMEM] + [VMEM] * 10, [room...  5.45 us
  transfers between devices with their start and end apart: 34, of which 8 were waited for; matrix products, arithmetic and copies ran while one was open for 0% of the time, Pallas kernels for 29%

profile of v5, /device:TPU:0, one launch (start us, length us, event | category | flops | bytes accessed | tf_op | source)
XLA Modules:
  0.0 136.5 jit_solution(17772405107495890461)
XLA Ops:
  0.1 1.6 %copy-done = f32[2,32,16,512]{3,2,1,0:T(8,128)S(1)} copy-done((f32[2,32,16,512]{3,2,1,0:T(8,128)S(1)}, f32[2,32,16,512]{3,2,1,0:T(8,128)}, u32[]{:S(2)}) %copy-start) | copy-done | bytes 2097176
  1.7 2.5 %deal.1 = (f32[2,2,40,16,128]{4,3,2,1,0:T(8,128)S(1)}, f32[2,2,40,16,128]{4,3,2,1,0:T(8,128)S(1)}) custom-call(s32[5]{0:T(128)S(1)} %stack.23.me, f32[2,32,16,512]{3,2,1,0:T(8,128)S(1)} %copy-done), custom_call_target="tpu_custom_call" | custom-call | tf_op jit(solution)/shard_map/deal/pallas_call | solution.py:503
  4.7 2.6 %collective-permute-start.1 = (s32[4,32]{1,0:T(4,128)S(1)}, s32[4,32]{1,0:T(4,128)S(1)}, u32[]{:S(2)}, u32[]{:S(2)}) collective-permute-start(s32[4,32]{1,0:T(4,128)S(1)} %bitcast.6), channel_id=1, source_target_pairs={{0,4},{4,0},{1,5},{5,1},{2,6},{6,2},{3,7},{7,3},{8,12},{12,8},{9,1... | collective-permute-start | bytes 1544 | tf_op jit(solution)/shard_map/ppermute | solution.py:501
  7.3 0.7 mix.1
  8.1 0.8 collective-permute-done.1.theirs
  8.9 2.2 %collective-permute-start.5 = (f32[20,32,128]{2,1,0:T(8,128)S(1)}, f32[20,32,128]{2,1,0:T(8,128)S(1)}, u32[]{:S(2)}, u32[]{:S(2)}) collective-permute-start(f32[20,32,128]{2,1,0:T(8,128)S(1)} %get-tuple-element.121), channel_id=1, source_target_pairs={{0,2},{2,0},{4,6},{6,4},{1,3},{3,1},{5,7},{7,5},{8,10},{10,8},{12,... | collective-permute-start | bytes 983048 | tf_op jit(solution)/shard_map/ppermute | solution.py:491
  11.0 1.5 %collective-permute-start.6 = (f32[20,32,128]{2,1,0:T(8,128)S(1)}, f32[20,32,128]{2,1,0:T(8,128)S(1)}, u32[]{:S(2)}, u32[]{:S(2)}) collective-permute-start(f32[20,32,128]{2,1,0:T(8,128)S(1)} %get-tuple-element.122), channel_id=1, source_target_pairs={{0,4},{2,6},{4,0},{6,2},{1,5},{3,7},{5,1},{7,3},{8,12},{10,14},{12... | collective-permute-start | bytes 983048 | tf_op jit(solution)/shard_map/ppermute | solution.py:491
  12.6 1.9 %collective-permute-start.2 = (f32[20,32,128]{2,1,0:T(8,128)S(1)}, f32[20,32,128]{2,1,0:T(8,128)S(1)}, u32[]{:S(2)}, u32[]{:S(2)}) collective-permute-start(f32[20,32,128]{2,1,0:T(8,128)S(1)} %get-tuple-element.117), channel_id=1, source_target_pairs={{0,2},{2,0},{4,6},{6,4},{1,3},{3,1},{5,7},{7,5},{8,10},{10,8},{12,... | collective-permute-start | bytes 983048 | tf_op jit(solution)/shard_map/ppermute | solution.py:491
  14.5 1.5 %collective-permute-start.3 = (f32[20,32,128]{2,1,0:T(8,128)S(1)}, f32[20,32,128]{2,1,0:T(8,128)S(1)}, u32[]{:S(2)}, u32[]{:S(2)}) collective-permute-start(f32[20,32,128]{2,1,0:T(8,128)S(1)} %get-tuple-element.118), channel_id=1, source_target_pairs={{0,4},{2,6},{4,0},{6,2},{1,5},{3,7},{5,1},{7,3},{8,12},{10,14},{12... | collective-permute-start | bytes 983048 | tf_op jit(solution)/shard_map/ppermute | solution.py:491
  16.1 3.5 %collective-permute-done.5.rest_1_ = f32[20,32,128]{2,1,0:T(8,128)S(1)} collective-permute-done((f32[20,32,128]{2,1,0:T(8,128)S(1)}, f32[20,32,128]{2,1,0:T(8,128)S(1)}, u32[]{:S(2)}, u32[]{:S(2)}) %collective-permute-start.5) | collective-permute-done | bytes 327712 | tf_op jit(solution)/shard_map/ppermute | solution.py:491
  19.5 3.0 %collective-permute-start.4 = (f32[20,32,128]{2,1,0:T(8,128)S(1)}, f32[20,32,128]{2,1,0:T(8,128)S(1)}, u32[]{:S(2)}, u32[]{:S(2)}) collective-permute-start(f32[20,32,128]{2,1,0:T(8,128)S(1)} %get-tuple-element.119), channel_id=1, source_target_pairs={{0,6},{2,4},{4,2},{6,0},{1,7},{3,5},{5,3},{7,1},{8,14},{10,12},{12... | collective-permute-start | bytes 983048 | tf_op jit(solution)/shard_map/ppermute | solution.py:491
  22.6 2.2 %weights.1 = (bf16[256,256]{1,0:T(8,128)(2,1)S(1)}, bf16[256,256]{1,0:T(8,128)(2,1)S(1)}, bf16[256,512]{1,0:T(8,128)(2,1)S(1)}, f32[31,8,128]{2,1,0:T(8,128)S(1)...) custom-call(s32[5]{0:T(128)S(1)} %stack.23.me, ...), custom_call_target="tpu_custom_call" | custom-call | flops 1000000000 | tf_op jit(solution)/shard_map/weights/pallas_call | solution.py:519
  24.8 3.9 %collective-permute-done.6.rest_2_ = f32[20,32,128]{2,1,0:T(8,128)S(1)} collective-permute-done((f32[20,32,128]{2,1,0:T(8,128)S(1)}, f32[20,32,128]{2,1,0:T(8,128)S(1)}, u32[]{:S(2)}, u32[]{:S(2)}) %collective-permute-start.6) | collective-permute-done | bytes 327712 | tf_op jit(solution)/shard_map/ppermute | solution.py:491
  28.7 1.2 join.2
  29.9 1.0 own.4
  30.9 1.3 outer.4
  32.2 1.7 %collective-permute-start.8 = (f32[15,64,128]{2,1,0:T(8,128)S(1)}, f32[15,64,128]{2,1,0:T(8,128)S(1)}, u32[]{:S(2)}, u32[]{:S(2)}) collective-permute-start(f32[15,64,128]{2,1,0:T(8,128)S(1)} %get-tuple-element.158), channel_id=1, source_target_pairs={{0,8},{8,0},{16,24},{24,16},{1,9},{9,1},{17,25},{25,17},{2,10},{10... | collective-permute-start | bytes 1474568 | tf_op jit(solution)/shard_map/ppermute | solution.py:544
  33.8 0.7 collective-permute-start.9
  34.5 1.4 %ahead.1.known = f32[64,64,128]{2,1,0:T(8,128)S(1)} custom-call(f32[32,64,128]{2,1,0:T(8,128)S(1)} %get-tuple-element.145.outer, f32[31,8,128]{2,1,0:T(8,128)S(1)} %get-tuple-element.146.wy), custom_call_target="tpu_custom_call" | custom-call | flops 300000000 | tf_op jit(solution)/shard_map/ahead/pallas_call | solution.py:559
  35.9 5.6 %collective-permute-done.3.rest_2_ = f32[20,32,128]{2,1,0:T(8,128)S(1)} collective-permute-done((f32[20,32,128]{2,1,0:T(8,128)S(1)}, f32[20,32,128]{2,1,0:T(8,128)S(1)}, u32[]{:S(2)}, u32[]{:S(2)}) %collective-permute-start.3) | collective-permute-done | bytes 327712 | tf_op jit(solution)/shard_map/ppermute | solution.py:491
  41.6 1.2 join.3
  42.8 4.5 %inner.3 = (f32[32,64,128]{2,1,0:T(8,128)S(1)}, f32[32,64,128]{2,1,0:T(8,128)S(1)}, f32[4,64,128]{2,1,0:T(8,128)S(1)}, f32[4,64,128]{2,1,0:T(8,128)S(1)}) custom-call(s32[5]{0:T(128)S(1)} %stack.23.me, f32[32,64,128]{2,1,0:T(8,128)S(1)} %get-tuple-element.151.cells.base, f32[4,64,128]{2,1,0:T(8,128)S(1)} %get-tuple-element.152.pair, ...), custom_call_target="tpu_custom_call" | custom-call | flops 3000000000 | tf_op jit(solution)/shard_map/inner/pallas_call | solution.py:578
  47.4 1.9 %final.3 = (f32[32,64,128]{2,1,0:T(8,128)S(1)}, f32[2,4,64,128]{3,2,1,0:T(8,128)S(1)}, f32[2,4,64,128]{3,2,1,0:T(8,128)S(1)}) custom-call(s32[5]{0:T(128)S(1)} %stack.23.me, f32[32,64,128]{2,1,0:T(8,128)S(1)} %get-tuple-element.157.part, f32[15,64,128]{2,1,0:T(8,128)S(1)} %collective-permute-done.8.recv_a, f32[15,64,128]{2,1,0:T(8,128)S(1)} %collective-permute-done.9.recv_b, ...), custom_call_target="tpu_custom_call" | custom-call | flops 2000000000 | tf_op jit(solution)/shard_map/final/pallas_call | solution.py:587
  49.3 0.7 collective-permute-start.11
  50.0 1.0 own.5
  51.0 1.3 outer.5
  52.3 1.7 %collective-permute-start.12 = (f32[15,64,128]{2,1,0:T(8,128)S(1)}, f32[15,64,128]{2,1,0:T(8,128)S(1)}, u32[]{:S(2)}, u32[]{:S(2)}) collective-permute-start(f32[15,64,128]{2,1,0:T(8,128)S(1)} %get-tuple-element.172), channel_id=1, source_target_pairs={{0,8},{8,0},{16,24},{24,16},{1,9},{9,1},{17,25},{25,17},{2,10},{10... | collective-permute-start | bytes 1474568 | tf_op jit(solution)/shard_map/ppermute | solution.py:544
  54.0 0.7 collective-permute-start.13
  54.7 5.7 %inner.4 = (f32[32,64,128]{2,1,0:T(8,128)S(1)}, f32[32,64,128]{2,1,0:T(8,128)S(1)}, f32[4,64,128]{2,1,0:T(8,128)S(1)}, f32[4,64,128]{2,1,0:T(8,128)S(1)}) custom-call(s32[5]{0:T(128)S(1)} %stack.23.me, f32[32,64,128]{2,1,0:T(8,128)S(1)} %get-tuple-element.156.cells, f32[2,4,64,128]{3,2,1,0:T(8,128)S(1)} %collective-permute-done.10.pair, ...), custom_call_target="tpu_custom_call" | custom-call | flops 3000000000 | tf_op jit(solution)/shard_map/inner/pallas_call | solution.py:578
  60.4 6.0 %collective-permute-start.14 = (f32[4,64,128]{2,1,0:T(8,128)S(1)}, f32[4,64,128]{2,1,0:T(8,128)S(1)}, u32[]{:S(2)}, u32[]{:S(2)}) collective-permute-start(f32[4,64,128]{2,1,0:T(8,128)S(1)} %get-tuple-element.175), channel_id=1, source_target_pairs={{0,1},{1,0},{2,3},{3,2},{4,5},{5,4},{6,7},{7,6},{8,9},{9,8},{10,11... | collective-permute-start | bytes 393224 | tf_op jit(solution)/shard_map/ppermute | solution.py:534
  66.4 0.7 collective-permute-start.15
  67.1 1.8 %final.4 = (f32[32,64,128]{2,1,0:T(8,128)S(1)}, f32[4,64,128]{2,1,0:T(8,128)S(1)}, f32[4,64,128]{2,1,0:T(8,128)S(1)}) custom-call(s32[5]{0:T(128)S(1)} %stack.23.me, f32[32,64,128]{2,1,0:T(8,128)S(1)} %get-tuple-element.171.part, f32[15,64,128]{2,1,0:T(8,128)S(1)} %collective-permute-done.12.recv_a, f32[15,64,128]{2,1,0:T(8,128)S(1)} %collective-permute-done.13.recv_b, ...), custom_call_target="tpu_custom_call" | custom-call | flops 2000000000 | tf_op jit(solution)/shard_map/final/pallas_call | solution.py:587
  68.8 2.6 %collective-permute-start.16 = (f32[4,64,128]{2,1,0:T(8,128)S(1)}, f32[4,64,128]{2,1,0:T(8,128)S(1)}, u32[]{:S(2)}, u32[]{:S(2)}) collective-permute-start(f32[4,64,128]{2,1,0:T(8,128)S(1)} %get-tuple-element.180), channel_id=1, source_target_pairs={{0,1},{1,0},{2,3},{3,2},{4,5},{5,4},{6,7},{7,6},{8,9},{9,8},{10,11... | collective-permute-start | bytes 393224 | tf_op jit(solution)/shard_map/ppermute | solution.py:534
  71.4 0.8 collective-permute-start.17
  72.3 1.0 own.6
  73.3 1.3 outer.6
  74.6 4.2 %collective-permute-start.18 = (f32[15,64,128]{2,1,0:T(8,128)S(1)}, f32[15,64,128]{2,1,0:T(8,128)S(1)}, u32[]{:S(2)}, u32[]{:S(2)}) collective-permute-start(f32[15,64,128]{2,1,0:T(8,128)S(1)} %get-tuple-element.185), channel_id=1, source_target_pairs={{0,8},{8,0},{16,24},{24,16},{1,9},{9,1},{17,25},{25,17},{2,10},{10... | collective-permute-start | bytes 1474568 | tf_op jit(solution)/shard_map/ppermute | solution.py:544
  78.8 0.7 collective-permute-start.19
  79.5 5.8 %inner.5 = (f32[32,64,128]{2,1,0:T(8,128)S(1)}, f32[32,64,128]{2,1,0:T(8,128)S(1)}, f32[4,64,128]{2,1,0:T(8,128)S(1)}, f32[4,64,128]{2,1,0:T(8,128)S(1)}) custom-call(s32[5]{0:T(128)S(1)} %stack.23.me, f32[32,64,128]{2,1,0:T(8,128)S(1)} %get-tuple-element.170.cells.base, f32[4,64,128]{2,1,0:T(8,128)S(1)} %collective-permute-done.14.pair, ...), custom_call_target="tpu_custom_call" | custom-call | flops 3000000000 | tf_op jit(solution)/shard_map/inner/pallas_call | solution.py:578
  85.3 3.6 %collective-permute-start.20 = (f32[4,64,128]{2,1,0:T(8,128)S(1)}, f32[4,64,128]{2,1,0:T(8,128)S(1)}, u32[]{:S(2)}, u32[]{:S(2)}) collective-permute-start(f32[4,64,128]{2,1,0:T(8,128)S(1)} %get-tuple-element.188), channel_id=1, source_target_pairs={{0,1},{1,0},{2,3},{3,2},{4,5},{5,4},{6,7},{7,6},{8,9},{9,8},{10,11... | collective-permute-start | bytes 393224 | tf_op jit(solution)/shard_map/ppermute | solution.py:534
  88.9 0.7 collective-permute-start.21
  89.6 1.8 %final.5 = (f32[32,64,128]{2,1,0:T(8,128)S(1)}, f32[4,64,128]{2,1,0:T(8,128)S(1)}, f32[4,64,128]{2,1,0:T(8,128)S(1)}) custom-call(s32[5]{0:T(128)S(1)} %stack.23.me, f32[32,64,128]{2,1,0:T(8,128)S(1)} %get-tuple-element.184.part, f32[15,64,128]{2,1,0:T(8,128)S(1)} %collective-permute-done.18.recv_a, f32[15,64,128]{2,1,0:T(8,128)S(1)} %collective-permute-done.19.recv_b, ...), custom_call_target="tpu_custom_call" | custom-call | flops 2000000000 | tf_op jit(solution)/shard_map/final/pallas_call | solution.py:587
  91.5 1.6 %collective-permute-start.22 = (f32[4,64,128]{2,1,0:T(8,128)S(1)}, f32[4,64,128]{2,1,0:T(8,128)S(1)}, u32[]{:S(2)}, u32[]{:S(2)}) collective-permute-start(f32[4,64,128]{2,1,0:T(8,128)S(1)} %get-tuple-element.193), channel_id=1, source_target_pairs={{0,1},{1,0},{2,3},{3,2},{4,5},{5,4},{6,7},{7,6},{8,9},{9,8},{10,11... | collective-permute-start | bytes 393224 | tf_op jit(solution)/shard_map/ppermute | solution.py:534
  93.0 0.7 collective-permute-start.23
  93.7 1.0 own.7
  94.7 1.3 outer.7
  96.0 3.5 %collective-permute-start.24 = (f32[15,64,128]{2,1,0:T(8,128)S(1)}, f32[15,64,128]{2,1,0:T(8,128)S(1)}, u32[]{:S(2)}, u32[]{:S(2)}) collective-permute-start(f32[15,64,128]{2,1,0:T(8,128)S(1)} %get-tuple-element.197), channel_id=1, source_target_pairs={{0,8},{8,0},{16,24},{24,16},{1,9},{9,1},{17,25},{25,17},{2,10},{10... | collective-permute-start | bytes 1474568 | tf_op jit(solution)/shard_map/ppermute | solution.py:544
  99.6 0.7 collective-permute-start.25
  100.3 5.5 %last_inner.1 = (f32[32,64,128]{2,1,0:T(8,128)S(1)}, f32[16,32,128]{2,1,0:T(8,128)S(1)}, f32[16,32,128]{2,1,0:T(8,128)S(1)}, f32[16,32,128]{2,1,0:T(8,128)S(1)}, f32[16,32,128]{2,1,0:T(8,128)S(1)}) custom-call(s32[5]{0:T(128)S(1)} %stack.23.me, f32[32,64,128]{2,1,0:T(8,128)S(1)} %get-tuple-element.183.cells, f32[4,64,128]{2,1,0:T(8,128)S(1)} %collective-permute-done.20.pair, ...), custom_call_target="tpu_custom_call" | custom-call | flops 3000000000 | tf_op jit(solution)/shard_map/last_inner/pallas_call | solution.py:567
  105.7 0.6 collective-permute-start.30
  106.3 1.2 collective-permute-start.31
  107.6 1.7 %collective-permute-start.32 = (f32[16,32,128]{2,1,0:T(8,128)S(1)}, f32[16,32,128]{2,1,0:T(8,128)S(1)}, u32[]{:S(2)}, u32[]{:S(2)}) collective-permute-start(f32[16,32,128]{2,1,0:T(8,128)S(1)} %get-tuple-element.206), channel_id=1, source_target_pairs={{0,6},{2,4},{4,2},{6,0},{1,7},{3,5},{5,3},{7,1},{8,14},{10,12},{12... | collective-permute-start | bytes 786440 | tf_op jit(solution)/shard_map/ppermute | solution.py:491
  109.3 1.4 %last.1 = (f32[16,32,128]{2,1,0:T(8,128)S(1)}, f32[16,32,128]{2,1,0:T(8,128)S(1)}, f32[16,32,128]{2,1,0:T(8,128)S(1)}, f32[16,32,128]{2,1,0:T(8,128)S(1)}) custom-call(s32[5]{0:T(128)S(1)} %stack.23.me, f32[32,64,128]{2,1,0:T(8,128)S(1)} %get-tuple-element.196.part, f32[15,64,128]{2,1,0:T(8,128)S(1)} %collective-permute-done.24.recv_a, ...), custom_call_target="tpu_custom_call" | custom-call | flops 2000000000 | tf_op jit(solution)/shard_map/last/pallas_call | solution.py:572
  110.8 0.6 collective-permute-start.26
  111.4 1.2 collective-permute-start.27
  112.6 1.7 %collective-permute-start.28 = (f32[16,32,128]{2,1,0:T(8,128)S(1)}, f32[16,32,128]{2,1,0:T(8,128)S(1)}, u32[]{:S(2)}, u32[]{:S(2)}) collective-permute-start(f32[16,32,128]{2,1,0:T(8,128)S(1)} %get-tuple-element.202), channel_id=1, source_target_pairs={{0,6},{2,4},{4,2},{6,0},{1,7},{3,5},{5,3},{7,1},{8,14},{10,12},{12... | collective-permute-start | bytes 786440 | tf_op jit(solution)/shard_map/ppermute | solution.py:491
  114.3 3.4 %collective-permute-done.32.rest_3_.rest_8_ = f32[16,32,128]{2,1,0:T(8,128)S(1)} collective-permute-done((f32[16,32,128]{2,1,0:T(8,128)S(1)}, f32[16,32,128]{2,1,0:T(8,128)S(1)}, u32[]{:S(2)}, u32[]{:S(2)}) %collective-permute-start.32) | collective-permute-done | bytes 262176 | tf_op jit(solution)/shard_map/ppermute | solution.py:491
  117.7 0.6 split_back.3
  118.3 5.9 %collective-permute-start.33 = (f32[4,16,16,128]{3,2,1,0:T(8,128)S(1)}, f32[4,16,16,128]{3,2,1,0:T(8,128)S(1)}, u32[]{:S(2)}, u32[]{:S(2)}) collective-permute-start(f32[4,16,16,128]{3,2,1,0:T(8,128)S(1)} %split_back.3), channel_id=1, source_target_pairs={{0,1},{1,0},{2,3},{3,2},{4,5},{5,4},{6,7},{7,6},{8,9},{9,8},{10,11... | collective-permute-start | bytes 1572872 | tf_op jit(solution)/shard_map/ppermute | solution.py:596
  124.2 2.1 %collective-permute-done.27.rest_2_ = f32[16,32,128]{2,1,0:T(8,128)S(1)} collective-permute-done((f32[16,32,128]{2,1,0:T(8,128)S(1)}, f32[16,32,128]{2,1,0:T(8,128)S(1)}, u32[]{:S(2)}, u32[]{:S(2)}) %collective-permute-start.27) | collective-permute-done | bytes 262176 | tf_op jit(solution)/shard_map/ppermute | solution.py:491
  126.3 2.7 %collective-permute-done.28.rest_3_ = f32[16,32,128]{2,1,0:T(8,128)S(1)} collective-permute-done((f32[16,32,128]{2,1,0:T(8,128)S(1)}, f32[16,32,128]{2,1,0:T(8,128)S(1)}, u32[]{:S(2)}, u32[]{:S(2)}) %collective-permute-start.28) | collective-permute-done | bytes 262176 | tf_op jit(solution)/shard_map/ppermute | solution.py:491
  129.5 3.3 %collective-permute-start.29 = (f32[4,16,16,128]{3,2,1,0:T(8,128)S(1)}, f32[4,16,16,128]{3,2,1,0:T(8,128)S(1)}, u32[]{:S(2)}, u32[]{:S(2)}) collective-permute-start(f32[4,16,16,128]{3,2,1,0:T(8,128)S(1)} %split_back.2), channel_id=1, source_target_pairs={{0,1},{1,0},{2,3},{3,2},{4,5},{5,4},{6,7},{7,6},{8,9},{9,8},{10,11... | collective-permute-start | bytes 1572872 | tf_op jit(solution)/shard_map/ppermute | solution.py:596
  132.9 1.5 %collective-permute-done.29.rest_4_ = f32[4,16,16,128]{3,2,1,0:T(8,128)S(1)} collective-permute-done((f32[4,16,16,128]{3,2,1,0:T(8,128)S(1)}, f32[4,16,16,128]{3,2,1,0:T(8,128)S(1)}, u32[]{:S(2)}, u32[]{:S(2)}) %collective-permute-start.29) | collective-permute-done | bytes 524320 | tf_op jit(solution)/shard_map/ppermute | solution.py:596
  134.4 2.1 %gather.1 = f32[2,32,16,512]{3,2,1,0:T(8,128)} custom-call(s32[5]{0:T(128)S(1)} %stack.23.me, f32[16,32,128]{2,1,0:T(8,128)S(1)} %get-tuple-element.199.rest_0_, f32[16,32,128]{2,1,0:T(8,128)S(1)} %collective-permute-done.26.rest_1_, f32[16,32,128]{2,1,0:T(8,128)S(1)} %collective-permute-done.27.rest_2_, f32[16,32,128]{2,1,0:T(8,128)S(1)} %collective-permute-done.28.rest_3_, ...), custom_call_target="tpu_custom_call" | custom-call | flops 2000000000 | tf_op jit(solution)/shard_map/gather/pallas_call | solution.py:598
  (40 shorter events, 1.4 us)
Async XLA Ops:
  0.0 4.7 %copy-start.1 = (s32[1,4,32]{2,1,0:T(4,128)S(1)}, s32[1,4,32]{2,1,0:T(4,128)}, u32[]{:S(2)}) copy-start(s32[1,4,32]{2,1,0:T(4,128)} %param.9) | copy-start | bytes 1540
  0.1 1.6 %copy-start = (f32[2,32,16,512]{3,2,1,0:T(8,128)S(1)}, f32[2,32,16,512]{3,2,1,0:T(8,128)}, u32[]{:S(2)}) copy-start(f32[2,32,16,512]{3,2,1,0:T(8,128)} %observed.1) | copy-start | bytes 6291460
  1.7 20.9 %copy-start.2 = (f32[2,31]{1,0:T(2,128)S(1)}, f32[2,31]{1,0:T(2,128)}, u32[]{:S(2)}) copy-start(f32[2,31]{1,0:T(2,128)} %rows.1) | copy-start | bytes 748
  1.7 20.9 %copy-start.3 = (f32[2,31]{1,0:T(2,128)S(1)}, f32[2,31]{1,0:T(2,128)}, u32[]{:S(2)}) copy-start(f32[2,31]{1,0:T(2,128)} %columns.1) | copy-start | bytes 748
  1.7 20.9 %copy-start.4 = (f32[2,101]{1,0:T(2,128)S(1)}, f32[2,101]{1,0:T(2,128)}, u32[]{:S(2)}) copy-start(f32[2,101]{1,0:T(2,128)} %axial.1) | copy-start | bytes 2428
  4.2 3.2 %collective-permute-start = (f32[2,2,40,16,128]{4,3,2,1,0:T(8,128)S(1)}, f32[2,2,40,16,128]{4,3,2,1,0:T(8,128)S(1)}, u32[]{:S(2)}, u32[]{:S(2)}) collective-permute-start(f32[2,2,40,16,128]{4,3,2,1,0:T(8,128)S(1)} %get-tuple-element.107), channel_id=1, source_target_pairs={{0,1},{1,0},{2,3},{3,2},{4,5},{5,4},{6,7},{7,6},{8,9},{9,8},{10,11... | collective-permute-start | bytes 3932168 | tf_op jit(solution)/shard_map/ppermute | solution.py:504
  4.7 4.2 %collective-permute-start.1 = (s32[4,32]{1,0:T(4,128)S(1)}, s32[4,32]{1,0:T(4,128)S(1)}, u32[]{:S(2)}, u32[]{:S(2)}) collective-permute-start(s32[4,32]{1,0:T(4,128)S(1)} %bitcast.6), channel_id=1, source_target_pairs={{0,4},{4,0},{1,5},{5,1},{2,6},{6,2},{3,7},{7,3},{8,12},{12,8},{9,1... | collective-permute-start | bytes 1544 | tf_op jit(solution)/shard_map/ppermute | solution.py:501
  8.9 10.7 %collective-permute-start.5 = (f32[20,32,128]{2,1,0:T(8,128)S(1)}, f32[20,32,128]{2,1,0:T(8,128)S(1)}, u32[]{:S(2)}, u32[]{:S(2)}) collective-permute-start(f32[20,32,128]{2,1,0:T(8,128)S(1)} %get-tuple-element.121), channel_id=1, source_target_pairs={{0,2},{2,0},{4,6},{6,4},{1,3},{3,1},{5,7},{7,5},{8,10},{10,8},{12,... | collective-permute-start | bytes 983048 | tf_op jit(solution)/shard_map/ppermute | solution.py:491
  11.0 17.6 %collective-permute-start.6 = (f32[20,32,128]{2,1,0:T(8,128)S(1)}, f32[20,32,128]{2,1,0:T(8,128)S(1)}, u32[]{:S(2)}, u32[]{:S(2)}) collective-permute-start(f32[20,32,128]{2,1,0:T(8,128)S(1)} %get-tuple-element.122), channel_id=1, source_target_pairs={{0,4},{2,6},{4,0},{6,2},{1,5},{3,7},{5,1},{7,3},{8,12},{10,14},{12... | collective-permute-start | bytes 983048 | tf_op jit(solution)/shard_map/ppermute | solution.py:491
  12.6 16.1 %collective-permute-start.7 = (f32[20,32,128]{2,1,0:T(8,128)S(1)}, f32[20,32,128]{2,1,0:T(8,128)S(1)}, u32[]{:S(2)}, u32[]{:S(2)}) collective-permute-start(f32[20,32,128]{2,1,0:T(8,128)S(1)} %get-tuple-element.123), channel_id=1, source_target_pairs={{0,6},{2,4},{4,2},{6,0},{1,7},{3,5},{5,3},{7,1},{8,14},{10,12},{12... | collective-permute-start | bytes 983048 | tf_op jit(solution)/shard_map/ppermute | solution.py:491
  12.6 23.4 %collective-permute-start.2 = (f32[20,32,128]{2,1,0:T(8,128)S(1)}, f32[20,32,128]{2,1,0:T(8,128)S(1)}, u32[]{:S(2)}, u32[]{:S(2)}) collective-permute-start(f32[20,32,128]{2,1,0:T(8,128)S(1)} %get-tuple-element.117), channel_id=1, source_target_pairs={{0,2},{2,0},{4,6},{6,4},{1,3},{3,1},{5,7},{7,5},{8,10},{10,8},{12,... | collective-permute-start | bytes 983048 | tf_op jit(solution)/shard_map/ppermute | solution.py:491
  14.5 27.1 %collective-permute-start.3 = (f32[20,32,128]{2,1,0:T(8,128)S(1)}, f32[20,32,128]{2,1,0:T(8,128)S(1)}, u32[]{:S(2)}, u32[]{:S(2)}) collective-permute-start(f32[20,32,128]{2,1,0:T(8,128)S(1)} %get-tuple-element.118), channel_id=1, source_target_pairs={{0,4},{2,6},{4,0},{6,2},{1,5},{3,7},{5,1},{7,3},{8,12},{10,14},{12... | collective-permute-start | bytes 983048 | tf_op jit(solution)/shard_map/ppermute | solution.py:491
  19.5 22.0 %collective-permute-start.4 = (f32[20,32,128]{2,1,0:T(8,128)S(1)}, f32[20,32,128]{2,1,0:T(8,128)S(1)}, u32[]{:S(2)}, u32[]{:S(2)}) collective-permute-start(f32[20,32,128]{2,1,0:T(8,128)S(1)} %get-tuple-element.119), channel_id=1, source_target_pairs={{0,6},{2,4},{4,2},{6,0},{1,7},{3,5},{5,3},{7,1},{8,14},{10,12},{12... | collective-permute-start | bytes 983048 | tf_op jit(solution)/shard_map/ppermute | solution.py:491
  32.2 15.1 %collective-permute-start.8 = (f32[15,64,128]{2,1,0:T(8,128)S(1)}, f32[15,64,128]{2,1,0:T(8,128)S(1)}, u32[]{:S(2)}, u32[]{:S(2)}) collective-permute-start(f32[15,64,128]{2,1,0:T(8,128)S(1)} %get-tuple-element.158), channel_id=1, source_target_pairs={{0,8},{8,0},{16,24},{24,16},{1,9},{9,1},{17,25},{25,17},{2,10},{10... | collective-permute-start | bytes 1474568 | tf_op jit(solution)/shard_map/ppermute | solution.py:544
  33.8 13.5 %collective-permute-start.9 = (f32[15,64,128]{2,1,0:T(8,128)S(1)}, f32[15,64,128]{2,1,0:T(8,128)S(1)}, u32[]{:S(2)}, u32[]{:S(2)}) collective-permute-start(f32[15,64,128]{2,1,0:T(8,128)S(1)} %get-tuple-element.159), channel_id=1, source_target_pairs={{8,16},{16,8},{9,17},{17,9},{10,18},{18,10},{11,19},{19,11},{12,20... | collective-permute-start | bytes 1474568 | tf_op jit(solution)/shard_map/ppermute | solution.py:544
  49.2 1.7 %collective-permute-start.10 = (f32[2,4,64,128]{3,2,1,0:T(8,128)S(1)}, f32[2,4,64,128]{3,2,1,0:T(8,128)S(1)}, u32[]{:S(2)}, u32[]{:S(2)}) collective-permute-start(f32[2,4,64,128]{3,2,1,0:T(8,128)S(1)} %get-tuple-element.162), channel_id=1, source_target_pairs={{0,1},{1,0},{2,3},{3,2},{4,5},{5,4},{6,7},{7,6},{8,9},{9,8},{10,11... | collective-permute-start | bytes 786440 | tf_op jit(solution)/shard_map/ppermute | solution.py:534
  49.3 1.7 %collective-permute-start.11 = (f32[2,4,64,128]{3,2,1,0:T(8,128)S(1)}, f32[2,4,64,128]{3,2,1,0:T(8,128)S(1)}, u32[]{:S(2)}, u32[]{:S(2)}) collective-permute-start(f32[2,4,64,128]{3,2,1,0:T(8,128)S(1)} %get-tuple-element.163), channel_id=1, source_target_pairs={{1,5},{5,1},{3,7},{7,3},{9,13},{13,9},{11,15},{15,11},{17,21},{21,... | collective-permute-start | bytes 786440 | tf_op jit(solution)/shard_map/ppermute | solution.py:533
  52.3 14.7 %collective-permute-start.12 = (f32[15,64,128]{2,1,0:T(8,128)S(1)}, f32[15,64,128]{2,1,0:T(8,128)S(1)}, u32[]{:S(2)}, u32[]{:S(2)}) collective-permute-start(f32[15,64,128]{2,1,0:T(8,128)S(1)} %get-tuple-element.172), channel_id=1, source_target_pairs={{0,8},{8,0},{16,24},{24,16},{1,9},{9,1},{17,25},{25,17},{2,10},{10... | collective-permute-start | bytes 1474568 | tf_op jit(solution)/shard_map/ppermute | solution.py:544
  54.0 13.1 %collective-permute-start.13 = (f32[15,64,128]{2,1,0:T(8,128)S(1)}, f32[15,64,128]{2,1,0:T(8,128)S(1)}, u32[]{:S(2)}, u32[]{:S(2)}) collective-permute-start(f32[15,64,128]{2,1,0:T(8,128)S(1)} %get-tuple-element.173), channel_id=1, source_target_pairs={{8,16},{16,8},{9,17},{17,9},{10,18},{18,10},{11,19},{19,11},{12,20... | collective-permute-start | bytes 1474568 | tf_op jit(solution)/shard_map/ppermute | solution.py:544
  60.4 11.9 %collective-permute-start.14 = (f32[4,64,128]{2,1,0:T(8,128)S(1)}, f32[4,64,128]{2,1,0:T(8,128)S(1)}, u32[]{:S(2)}, u32[]{:S(2)}) collective-permute-start(f32[4,64,128]{2,1,0:T(8,128)S(1)} %get-tuple-element.175), channel_id=1, source_target_pairs={{0,1},{1,0},{2,3},{3,2},{4,5},{5,4},{6,7},{7,6},{8,9},{9,8},{10,11... | collective-permute-start | bytes 393224 | tf_op jit(solution)/shard_map/ppermute | solution.py:534
  66.4 5.9 %collective-permute-start.15 = (f32[4,64,128]{2,1,0:T(8,128)S(1)}, f32[4,64,128]{2,1,0:T(8,128)S(1)}, u32[]{:S(2)}, u32[]{:S(2)}) collective-permute-start(f32[4,64,128]{2,1,0:T(8,128)S(1)} %get-tuple-element.176), channel_id=1, source_target_pairs={{1,5},{5,1},{3,7},{7,3},{9,13},{13,9},{11,15},{15,11},{17,21},{21,... | collective-permute-start | bytes 393224 | tf_op jit(solution)/shard_map/ppermute | solution.py:533
  68.8 4.4 %collective-permute-start.16 = (f32[4,64,128]{2,1,0:T(8,128)S(1)}, f32[4,64,128]{2,1,0:T(8,128)S(1)}, u32[]{:S(2)}, u32[]{:S(2)}) collective-permute-start(f32[4,64,128]{2,1,0:T(8,128)S(1)} %get-tuple-element.180), channel_id=1, source_target_pairs={{0,1},{1,0},{2,3},{3,2},{4,5},{5,4},{6,7},{7,6},{8,9},{9,8},{10,11... | collective-permute-start | bytes 393224 | tf_op jit(solution)/shard_map/ppermute | solution.py:534
  71.4 1.9 %collective-permute-start.17 = (f32[4,64,128]{2,1,0:T(8,128)S(1)}, f32[4,64,128]{2,1,0:T(8,128)S(1)}, u32[]{:S(2)}, u32[]{:S(2)}) collective-permute-start(f32[4,64,128]{2,1,0:T(8,128)S(1)} %get-tuple-element.181), channel_id=1, source_target_pairs={{1,5},{5,1},{3,7},{7,3},{9,13},{13,9},{11,15},{15,11},{17,21},{21,... | collective-permute-start | bytes 393224 | tf_op jit(solution)/shard_map/ppermute | solution.py:533
  74.6 15.0 %collective-permute-start.18 = (f32[15,64,128]{2,1,0:T(8,128)S(1)}, f32[15,64,128]{2,1,0:T(8,128)S(1)}, u32[]{:S(2)}, u32[]{:S(2)}) collective-permute-start(f32[15,64,128]{2,1,0:T(8,128)S(1)} %get-tuple-element.185), channel_id=1, source_target_pairs={{0,8},{8,0},{16,24},{24,16},{1,9},{9,1},{17,25},{25,17},{2,10},{10... | collective-permute-start | bytes 1474568 | tf_op jit(solution)/shard_map/ppermute | solution.py:544
  78.8 10.8 %collective-permute-start.19 = (f32[15,64,128]{2,1,0:T(8,128)S(1)}, f32[15,64,128]{2,1,0:T(8,128)S(1)}, u32[]{:S(2)}, u32[]{:S(2)}) collective-permute-start(f32[15,64,128]{2,1,0:T(8,128)S(1)} %get-tuple-element.186), channel_id=1, source_target_pairs={{8,16},{16,8},{9,17},{17,9},{10,18},{18,10},{11,19},{19,11},{12,20... | collective-permute-start | bytes 1474568 | tf_op jit(solution)/shard_map/ppermute | solution.py:544
  85.3 8.4 %collective-permute-start.20 = (f32[4,64,128]{2,1,0:T(8,128)S(1)}, f32[4,64,128]{2,1,0:T(8,128)S(1)}, u32[]{:S(2)}, u32[]{:S(2)}) collective-permute-start(f32[4,64,128]{2,1,0:T(8,128)S(1)} %get-tuple-element.188), channel_id=1, source_target_pairs={{0,1},{1,0},{2,3},{3,2},{4,5},{5,4},{6,7},{7,6},{8,9},{9,8},{10,11... | collective-permute-start | bytes 393224 | tf_op jit(solution)/shard_map/ppermute | solution.py:534
  88.9 4.8 %collective-permute-start.21 = (f32[4,64,128]{2,1,0:T(8,128)S(1)}, f32[4,64,128]{2,1,0:T(8,128)S(1)}, u32[]{:S(2)}, u32[]{:S(2)}) collective-permute-start(f32[4,64,128]{2,1,0:T(8,128)S(1)} %get-tuple-element.189), channel_id=1, source_target_pairs={{1,5},{5,1},{3,7},{7,3},{9,13},{13,9},{11,15},{15,11},{17,21},{21,... | collective-permute-start | bytes 393224 | tf_op jit(solution)/shard_map/ppermute | solution.py:533
  91.5 3.2 %collective-permute-start.22 = (f32[4,64,128]{2,1,0:T(8,128)S(1)}, f32[4,64,128]{2,1,0:T(8,128)S(1)}, u32[]{:S(2)}, u32[]{:S(2)}) collective-permute-start(f32[4,64,128]{2,1,0:T(8,128)S(1)} %get-tuple-element.193), channel_id=1, source_target_pairs={{0,1},{1,0},{2,3},{3,2},{4,5},{5,4},{6,7},{7,6},{8,9},{9,8},{10,11... | collective-permute-start | bytes 393224 | tf_op jit(solution)/shard_map/ppermute | solution.py:534
  93.0 1.7 %collective-permute-start.23 = (f32[4,64,128]{2,1,0:T(8,128)S(1)}, f32[4,64,128]{2,1,0:T(8,128)S(1)}, u32[]{:S(2)}, u32[]{:S(2)}) collective-permute-start(f32[4,64,128]{2,1,0:T(8,128)S(1)} %get-tuple-element.194), channel_id=1, source_target_pairs={{1,5},{5,1},{3,7},{7,3},{9,13},{13,9},{11,15},{15,11},{17,21},{21,... | collective-permute-start | bytes 393224 | tf_op jit(solution)/shard_map/ppermute | solution.py:533
  96.0 13.2 %collective-permute-start.24 = (f32[15,64,128]{2,1,0:T(8,128)S(1)}, f32[15,64,128]{2,1,0:T(8,128)S(1)}, u32[]{:S(2)}, u32[]{:S(2)}) collective-permute-start(f32[15,64,128]{2,1,0:T(8,128)S(1)} %get-tuple-element.197), channel_id=1, source_target_pairs={{0,8},{8,0},{16,24},{24,16},{1,9},{9,1},{17,25},{25,17},{2,10},{10... | collective-permute-start | bytes 1474568 | tf_op jit(solution)/shard_map/ppermute | solution.py:544
  99.6 9.7 %collective-permute-start.25 = (f32[15,64,128]{2,1,0:T(8,128)S(1)}, f32[15,64,128]{2,1,0:T(8,128)S(1)}, u32[]{:S(2)}, u32[]{:S(2)}) collective-permute-start(f32[15,64,128]{2,1,0:T(8,128)S(1)} %get-tuple-element.198), channel_id=1, source_target_pairs={{8,16},{16,8},{9,17},{17,9},{10,18},{18,10},{11,19},{19,11},{12,20... | collective-permute-start | bytes 1474568 | tf_op jit(solution)/shard_map/ppermute | solution.py:544
  105.7 6.9 %collective-permute-start.30 = (f32[16,32,128]{2,1,0:T(8,128)S(1)}, f32[16,32,128]{2,1,0:T(8,128)S(1)}, u32[]{:S(2)}, u32[]{:S(2)}) collective-permute-start(f32[16,32,128]{2,1,0:T(8,128)S(1)} %get-tuple-element.204), channel_id=1, source_target_pairs={{0,2},{2,0},{4,6},{6,4},{1,3},{3,1},{5,7},{7,5},{8,10},{10,8},{12,... | collective-permute-start | bytes 786440 | tf_op jit(solution)/shard_map/ppermute | solution.py:491
  106.3 8.0 %collective-permute-start.31 = (f32[16,32,128]{2,1,0:T(8,128)S(1)}, f32[16,32,128]{2,1,0:T(8,128)S(1)}, u32[]{:S(2)}, u32[]{:S(2)}) collective-permute-start(f32[16,32,128]{2,1,0:T(8,128)S(1)} %get-tuple-element.205), channel_id=1, source_target_pairs={{0,4},{2,6},{4,0},{6,2},{1,5},{3,7},{5,1},{7,3},{8,12},{10,14},{12... | collective-permute-start | bytes 786440 | tf_op jit(solution)/shard_map/ppermute | solution.py:491
  107.6 10.1 %collective-permute-start.32 = (f32[16,32,128]{2,1,0:T(8,128)S(1)}, f32[16,32,128]{2,1,0:T(8,128)S(1)}, u32[]{:S(2)}, u32[]{:S(2)}) collective-permute-start(f32[16,32,128]{2,1,0:T(8,128)S(1)} %get-tuple-element.206), channel_id=1, source_target_pairs={{0,6},{2,4},{4,2},{6,0},{1,7},{3,5},{5,3},{7,1},{8,14},{10,12},{12... | collective-permute-start | bytes 786440 | tf_op jit(solution)/shard_map/ppermute | solution.py:491
  110.8 13.4 %collective-permute-start.26 = (f32[16,32,128]{2,1,0:T(8,128)S(1)}, f32[16,32,128]{2,1,0:T(8,128)S(1)}, u32[]{:S(2)}, u32[]{:S(2)}) collective-permute-start(f32[16,32,128]{2,1,0:T(8,128)S(1)} %get-tuple-element.200), channel_id=1, source_target_pairs={{0,2},{2,0},{4,6},{6,4},{1,3},{3,1},{5,7},{7,5},{8,10},{10,8},{12,... | collective-permute-start | bytes 786440 | tf_op jit(solution)/shard_map/ppermute | solution.py:491
  111.4 14.9 %collective-permute-start.27 = (f32[16,32,128]{2,1,0:T(8,128)S(1)}, f32[16,32,128]{2,1,0:T(8,128)S(1)}, u32[]{:S(2)}, u32[]{:S(2)}) collective-permute-start(f32[16,32,128]{2,1,0:T(8,128)S(1)} %get-tuple-element.201), channel_id=1, source_target_pairs={{0,4},{2,6},{4,0},{6,2},{1,5},{3,7},{5,1},{7,3},{8,12},{10,14},{12... | collective-permute-start | bytes 786440 | tf_op jit(solution)/shard_map/ppermute | solution.py:491
  112.6 16.3 %collective-permute-start.28 = (f32[16,32,128]{2,1,0:T(8,128)S(1)}, f32[16,32,128]{2,1,0:T(8,128)S(1)}, u32[]{:S(2)}, u32[]{:S(2)}) collective-permute-start(f32[16,32,128]{2,1,0:T(8,128)S(1)} %get-tuple-element.202), channel_id=1, source_target_pairs={{0,6},{2,4},{4,2},{6,0},{1,7},{3,5},{5,3},{7,1},{8,14},{10,12},{12... | collective-permute-start | bytes 786440 | tf_op jit(solution)/shard_map/ppermute | solution.py:491
  118.3 14.6 %collective-permute-start.33 = (f32[4,16,16,128]{3,2,1,0:T(8,128)S(1)}, f32[4,16,16,128]{3,2,1,0:T(8,128)S(1)}, u32[]{:S(2)}, u32[]{:S(2)}) collective-permute-start(f32[4,16,16,128]{3,2,1,0:T(8,128)S(1)} %split_back.3), channel_id=1, source_target_pairs={{0,1},{1,0},{2,3},{3,2},{4,5},{5,4},{6,7},{7,6},{8,9},{9,8},{10,11... | collective-permute-start | bytes 1572872 | tf_op jit(solution)/shard_map/ppermute | solution.py:596
  129.5 4.9 %collective-permute-start.29 = (f32[4,16,16,128]{3,2,1,0:T(8,128)S(1)}, f32[4,16,16,128]{3,2,1,0:T(8,128)S(1)}, u32[]{:S(2)}, u32[]{:S(2)}) collective-permute-start(f32[4,16,16,128]{3,2,1,0:T(8,128)S(1)} %split_back.2), channel_id=1, source_target_pairs={{0,1},{1,0},{2,3},{3,2},{4,5},{5,4},{6,7},{7,6},{8,9},{9,8},{10,11... | collective-permute-start | bytes 1572872 | tf_op jit(solution)/shard_map/ppermute | solution.py:596

commit v6 on v5

--- a/solution.py
+++ b/solution.py
@@ -153,7 +153,7 @@
         body(pl.ds(pl.multiple_of(8 * t, 8), 8))
         return 0
 
-    lax.fori_loop(0, depth // 8, one, 0)
+    lax.fori_loop(0, depth // 8, one, 0, unroll=4)
 
 
 def weights_kernel(me, rows, columns, axial, listed, theirs, *outs):

time: 137 us -> 134 us (0.978)
  Pallas kernels: 50.3 us -> 46.5 us
    pallas_call x3, Pallas kernels: 16.1 us -> 14.7 us  [per_device(): call(functools.partial(inner_kernel, step == 0, rule), [half, half, strip...]
  transfers between devices with their start and end apart: 34 -> 34, of which waited for: 8 -> 8; matrix products, arithmetic and copies ran while one was open for 0% -> 0% of each run, Pallas kernels for 29% -> 27%
where the time goes in v6:
time: 134 us
  starting transfers between devices  61.4 us (46%)
  Pallas kernels  46.5 us (35%)
  waiting for transfers between devices  24.1 us (18%)
  local copies, waits for them, and re-layouts  1.69 us (1%)
    ppermute x12, waiting for transfers between devices, trade(): lax.ppermute(pieces[e], ('yl', 'zh'), [(i, i ^ e) for i in range(4)])  21.7 us
    ppermute x12, starting transfers between devices, trade(): lax.ppermute(pieces[e], ('yl', 'zh'), [(i, i ^ e) for i in range(4)])  17.3 us
    pallas_call x3, Pallas kernels, per_device(): call(functools.partial(inner_kernel, step == 0, rule), [half, half, strip...  14.7 us
    ppermute x5, starting transfers between devices, exchange(): return (lax.ppermute(to_pair, 'zl', swaps), after)  14 us
    ppermute x4, starting transfers between devices, send_outer(): lax.ppermute(send_a, 'yh', evens)  11.3 us
    ppermute x2, starting transfers between devices, back(): return (*pieces, lax.ppermute(sent, 'zl', swaps))  9.2 us
    pallas_call x4, Pallas kernels, send_outer(): call(outer_kernel, [half, halo, halo], [SMEM] + [VMEM] * 5, us=0.3, name=...  5.33 us
    pallas_call x1, Pallas kernels, per_device(): call(last_inner_kernel, [half] + [along] * 4, [SMEM] + [VMEM] * 10, [room...  5.32 us
  transfers between devices with their start and end apart: 34, of which 8 were waited for; matrix products, arithmetic and copies ran while one was open for 0% of the time, Pallas kernels for 27%

profile of v6, /device:TPU:0, one launch (start us, length us, event | category | flops | bytes accessed | tf_op | source)
XLA Modules:
  0.0 134.0 jit_solution(5720074884275787128)
XLA Ops:
  0.1 1.6 %copy-done = f32[2,32,16,512]{3,2,1,0:T(8,128)S(1)} copy-done((f32[2,32,16,512]{3,2,1,0:T(8,128)S(1)}, f32[2,32,16,512]{3,2,1,0:T(8,128)}, u32[]{:S(2)}) %copy-start) | copy-done | bytes 2097176
  1.7 2.5 %deal.1 = (f32[2,2,40,16,128]{4,3,2,1,0:T(8,128)S(1)}, f32[2,2,40,16,128]{4,3,2,1,0:T(8,128)S(1)}) custom-call(s32[5]{0:T(128)S(1)} %stack.23.me, f32[2,32,16,512]{3,2,1,0:T(8,128)S(1)} %copy-done), custom_call_target="tpu_custom_call" | custom-call | tf_op jit(solution)/shard_map/deal/pallas_call | solution.py:503
  4.7 2.6 %collective-permute-start.1 = (s32[4,32]{1,0:T(4,128)S(1)}, s32[4,32]{1,0:T(4,128)S(1)}, u32[]{:S(2)}, u32[]{:S(2)}) collective-permute-start(s32[4,32]{1,0:T(4,128)S(1)} %bitcast.6), channel_id=1, source_target_pairs={{0,4},{4,0},{1,5},{5,1},{2,6},{6,2},{3,7},{7,3},{8,12},{12,8},{9,1... | collective-permute-start | bytes 1544 | tf_op jit(solution)/shard_map/ppermute | solution.py:501
  7.3 0.7 mix.1
  8.1 0.8 collective-permute-done.1.theirs
  8.9 2.2 %collective-permute-start.5 = (f32[20,32,128]{2,1,0:T(8,128)S(1)}, f32[20,32,128]{2,1,0:T(8,128)S(1)}, u32[]{:S(2)}, u32[]{:S(2)}) collective-permute-start(f32[20,32,128]{2,1,0:T(8,128)S(1)} %get-tuple-element.121), channel_id=1, source_target_pairs={{0,2},{2,0},{4,6},{6,4},{1,3},{3,1},{5,7},{7,5},{8,10},{10,8},{12,... | collective-permute-start | bytes 983048 | tf_op jit(solution)/shard_map/ppermute | solution.py:491
  11.0 1.5 %collective-permute-start.6 = (f32[20,32,128]{2,1,0:T(8,128)S(1)}, f32[20,32,128]{2,1,0:T(8,128)S(1)}, u32[]{:S(2)}, u32[]{:S(2)}) collective-permute-start(f32[20,32,128]{2,1,0:T(8,128)S(1)} %get-tuple-element.122), channel_id=1, source_target_pairs={{0,4},{2,6},{4,0},{6,2},{1,5},{3,7},{5,1},{7,3},{8,12},{10,14},{12... | collective-permute-start | bytes 983048 | tf_op jit(solution)/shard_map/ppermute | solution.py:491
  12.6 1.9 %collective-permute-start.2 = (f32[20,32,128]{2,1,0:T(8,128)S(1)}, f32[20,32,128]{2,1,0:T(8,128)S(1)}, u32[]{:S(2)}, u32[]{:S(2)}) collective-permute-start(f32[20,32,128]{2,1,0:T(8,128)S(1)} %get-tuple-element.117), channel_id=1, source_target_pairs={{0,2},{2,0},{4,6},{6,4},{1,3},{3,1},{5,7},{7,5},{8,10},{10,8},{12,... | collective-permute-start | bytes 983048 | tf_op jit(solution)/shard_map/ppermute | solution.py:491
  14.5 1.5 %collective-permute-start.3 = (f32[20,32,128]{2,1,0:T(8,128)S(1)}, f32[20,32,128]{2,1,0:T(8,128)S(1)}, u32[]{:S(2)}, u32[]{:S(2)}) collective-permute-start(f32[20,32,128]{2,1,0:T(8,128)S(1)} %get-tuple-element.118), channel_id=1, source_target_pairs={{0,4},{2,6},{4,0},{6,2},{1,5},{3,7},{5,1},{7,3},{8,12},{10,14},{12... | collective-permute-start | bytes 983048 | tf_op jit(solution)/shard_map/ppermute | solution.py:491
  16.1 3.5 %collective-permute-done.5.rest_1_ = f32[20,32,128]{2,1,0:T(8,128)S(1)} collective-permute-done((f32[20,32,128]{2,1,0:T(8,128)S(1)}, f32[20,32,128]{2,1,0:T(8,128)S(1)}, u32[]{:S(2)}, u32[]{:S(2)}) %collective-permute-start.5) | collective-permute-done | bytes 327712 | tf_op jit(solution)/shard_map/ppermute | solution.py:491
  19.5 3.0 %collective-permute-start.4 = (f32[20,32,128]{2,1,0:T(8,128)S(1)}, f32[20,32,128]{2,1,0:T(8,128)S(1)}, u32[]{:S(2)}, u32[]{:S(2)}) collective-permute-start(f32[20,32,128]{2,1,0:T(8,128)S(1)} %get-tuple-element.119), channel_id=1, source_target_pairs={{0,6},{2,4},{4,2},{6,0},{1,7},{3,5},{5,3},{7,1},{8,14},{10,12},{12... | collective-permute-start | bytes 983048 | tf_op jit(solution)/shard_map/ppermute | solution.py:491
  22.6 2.2 %weights.1 = (bf16[256,256]{1,0:T(8,128)(2,1)S(1)}, bf16[256,256]{1,0:T(8,128)(2,1)S(1)}, bf16[256,512]{1,0:T(8,128)(2,1)S(1)}, f32[31,8,128]{2,1,0:T(8,128)S(1)...) custom-call(s32[5]{0:T(128)S(1)} %stack.23.me, ...), custom_call_target="tpu_custom_call" | custom-call | flops 1000000000 | tf_op jit(solution)/shard_map/weights/pallas_call | solution.py:519
  24.8 3.9 %collective-permute-done.6.rest_2_ = f32[20,32,128]{2,1,0:T(8,128)S(1)} collective-permute-done((f32[20,32,128]{2,1,0:T(8,128)S(1)}, f32[20,32,128]{2,1,0:T(8,128)S(1)}, u32[]{:S(2)}, u32[]{:S(2)}) %collective-permute-start.6) | collective-permute-done | bytes 327712 | tf_op jit(solution)/shard_map/ppermute | solution.py:491
  28.7 0.8 join.2
  29.5 1.0 own.4
  30.4 1.3 outer.4
  31.8 1.7 %collective-permute-start.8 = (f32[15,64,128]{2,1,0:T(8,128)S(1)}, f32[15,64,128]{2,1,0:T(8,128)S(1)}, u32[]{:S(2)}, u32[]{:S(2)}) collective-permute-start(f32[15,64,128]{2,1,0:T(8,128)S(1)} %get-tuple-element.158), channel_id=1, source_target_pairs={{0,8},{8,0},{16,24},{24,16},{1,9},{9,1},{17,25},{25,17},{2,10},{10... | collective-permute-start | bytes 1474568 | tf_op jit(solution)/shard_map/ppermute | solution.py:544
  33.4 0.7 collective-permute-start.9
  34.1 1.3 ahead.1.known
  35.5 6.1 %collective-permute-done.3.rest_2_ = f32[20,32,128]{2,1,0:T(8,128)S(1)} collective-permute-done((f32[20,32,128]{2,1,0:T(8,128)S(1)}, f32[20,32,128]{2,1,0:T(8,128)S(1)}, u32[]{:S(2)}, u32[]{:S(2)}) %collective-permute-start.3) | collective-permute-done | bytes 327712 | tf_op jit(solution)/shard_map/ppermute | solution.py:491
  41.6 0.8 join.3
  42.4 4.1 %inner.3 = (f32[32,64,128]{2,1,0:T(8,128)S(1)}, f32[32,64,128]{2,1,0:T(8,128)S(1)}, f32[4,64,128]{2,1,0:T(8,128)S(1)}, f32[4,64,128]{2,1,0:T(8,128)S(1)}) custom-call(s32[5]{0:T(128)S(1)} %stack.23.me, f32[32,64,128]{2,1,0:T(8,128)S(1)} %get-tuple-element.151.cells.base, f32[4,64,128]{2,1,0:T(8,128)S(1)} %get-tuple-element.152.pair, ...), custom_call_target="tpu_custom_call" | custom-call | flops 3000000000 | tf_op jit(solution)/shard_map/inner/pallas_call | solution.py:578
  46.5 1.4 %final.3 = (f32[32,64,128]{2,1,0:T(8,128)S(1)}, f32[2,4,64,128]{3,2,1,0:T(8,128)S(1)}, f32[2,4,64,128]{3,2,1,0:T(8,128)S(1)}) custom-call(s32[5]{0:T(128)S(1)} %stack.23.me, f32[32,64,128]{2,1,0:T(8,128)S(1)} %get-tuple-element.157.part, f32[15,64,128]{2,1,0:T(8,128)S(1)} %collective-permute-done.8.recv_a, f32[15,64,128]{2,1,0:T(8,128)S(1)} %collective-permute-done.9.recv_b, ...), custom_call_target="tpu_custom_call" | custom-call | flops 2000000000 | tf_op jit(solution)/shard_map/final/pallas_call | solution.py:587
  48.0 0.7 collective-permute-start.11
  48.7 1.0 own.5
  49.7 1.3 outer.5
  51.0 1.7 %collective-permute-start.12 = (f32[15,64,128]{2,1,0:T(8,128)S(1)}, f32[15,64,128]{2,1,0:T(8,128)S(1)}, u32[]{:S(2)}, u32[]{:S(2)}) collective-permute-start(f32[15,64,128]{2,1,0:T(8,128)S(1)} %get-tuple-element.172), channel_id=1, source_target_pairs={{0,8},{8,0},{16,24},{24,16},{1,9},{9,1},{17,25},{25,17},{2,10},{10... | collective-permute-start | bytes 1474568 | tf_op jit(solution)/shard_map/ppermute | solution.py:544
  52.7 0.9 collective-permute-start.13
  53.5 5.3 %inner.4 = (f32[32,64,128]{2,1,0:T(8,128)S(1)}, f32[32,64,128]{2,1,0:T(8,128)S(1)}, f32[4,64,128]{2,1,0:T(8,128)S(1)}, f32[4,64,128]{2,1,0:T(8,128)S(1)}) custom-call(s32[5]{0:T(128)S(1)} %stack.23.me, f32[32,64,128]{2,1,0:T(8,128)S(1)} %get-tuple-element.156.cells, f32[2,4,64,128]{3,2,1,0:T(8,128)S(1)} %collective-permute-done.10.pair, ...), custom_call_target="tpu_custom_call" | custom-call | flops 3000000000 | tf_op jit(solution)/shard_map/inner/pallas_call | solution.py:578
  58.8 6.0 %collective-permute-start.14 = (f32[4,64,128]{2,1,0:T(8,128)S(1)}, f32[4,64,128]{2,1,0:T(8,128)S(1)}, u32[]{:S(2)}, u32[]{:S(2)}) collective-permute-start(f32[4,64,128]{2,1,0:T(8,128)S(1)} %get-tuple-element.175), channel_id=1, source_target_pairs={{0,1},{1,0},{2,3},{3,2},{4,5},{5,4},{6,7},{7,6},{8,9},{9,8},{10,11... | collective-permute-start | bytes 393224 | tf_op jit(solution)/shard_map/ppermute | solution.py:534
  64.8 0.7 collective-permute-start.15
  65.5 1.4 %final.4 = (f32[32,64,128]{2,1,0:T(8,128)S(1)}, f32[4,64,128]{2,1,0:T(8,128)S(1)}, f32[4,64,128]{2,1,0:T(8,128)S(1)}) custom-call(s32[5]{0:T(128)S(1)} %stack.23.me, f32[32,64,128]{2,1,0:T(8,128)S(1)} %get-tuple-element.171.part, f32[15,64,128]{2,1,0:T(8,128)S(1)} %collective-permute-done.12.recv_a, f32[15,64,128]{2,1,0:T(8,128)S(1)} %collective-permute-done.13.recv_b, ...), custom_call_target="tpu_custom_call" | custom-call | flops 2000000000 | tf_op jit(solution)/shard_map/final/pallas_call | solution.py:587
  66.9 2.6 %collective-permute-start.16 = (f32[4,64,128]{2,1,0:T(8,128)S(1)}, f32[4,64,128]{2,1,0:T(8,128)S(1)}, u32[]{:S(2)}, u32[]{:S(2)}) collective-permute-start(f32[4,64,128]{2,1,0:T(8,128)S(1)} %get-tuple-element.180), channel_id=1, source_target_pairs={{0,1},{1,0},{2,3},{3,2},{4,5},{5,4},{6,7},{7,6},{8,9},{9,8},{10,11... | collective-permute-start | bytes 393224 | tf_op jit(solution)/shard_map/ppermute | solution.py:534
  69.5 0.7 collective-permute-start.17
  70.1 1.0 own.6
  71.1 1.3 outer.6
  72.5 4.2 %collective-permute-start.18 = (f32[15,64,128]{2,1,0:T(8,128)S(1)}, f32[15,64,128]{2,1,0:T(8,128)S(1)}, u32[]{:S(2)}, u32[]{:S(2)}) collective-permute-start(f32[15,64,128]{2,1,0:T(8,128)S(1)} %get-tuple-element.185), channel_id=1, source_target_pairs={{0,8},{8,0},{16,24},{24,16},{1,9},{9,1},{17,25},{25,17},{2,10},{10... | collective-permute-start | bytes 1474568 | tf_op jit(solution)/shard_map/ppermute | solution.py:544
  76.6 0.7 collective-permute-start.19
  77.3 5.3 %inner.5 = (f32[32,64,128]{2,1,0:T(8,128)S(1)}, f32[32,64,128]{2,1,0:T(8,128)S(1)}, f32[4,64,128]{2,1,0:T(8,128)S(1)}, f32[4,64,128]{2,1,0:T(8,128)S(1)}) custom-call(s32[5]{0:T(128)S(1)} %stack.23.me, f32[32,64,128]{2,1,0:T(8,128)S(1)} %get-tuple-element.170.cells.base, f32[4,64,128]{2,1,0:T(8,128)S(1)} %collective-permute-done.14.pair, ...), custom_call_target="tpu_custom_call" | custom-call | flops 3000000000 | tf_op jit(solution)/shard_map/inner/pallas_call | solution.py:578
  82.7 3.8 %collective-permute-start.20 = (f32[4,64,128]{2,1,0:T(8,128)S(1)}, f32[4,64,128]{2,1,0:T(8,128)S(1)}, u32[]{:S(2)}, u32[]{:S(2)}) collective-permute-start(f32[4,64,128]{2,1,0:T(8,128)S(1)} %get-tuple-element.188), channel_id=1, source_target_pairs={{0,1},{1,0},{2,3},{3,2},{4,5},{5,4},{6,7},{7,6},{8,9},{9,8},{10,11... | collective-permute-start | bytes 393224 | tf_op jit(solution)/shard_map/ppermute | solution.py:534
  86.5 0.7 collective-permute-start.21
  87.2 1.4 %final.5 = (f32[32,64,128]{2,1,0:T(8,128)S(1)}, f32[4,64,128]{2,1,0:T(8,128)S(1)}, f32[4,64,128]{2,1,0:T(8,128)S(1)}) custom-call(s32[5]{0:T(128)S(1)} %stack.23.me, f32[32,64,128]{2,1,0:T(8,128)S(1)} %get-tuple-element.184.part, f32[15,64,128]{2,1,0:T(8,128)S(1)} %collective-permute-done.18.recv_a, f32[15,64,128]{2,1,0:T(8,128)S(1)} %collective-permute-done.19.recv_b, ...), custom_call_target="tpu_custom_call" | custom-call | flops 2000000000 | tf_op jit(solution)/shard_map/final/pallas_call | solution.py:587
  88.6 1.5 %collective-permute-start.22 = (f32[4,64,128]{2,1,0:T(8,128)S(1)}, f32[4,64,128]{2,1,0:T(8,128)S(1)}, u32[]{:S(2)}, u32[]{:S(2)}) collective-permute-start(f32[4,64,128]{2,1,0:T(8,128)S(1)} %get-tuple-element.193), channel_id=1, source_target_pairs={{0,1},{1,0},{2,3},{3,2},{4,5},{5,4},{6,7},{7,6},{8,9},{9,8},{10,11... | collective-permute-start | bytes 393224 | tf_op jit(solution)/shard_map/ppermute | solution.py:534
  90.1 0.7 collective-permute-start.23
  90.8 1.0 own.7
  91.8 1.3 outer.7
  93.2 3.8 %collective-permute-start.24 = (f32[15,64,128]{2,1,0:T(8,128)S(1)}, f32[15,64,128]{2,1,0:T(8,128)S(1)}, u32[]{:S(2)}, u32[]{:S(2)}) collective-permute-start(f32[15,64,128]{2,1,0:T(8,128)S(1)} %get-tuple-element.197), channel_id=1, source_target_pairs={{0,8},{8,0},{16,24},{24,16},{1,9},{9,1},{17,25},{25,17},{2,10},{10... | collective-permute-start | bytes 1474568 | tf_op jit(solution)/shard_map/ppermute | solution.py:544
  97.0 0.9 collective-permute-start.25
  97.9 5.3 %last_inner.1 = (f32[32,64,128]{2,1,0:T(8,128)S(1)}, f32[16,32,128]{2,1,0:T(8,128)S(1)}, f32[16,32,128]{2,1,0:T(8,128)S(1)}, f32[16,32,128]{2,1,0:T(8,128)S(1)}, f32[16,32,128]{2,1,0:T(8,128)S(1)}) custom-call(s32[5]{0:T(128)S(1)} %stack.23.me, f32[32,64,128]{2,1,0:T(8,128)S(1)} %get-tuple-element.183.cells, f32[4,64,128]{2,1,0:T(8,128)S(1)} %collective-permute-done.20.pair, ...), custom_call_target="tpu_custom_call" | custom-call | flops 3000000000 | tf_op jit(solution)/shard_map/last_inner/pallas_call | solution.py:567
  103.3 0.6 collective-permute-start.30
  103.9 1.2 collective-permute-start.31
  105.1 1.7 %collective-permute-start.32 = (f32[16,32,128]{2,1,0:T(8,128)S(1)}, f32[16,32,128]{2,1,0:T(8,128)S(1)}, u32[]{:S(2)}, u32[]{:S(2)}) collective-permute-start(f32[16,32,128]{2,1,0:T(8,128)S(1)} %get-tuple-element.206), channel_id=1, source_target_pairs={{0,6},{2,4},{4,2},{6,0},{1,7},{3,5},{5,3},{7,1},{8,14},{10,12},{12... | collective-permute-start | bytes 786440 | tf_op jit(solution)/shard_map/ppermute | solution.py:491
  106.8 1.3 last.1
  108.2 0.6 collective-permute-start.26
  108.8 1.2 collective-permute-start.27
  110.0 1.7 %collective-permute-start.28 = (f32[16,32,128]{2,1,0:T(8,128)S(1)}, f32[16,32,128]{2,1,0:T(8,128)S(1)}, u32[]{:S(2)}, u32[]{:S(2)}) collective-permute-start(f32[16,32,128]{2,1,0:T(8,128)S(1)} %get-tuple-element.202), channel_id=1, source_target_pairs={{0,6},{2,4},{4,2},{6,0},{1,7},{3,5},{5,3},{7,1},{8,14},{10,12},{12... | collective-permute-start | bytes 786440 | tf_op jit(solution)/shard_map/ppermute | solution.py:491
  111.7 3.5 %collective-permute-done.32.rest_3_.rest_8_ = f32[16,32,128]{2,1,0:T(8,128)S(1)} collective-permute-done((f32[16,32,128]{2,1,0:T(8,128)S(1)}, f32[16,32,128]{2,1,0:T(8,128)S(1)}, u32[]{:S(2)}, u32[]{:S(2)}) %collective-permute-start.32) | collective-permute-done | bytes 262176 | tf_op jit(solution)/shard_map/ppermute | solution.py:491
  115.2 0.6 split_back.3
  115.8 5.9 %collective-permute-start.33 = (f32[4,16,16,128]{3,2,1,0:T(8,128)S(1)}, f32[4,16,16,128]{3,2,1,0:T(8,128)S(1)}, u32[]{:S(2)}, u32[]{:S(2)}) collective-permute-start(f32[4,16,16,128]{3,2,1,0:T(8,128)S(1)} %split_back.3), channel_id=1, source_target_pairs={{0,1},{1,0},{2,3},{3,2},{4,5},{5,4},{6,7},{7,6},{8,9},{9,8},{10,11... | collective-permute-start | bytes 1572872 | tf_op jit(solution)/shard_map/ppermute | solution.py:596
  121.7 2.0 %collective-permute-done.27.rest_2_ = f32[16,32,128]{2,1,0:T(8,128)S(1)} collective-permute-done((f32[16,32,128]{2,1,0:T(8,128)S(1)}, f32[16,32,128]{2,1,0:T(8,128)S(1)}, u32[]{:S(2)}, u32[]{:S(2)}) %collective-permute-start.27) | collective-permute-done | bytes 262176 | tf_op jit(solution)/shard_map/ppermute | solution.py:491
  123.7 2.8 %collective-permute-done.28.rest_3_ = f32[16,32,128]{2,1,0:T(8,128)S(1)} collective-permute-done((f32[16,32,128]{2,1,0:T(8,128)S(1)}, f32[16,32,128]{2,1,0:T(8,128)S(1)}, u32[]{:S(2)}, u32[]{:S(2)}) %collective-permute-start.28) | collective-permute-done | bytes 262176 | tf_op jit(solution)/shard_map/ppermute | solution.py:491
  127.0 3.3 %collective-permute-start.29 = (f32[4,16,16,128]{3,2,1,0:T(8,128)S(1)}, f32[4,16,16,128]{3,2,1,0:T(8,128)S(1)}, u32[]{:S(2)}, u32[]{:S(2)}) collective-permute-start(f32[4,16,16,128]{3,2,1,0:T(8,128)S(1)} %split_back.2), channel_id=1, source_target_pairs={{0,1},{1,0},{2,3},{3,2},{4,5},{5,4},{6,7},{7,6},{8,9},{9,8},{10,11... | collective-permute-start | bytes 1572872 | tf_op jit(solution)/shard_map/ppermute | solution.py:596
  130.4 1.5 %collective-permute-done.29.rest_4_ = f32[4,16,16,128]{3,2,1,0:T(8,128)S(1)} collective-permute-done((f32[4,16,16,128]{3,2,1,0:T(8,128)S(1)}, f32[4,16,16,128]{3,2,1,0:T(8,128)S(1)}, u32[]{:S(2)}, u32[]{:S(2)}) %collective-permute-start.29) | collective-permute-done | bytes 524320 | tf_op jit(solution)/shard_map/ppermute | solution.py:596
  131.9 2.1 %gather.1 = f32[2,32,16,512]{3,2,1,0:T(8,128)} custom-call(s32[5]{0:T(128)S(1)} %stack.23.me, f32[16,32,128]{2,1,0:T(8,128)S(1)} %get-tuple-element.199.rest_0_, f32[16,32,128]{2,1,0:T(8,128)S(1)} %collective-permute-done.26.rest_1_, f32[16,32,128]{2,1,0:T(8,128)S(1)} %collective-permute-done.27.rest_2_, f32[16,32,128]{2,1,0:T(8,128)S(1)} %collective-permute-done.28.rest_3_, ...), custom_call_target="tpu_custom_call" | custom-call | flops 2000000000 | tf_op jit(solution)/shard_map/gather/pallas_call | solution.py:598
  (40 shorter events, 1.4 us)
Async XLA Ops:
  0.0 4.7 %copy-start.1 = (s32[1,4,32]{2,1,0:T(4,128)S(1)}, s32[1,4,32]{2,1,0:T(4,128)}, u32[]{:S(2)}) copy-start(s32[1,4,32]{2,1,0:T(4,128)} %param.9) | copy-start | bytes 1540
  0.1 1.6 %copy-start = (f32[2,32,16,512]{3,2,1,0:T(8,128)S(1)}, f32[2,32,16,512]{3,2,1,0:T(8,128)}, u32[]{:S(2)}) copy-start(f32[2,32,16,512]{3,2,1,0:T(8,128)} %observed.1) | copy-start | bytes 6291460
  1.7 20.9 %copy-start.2 = (f32[2,31]{1,0:T(2,128)S(1)}, f32[2,31]{1,0:T(2,128)}, u32[]{:S(2)}) copy-start(f32[2,31]{1,0:T(2,128)} %rows.1) | copy-start | bytes 748
  1.7 20.9 %copy-start.3 = (f32[2,31]{1,0:T(2,128)S(1)}, f32[2,31]{1,0:T(2,128)}, u32[]{:S(2)}) copy-start(f32[2,31]{1,0:T(2,128)} %columns.1) | copy-start | bytes 748
  1.7 20.9 %copy-start.4 = (f32[2,101]{1,0:T(2,128)S(1)}, f32[2,101]{1,0:T(2,128)}, u32[]{:S(2)}) copy-start(f32[2,101]{1,0:T(2,128)} %axial.1) | copy-start | bytes 2428
  4.2 3.2 %collective-permute-start = (f32[2,2,40,16,128]{4,3,2,1,0:T(8,128)S(1)}, f32[2,2,40,16,128]{4,3,2,1,0:T(8,128)S(1)}, u32[]{:S(2)}, u32[]{:S(2)}) collective-permute-start(f32[2,2,40,16,128]{4,3,2,1,0:T(8,128)S(1)} %get-tuple-element.107), channel_id=1, source_target_pairs={{0,1},{1,0},{2,3},{3,2},{4,5},{5,4},{6,7},{7,6},{8,9},{9,8},{10,11... | collective-permute-start | bytes 3932168 | tf_op jit(solution)/shard_map/ppermute | solution.py:504
  4.7 4.2 %collective-permute-start.1 = (s32[4,32]{1,0:T(4,128)S(1)}, s32[4,32]{1,0:T(4,128)S(1)}, u32[]{:S(2)}, u32[]{:S(2)}) collective-permute-start(s32[4,32]{1,0:T(4,128)S(1)} %bitcast.6), channel_id=1, source_target_pairs={{0,4},{4,0},{1,5},{5,1},{2,6},{6,2},{3,7},{7,3},{8,12},{12,8},{9,1... | collective-permute-start | bytes 1544 | tf_op jit(solution)/shard_map/ppermute | solution.py:501
  8.9 10.7 %collective-permute-start.5 = (f32[20,32,128]{2,1,0:T(8,128)S(1)}, f32[20,32,128]{2,1,0:T(8,128)S(1)}, u32[]{:S(2)}, u32[]{:S(2)}) collective-permute-start(f32[20,32,128]{2,1,0:T(8,128)S(1)} %get-tuple-element.121), channel_id=1, source_target_pairs={{0,2},{2,0},{4,6},{6,4},{1,3},{3,1},{5,7},{7,5},{8,10},{10,8},{12,... | collective-permute-start | bytes 983048 | tf_op jit(solution)/shard_map/ppermute | solution.py:491
  11.0 17.6 %collective-permute-start.6 = (f32[20,32,128]{2,1,0:T(8,128)S(1)}, f32[20,32,128]{2,1,0:T(8,128)S(1)}, u32[]{:S(2)}, u32[]{:S(2)}) collective-permute-start(f32[20,32,128]{2,1,0:T(8,128)S(1)} %get-tuple-element.122), channel_id=1, source_target_pairs={{0,4},{2,6},{4,0},{6,2},{1,5},{3,7},{5,1},{7,3},{8,12},{10,14},{12... | collective-permute-start | bytes 983048 | tf_op jit(solution)/shard_map/ppermute | solution.py:491
  12.6 16.1 %collective-permute-start.7 = (f32[20,32,128]{2,1,0:T(8,128)S(1)}, f32[20,32,128]{2,1,0:T(8,128)S(1)}, u32[]{:S(2)}, u32[]{:S(2)}) collective-permute-start(f32[20,32,128]{2,1,0:T(8,128)S(1)} %get-tuple-element.123), channel_id=1, source_target_pairs={{0,6},{2,4},{4,2},{6,0},{1,7},{3,5},{5,3},{7,1},{8,14},{10,12},{12... | collective-permute-start | bytes 983048 | tf_op jit(solution)/shard_map/ppermute | solution.py:491
  12.6 22.9 %collective-permute-start.2 = (f32[20,32,128]{2,1,0:T(8,128)S(1)}, f32[20,32,128]{2,1,0:T(8,128)S(1)}, u32[]{:S(2)}, u32[]{:S(2)}) collective-permute-start(f32[20,32,128]{2,1,0:T(8,128)S(1)} %get-tuple-element.117), channel_id=1, source_target_pairs={{0,2},{2,0},{4,6},{6,4},{1,3},{3,1},{5,7},{7,5},{8,10},{10,8},{12,... | collective-permute-start | bytes 983048 | tf_op jit(solution)/shard_map/ppermute | solution.py:491
  14.5 27.1 %collective-permute-start.3 = (f32[20,32,128]{2,1,0:T(8,128)S(1)}, f32[20,32,128]{2,1,0:T(8,128)S(1)}, u32[]{:S(2)}, u32[]{:S(2)}) collective-permute-start(f32[20,32,128]{2,1,0:T(8,128)S(1)} %get-tuple-element.118), channel_id=1, source_target_pairs={{0,4},{2,6},{4,0},{6,2},{1,5},{3,7},{5,1},{7,3},{8,12},{10,14},{12... | collective-permute-start | bytes 983048 | tf_op jit(solution)/shard_map/ppermute | solution.py:491
  19.5 22.0 %collective-permute-start.4 = (f32[20,32,128]{2,1,0:T(8,128)S(1)}, f32[20,32,128]{2,1,0:T(8,128)S(1)}, u32[]{:S(2)}, u32[]{:S(2)}) collective-permute-start(f32[20,32,128]{2,1,0:T(8,128)S(1)} %get-tuple-element.119), channel_id=1, source_target_pairs={{0,6},{2,4},{4,2},{6,0},{1,7},{3,5},{5,3},{7,1},{8,14},{10,12},{12... | collective-permute-start | bytes 983048 | tf_op jit(solution)/shard_map/ppermute | solution.py:491
  31.8 14.7 %collective-permute-start.8 = (f32[15,64,128]{2,1,0:T(8,128)S(1)}, f32[15,64,128]{2,1,0:T(8,128)S(1)}, u32[]{:S(2)}, u32[]{:S(2)}) collective-permute-start(f32[15,64,128]{2,1,0:T(8,128)S(1)} %get-tuple-element.158), channel_id=1, source_target_pairs={{0,8},{8,0},{16,24},{24,16},{1,9},{9,1},{17,25},{25,17},{2,10},{10... | collective-permute-start | bytes 1474568 | tf_op jit(solution)/shard_map/ppermute | solution.py:544
  33.4 13.1 %collective-permute-start.9 = (f32[15,64,128]{2,1,0:T(8,128)S(1)}, f32[15,64,128]{2,1,0:T(8,128)S(1)}, u32[]{:S(2)}, u32[]{:S(2)}) collective-permute-start(f32[15,64,128]{2,1,0:T(8,128)S(1)} %get-tuple-element.159), channel_id=1, source_target_pairs={{8,16},{16,8},{9,17},{17,9},{10,18},{18,10},{11,19},{19,11},{12,20... | collective-permute-start | bytes 1474568 | tf_op jit(solution)/shard_map/ppermute | solution.py:544
  47.9 1.7 %collective-permute-start.10 = (f32[2,4,64,128]{3,2,1,0:T(8,128)S(1)}, f32[2,4,64,128]{3,2,1,0:T(8,128)S(1)}, u32[]{:S(2)}, u32[]{:S(2)}) collective-permute-start(f32[2,4,64,128]{3,2,1,0:T(8,128)S(1)} %get-tuple-element.162), channel_id=1, source_target_pairs={{0,1},{1,0},{2,3},{3,2},{4,5},{5,4},{6,7},{7,6},{8,9},{9,8},{10,11... | collective-permute-start | bytes 786440 | tf_op jit(solution)/shard_map/ppermute | solution.py:534
  48.0 1.7 %collective-permute-start.11 = (f32[2,4,64,128]{3,2,1,0:T(8,128)S(1)}, f32[2,4,64,128]{3,2,1,0:T(8,128)S(1)}, u32[]{:S(2)}, u32[]{:S(2)}) collective-permute-start(f32[2,4,64,128]{3,2,1,0:T(8,128)S(1)} %get-tuple-element.163), channel_id=1, source_target_pairs={{1,5},{5,1},{3,7},{7,3},{9,13},{13,9},{11,15},{15,11},{17,21},{21,... | collective-permute-start | bytes 786440 | tf_op jit(solution)/shard_map/ppermute | solution.py:533
  51.0 14.5 %collective-permute-start.12 = (f32[15,64,128]{2,1,0:T(8,128)S(1)}, f32[15,64,128]{2,1,0:T(8,128)S(1)}, u32[]{:S(2)}, u32[]{:S(2)}) collective-permute-start(f32[15,64,128]{2,1,0:T(8,128)S(1)} %get-tuple-element.172), channel_id=1, source_target_pairs={{0,8},{8,0},{16,24},{24,16},{1,9},{9,1},{17,25},{25,17},{2,10},{10... | collective-permute-start | bytes 1474568 | tf_op jit(solution)/shard_map/ppermute | solution.py:544
  52.7 12.8 %collective-permute-start.13 = (f32[15,64,128]{2,1,0:T(8,128)S(1)}, f32[15,64,128]{2,1,0:T(8,128)S(1)}, u32[]{:S(2)}, u32[]{:S(2)}) collective-permute-start(f32[15,64,128]{2,1,0:T(8,128)S(1)} %get-tuple-element.173), channel_id=1, source_target_pairs={{8,16},{16,8},{9,17},{17,9},{10,18},{18,10},{11,19},{19,11},{12,20... | collective-permute-start | bytes 1474568 | tf_op jit(solution)/shard_map/ppermute | solution.py:544
  58.8 11.3 %collective-permute-start.14 = (f32[4,64,128]{2,1,0:T(8,128)S(1)}, f32[4,64,128]{2,1,0:T(8,128)S(1)}, u32[]{:S(2)}, u32[]{:S(2)}) collective-permute-start(f32[4,64,128]{2,1,0:T(8,128)S(1)} %get-tuple-element.175), channel_id=1, source_target_pairs={{0,1},{1,0},{2,3},{3,2},{4,5},{5,4},{6,7},{7,6},{8,9},{9,8},{10,11... | collective-permute-start | bytes 393224 | tf_op jit(solution)/shard_map/ppermute | solution.py:534
  64.8 5.3 %collective-permute-start.15 = (f32[4,64,128]{2,1,0:T(8,128)S(1)}, f32[4,64,128]{2,1,0:T(8,128)S(1)}, u32[]{:S(2)}, u32[]{:S(2)}) collective-permute-start(f32[4,64,128]{2,1,0:T(8,128)S(1)} %get-tuple-element.176), channel_id=1, source_target_pairs={{1,5},{5,1},{3,7},{7,3},{9,13},{13,9},{11,15},{15,11},{17,21},{21,... | collective-permute-start | bytes 393224 | tf_op jit(solution)/shard_map/ppermute | solution.py:533
  66.9 4.2 %collective-permute-start.16 = (f32[4,64,128]{2,1,0:T(8,128)S(1)}, f32[4,64,128]{2,1,0:T(8,128)S(1)}, u32[]{:S(2)}, u32[]{:S(2)}) collective-permute-start(f32[4,64,128]{2,1,0:T(8,128)S(1)} %get-tuple-element.180), channel_id=1, source_target_pairs={{0,1},{1,0},{2,3},{3,2},{4,5},{5,4},{6,7},{7,6},{8,9},{9,8},{10,11... | collective-permute-start | bytes 393224 | tf_op jit(solution)/shard_map/ppermute | solution.py:534
  69.5 1.7 %collective-permute-start.17 = (f32[4,64,128]{2,1,0:T(8,128)S(1)}, f32[4,64,128]{2,1,0:T(8,128)S(1)}, u32[]{:S(2)}, u32[]{:S(2)}) collective-permute-start(f32[4,64,128]{2,1,0:T(8,128)S(1)} %get-tuple-element.181), channel_id=1, source_target_pairs={{1,5},{5,1},{3,7},{7,3},{9,13},{13,9},{11,15},{15,11},{17,21},{21,... | collective-permute-start | bytes 393224 | tf_op jit(solution)/shard_map/ppermute | solution.py:533
  72.5 14.7 %collective-permute-start.18 = (f32[15,64,128]{2,1,0:T(8,128)S(1)}, f32[15,64,128]{2,1,0:T(8,128)S(1)}, u32[]{:S(2)}, u32[]{:S(2)}) collective-permute-start(f32[15,64,128]{2,1,0:T(8,128)S(1)} %get-tuple-element.185), channel_id=1, source_target_pairs={{0,8},{8,0},{16,24},{24,16},{1,9},{9,1},{17,25},{25,17},{2,10},{10... | collective-permute-start | bytes 1474568 | tf_op jit(solution)/shard_map/ppermute | solution.py:544
  76.6 10.6 %collective-permute-start.19 = (f32[15,64,128]{2,1,0:T(8,128)S(1)}, f32[15,64,128]{2,1,0:T(8,128)S(1)}, u32[]{:S(2)}, u32[]{:S(2)}) collective-permute-start(f32[15,64,128]{2,1,0:T(8,128)S(1)} %get-tuple-element.186), channel_id=1, source_target_pairs={{8,16},{16,8},{9,17},{17,9},{10,18},{18,10},{11,19},{19,11},{12,20... | collective-permute-start | bytes 1474568 | tf_op jit(solution)/shard_map/ppermute | solution.py:544
  82.7 8.1 %collective-permute-start.20 = (f32[4,64,128]{2,1,0:T(8,128)S(1)}, f32[4,64,128]{2,1,0:T(8,128)S(1)}, u32[]{:S(2)}, u32[]{:S(2)}) collective-permute-start(f32[4,64,128]{2,1,0:T(8,128)S(1)} %get-tuple-element.188), channel_id=1, source_target_pairs={{0,1},{1,0},{2,3},{3,2},{4,5},{5,4},{6,7},{7,6},{8,9},{9,8},{10,11... | collective-permute-start | bytes 393224 | tf_op jit(solution)/shard_map/ppermute | solution.py:534
  86.5 4.3 %collective-permute-start.21 = (f32[4,64,128]{2,1,0:T(8,128)S(1)}, f32[4,64,128]{2,1,0:T(8,128)S(1)}, u32[]{:S(2)}, u32[]{:S(2)}) collective-permute-start(f32[4,64,128]{2,1,0:T(8,128)S(1)} %get-tuple-element.189), channel_id=1, source_target_pairs={{1,5},{5,1},{3,7},{7,3},{9,13},{13,9},{11,15},{15,11},{17,21},{21,... | collective-permute-start | bytes 393224 | tf_op jit(solution)/shard_map/ppermute | solution.py:533
  88.6 3.2 %collective-permute-start.22 = (f32[4,64,128]{2,1,0:T(8,128)S(1)}, f32[4,64,128]{2,1,0:T(8,128)S(1)}, u32[]{:S(2)}, u32[]{:S(2)}) collective-permute-start(f32[4,64,128]{2,1,0:T(8,128)S(1)} %get-tuple-element.193), channel_id=1, source_target_pairs={{0,1},{1,0},{2,3},{3,2},{4,5},{5,4},{6,7},{7,6},{8,9},{9,8},{10,11... | collective-permute-start | bytes 393224 | tf_op jit(solution)/shard_map/ppermute | solution.py:534
  90.1 1.7 %collective-permute-start.23 = (f32[4,64,128]{2,1,0:T(8,128)S(1)}, f32[4,64,128]{2,1,0:T(8,128)S(1)}, u32[]{:S(2)}, u32[]{:S(2)}) collective-permute-start(f32[4,64,128]{2,1,0:T(8,128)S(1)} %get-tuple-element.194), channel_id=1, source_target_pairs={{1,5},{5,1},{3,7},{7,3},{9,13},{13,9},{11,15},{15,11},{17,21},{21,... | collective-permute-start | bytes 393224 | tf_op jit(solution)/shard_map/ppermute | solution.py:533
  93.2 13.6 %collective-permute-start.24 = (f32[15,64,128]{2,1,0:T(8,128)S(1)}, f32[15,64,128]{2,1,0:T(8,128)S(1)}, u32[]{:S(2)}, u32[]{:S(2)}) collective-permute-start(f32[15,64,128]{2,1,0:T(8,128)S(1)} %get-tuple-element.197), channel_id=1, source_target_pairs={{0,8},{8,0},{16,24},{24,16},{1,9},{9,1},{17,25},{25,17},{2,10},{10... | collective-permute-start | bytes 1474568 | tf_op jit(solution)/shard_map/ppermute | solution.py:544
  97.0 9.8 %collective-permute-start.25 = (f32[15,64,128]{2,1,0:T(8,128)S(1)}, f32[15,64,128]{2,1,0:T(8,128)S(1)}, u32[]{:S(2)}, u32[]{:S(2)}) collective-permute-start(f32[15,64,128]{2,1,0:T(8,128)S(1)} %get-tuple-element.198), channel_id=1, source_target_pairs={{8,16},{16,8},{9,17},{17,9},{10,18},{18,10},{11,19},{19,11},{12,20... | collective-permute-start | bytes 1474568 | tf_op jit(solution)/shard_map/ppermute | solution.py:544
  103.3 6.7 %collective-permute-start.30 = (f32[16,32,128]{2,1,0:T(8,128)S(1)}, f32[16,32,128]{2,1,0:T(8,128)S(1)}, u32[]{:S(2)}, u32[]{:S(2)}) collective-permute-start(f32[16,32,128]{2,1,0:T(8,128)S(1)} %get-tuple-element.204), channel_id=1, source_target_pairs={{0,2},{2,0},{4,6},{6,4},{1,3},{3,1},{5,7},{7,5},{8,10},{10,8},{12,... | collective-permute-start | bytes 786440 | tf_op jit(solution)/shard_map/ppermute | solution.py:491
  103.9 7.9 %collective-permute-start.31 = (f32[16,32,128]{2,1,0:T(8,128)S(1)}, f32[16,32,128]{2,1,0:T(8,128)S(1)}, u32[]{:S(2)}, u32[]{:S(2)}) collective-permute-start(f32[16,32,128]{2,1,0:T(8,128)S(1)} %get-tuple-element.205), channel_id=1, source_target_pairs={{0,4},{2,6},{4,0},{6,2},{1,5},{3,7},{5,1},{7,3},{8,12},{10,14},{12... | collective-permute-start | bytes 786440 | tf_op jit(solution)/shard_map/ppermute | solution.py:491
  105.1 10.1 %collective-permute-start.32 = (f32[16,32,128]{2,1,0:T(8,128)S(1)}, f32[16,32,128]{2,1,0:T(8,128)S(1)}, u32[]{:S(2)}, u32[]{:S(2)}) collective-permute-start(f32[16,32,128]{2,1,0:T(8,128)S(1)} %get-tuple-element.206), channel_id=1, source_target_pairs={{0,6},{2,4},{4,2},{6,0},{1,7},{3,5},{5,3},{7,1},{8,14},{10,12},{12... | collective-permute-start | bytes 786440 | tf_op jit(solution)/shard_map/ppermute | solution.py:491
  108.2 13.5 %collective-permute-start.26 = (f32[16,32,128]{2,1,0:T(8,128)S(1)}, f32[16,32,128]{2,1,0:T(8,128)S(1)}, u32[]{:S(2)}, u32[]{:S(2)}) collective-permute-start(f32[16,32,128]{2,1,0:T(8,128)S(1)} %get-tuple-element.200), channel_id=1, source_target_pairs={{0,2},{2,0},{4,6},{6,4},{1,3},{3,1},{5,7},{7,5},{8,10},{10,8},{12,... | collective-permute-start | bytes 786440 | tf_op jit(solution)/shard_map/ppermute | solution.py:491
  108.8 14.9 %collective-permute-start.27 = (f32[16,32,128]{2,1,0:T(8,128)S(1)}, f32[16,32,128]{2,1,0:T(8,128)S(1)}, u32[]{:S(2)}, u32[]{:S(2)}) collective-permute-start(f32[16,32,128]{2,1,0:T(8,128)S(1)} %get-tuple-element.201), channel_id=1, source_target_pairs={{0,4},{2,6},{4,0},{6,2},{1,5},{3,7},{5,1},{7,3},{8,12},{10,14},{12... | collective-permute-start | bytes 786440 | tf_op jit(solution)/shard_map/ppermute | solution.py:491
  110.0 16.4 %collective-permute-start.28 = (f32[16,32,128]{2,1,0:T(8,128)S(1)}, f32[16,32,128]{2,1,0:T(8,128)S(1)}, u32[]{:S(2)}, u32[]{:S(2)}) collective-permute-start(f32[16,32,128]{2,1,0:T(8,128)S(1)} %get-tuple-element.202), channel_id=1, source_target_pairs={{0,6},{2,4},{4,2},{6,0},{1,7},{3,5},{5,3},{7,1},{8,14},{10,12},{12... | collective-permute-start | bytes 786440 | tf_op jit(solution)/shard_map/ppermute | solution.py:491
  115.8 14.6 %collective-permute-start.33 = (f32[4,16,16,128]{3,2,1,0:T(8,128)S(1)}, f32[4,16,16,128]{3,2,1,0:T(8,128)S(1)}, u32[]{:S(2)}, u32[]{:S(2)}) collective-permute-start(f32[4,16,16,128]{3,2,1,0:T(8,128)S(1)} %split_back.3), channel_id=1, source_target_pairs={{0,1},{1,0},{2,3},{3,2},{4,5},{5,4},{6,7},{7,6},{8,9},{9,8},{10,11... | collective-permute-start | bytes 1572872 | tf_op jit(solution)/shard_map/ppermute | solution.py:596
  127.0 4.9 %collective-permute-start.29 = (f32[4,16,16,128]{3,2,1,0:T(8,128)S(1)}, f32[4,16,16,128]{3,2,1,0:T(8,128)S(1)}, u32[]{:S(2)}, u32[]{:S(2)}) collective-permute-start(f32[4,16,16,128]{3,2,1,0:T(8,128)S(1)} %split_back.2), channel_id=1, source_target_pairs={{0,1},{1,0},{2,3},{3,2},{4,5},{5,4},{6,7},{7,6},{8,9},{9,8},{10,11... | collective-permute-start | bytes 1572872 | tf_op jit(solution)/shard_map/ppermute | solution.py:596
